TPU v7x, 32 devices: a whole 2x2x4 slice. The times are simulated.
32 devices in a mesh: ctx: 8 (over y, x, core), fsdp: 4 (over z).
Axes of the slice: x: 2, y: 2, z: 4, core: 2. Of those that a mesh axis runs over, the one named last changes fastest.
Arguments:
- tokens: bfloat16 [4, 1024, 1024], P('fsdp', 'ctx'), may hold values from -6 to 6
- cotangent: bfloat16 [4, 1024, 1024], P('fsdp', 'ctx'), may hold values from -6 to 6
- stretch_order: int32 [16], replicated, may hold values from 0 to 15, as said below
- doc_lengths: int32 [4, 3], P('fsdp'), may hold values from 1 to 896, 1024 in all within a row
- master: float32 [15730944], P(('ctx', 'fsdp'))
- first_moment: float32 [15730944], P(('ctx', 'fsdp'))
- second_moment: float32 [15730944], P(('ctx', 'fsdp')), as said below
Outputs:
- layer_out: bfloat16 [4, 1024, 1024], P('fsdp', 'ctx')
- input_grad: bfloat16 [4, 1024, 1024], P('fsdp', 'ctx')
- new_master: float32 [15730944], P(('ctx', 'fsdp'))
- new_first: float32 [15730944], P(('ctx', 'fsdp'))
- new_second: float32 [15730944], P(('ctx', 'fsdp'))
Inputs may be any that keep to these rules, and one draw needn't show every extreme that they name: `stretch_order`: slots 2 j and 2 j + 1 hold two stretches c and 15 - c; every stretch appears once. `doc_lengths`: each row sums to 1024; its largest entry is exactly 896. `second_moment`: every entry is positive.
All inputs are finite; a program needn't handle non-finite values.
Results may differ from a plain program's by a relative error of at most 0.017.
Values may be sent and summed in bfloat16 or wider, within the bound.
A program may use at most 256 MiB of HBM per device.

v0:
```python
import jax
import jax.numpy as jnp
from jax import lax
from jax.sharding import PartitionSpec as P

MODEL_WIDTH = 1024
QUERY_HEADS = 16
KEY_VALUE_HEADS = 8
HEAD_SIZE = 128
FEED_WIDTH = 3072
STRETCH = 64
STEP = 7


NORM_EPS = 1e-06
ROPE_BASE = 1000000.0
BETA_ONE = 0.5
BETA_TWO = 0.5
DECAY_RATE = 0.1
ADAM_EPS = 1e-08
MASKED = -1e30


def from_behind(x, axis, by):
    peers = lax.axis_size(axis)
    return lax.ppermute(x, axis, [(i, (i + by) % peers) for i in range(peers)])


def segment_shapes():
    return [
        (MODEL_WIDTH, (QUERY_HEADS + 2 * KEY_VALUE_HEADS) * HEAD_SIZE),
        (QUERY_HEADS * HEAD_SIZE, MODEL_WIDTH),
        (MODEL_WIDTH, 2 * FEED_WIDTH),
        (FEED_WIDTH, MODEL_WIDTH),
        (2 * MODEL_WIDTH + 2 * HEAD_SIZE, 1),
    ]


def unpack(flat_params, count_of_shards):
    param_table = flat_params.reshape(count_of_shards, -1)
    pieces = []
    offset = 0
    for row_total, column_total in segment_shapes():
        shard_span = row_total // count_of_shards * column_total
        pieces.append(param_table[:, offset : offset + shard_span].reshape(row_total, column_total))
        offset += shard_span
    return pieces


def pack(matrices, count_of_shards):
    return jnp.concatenate(
        [matrix.reshape(count_of_shards, -1) for matrix in matrices], axis=1
    ).reshape(-1)


def rate_rows(count_of_shards, seq_length):
    settings = [
        (MODEL_WIDTH ** (-0.5), DECAY_RATE),
        ((seq_length / (3.0 * QUERY_HEADS * HEAD_SIZE)) ** 0.5, DECAY_RATE),
        (MODEL_WIDTH ** (-0.5), DECAY_RATE),
        (FEED_WIDTH ** (-0.5), DECAY_RATE),
        (0.2, 0.0),
    ]
    step_parts = []
    decay_parts = []
    for (row_total, column_total), (step_rate, decay_value) in zip(segment_shapes(), settings):
        shard_span = row_total // count_of_shards * column_total
        step_parts.append(jnp.full((shard_span,), step_rate, jnp.float32))
        decay_parts.append(jnp.full((shard_span,), decay_value, jnp.float32))
    return (jnp.concatenate(step_parts), jnp.concatenate(decay_parts))


def slot_positions(stretch_order, first_row, count_of_rows):
    row_ids = first_row + jnp.arange(count_of_rows, dtype=jnp.int32)
    slot_ids = row_ids // STRETCH
    slot_table = jnp.arange(stretch_order.shape[0], dtype=jnp.int32)
    stretch_ids = jnp.sum(
        jnp.where(slot_ids[:, None] == slot_table[None, :], stretch_order[None, :], 0), axis=1
    )
    return stretch_ids * STRETCH + row_ids % STRETCH


def documents(positions, doc_lengths):
    doc_ends = jnp.cumsum(doc_lengths, axis=1)
    doc_starts = doc_ends - doc_lengths
    passed = positions[None, :, None] >= doc_ends[:, None, :-1]
    doc_ids = jnp.sum(passed.astype(jnp.int32), axis=2)
    doc_table = jnp.arange(doc_lengths.shape[1], dtype=jnp.int32)
    owner = doc_ids[:, :, None] == doc_table[None, None, :]
    start_of = jnp.sum(jnp.where(owner, doc_starts[:, None, :], 0), axis=2)
    return (doc_ids, positions[None, :] - start_of)


def key_mask(stretch_order, doc_lengths, query_pos, query_doc, first_row, count_of_rows):
    key_pos = slot_positions(stretch_order, first_row, count_of_rows)
    key_doc, _ = documents(key_pos, doc_lengths)
    same_doc = query_doc[:, :, None] == key_doc[:, None, :]
    return same_doc & (key_pos[None, None, :] <= query_pos[None, :, None])


def rope_tables(relative):
    half_dim = HEAD_SIZE // 2
    frequency = ROPE_BASE ** (-(jnp.arange(half_dim, dtype=jnp.float32) * 2.0 / HEAD_SIZE))
    angles = relative.astype(jnp.float32)[..., None] * frequency
    cosine_table = jnp.cos(angles)
    sine_values = jnp.sin(angles)
    return (
        jnp.concatenate([cosine_table, cosine_table], axis=-1),
        jnp.concatenate([sine_values, sine_values], axis=-1),
    )


def rotate(values, cosine_table, sine_values):
    half_dim = values.shape[-1] // 2
    turned = jnp.concatenate([-values[..., half_dim:], values[..., :half_dim]], axis=-1)
    return values * cosine_table[..., None, :] + turned * sine_values[..., None, :]


def rotate_back(grads, cosine_table, sine_values):
    half_dim = grads.shape[-1] // 2
    moved = grads * sine_values[..., None, :]
    unturned = jnp.concatenate([moved[..., half_dim:], -moved[..., :half_dim]], axis=-1)
    return grads * cosine_table[..., None, :] + unturned


def rms_norm(values, scaling):
    factor = lax.rsqrt(jnp.mean(values * values, axis=-1, keepdims=True) + NORM_EPS)
    return values * factor * scaling


def norm_back(values, grads, scaling):
    factor = lax.rsqrt(jnp.mean(values * values, axis=-1, keepdims=True) + NORM_EPS)
    unit_values = values * factor
    scaled_grads = grads * scaling
    inner = jnp.mean(scaled_grads * unit_values, axis=-1, keepdims=True)
    return (factor * (scaled_grads - unit_values * inner), grads * unit_values)


def attend_block(state, queries, key_value_block, allowed, score_scale):
    running, top_now, total_now = state
    sequence_count, count_of_keys = (key_value_block.shape[1], key_value_block.shape[2])
    block_keys = key_value_block[0].reshape(
        sequence_count, count_of_keys, KEY_VALUE_HEADS, HEAD_SIZE
    )
    block_values = key_value_block[1].reshape(
        sequence_count, count_of_keys, KEY_VALUE_HEADS, HEAD_SIZE
    )
    mask_wide = allowed[:, :, None, None, :]
    scores = (
        jnp.einsum("sqhgd,snhd->sqhgn", queries, block_keys, preferred_element_type=jnp.float32)
        * score_scale
    )
    new_top = jnp.maximum(top_now, jnp.max(jnp.where(mask_wide, scores, MASKED), axis=-1))
    weights = jnp.where(mask_wide, jnp.exp(scores - new_top[..., None]), 0.0)
    factor = jnp.exp(top_now - new_top)
    total_now = total_now * factor + jnp.sum(weights, axis=-1)
    running = running * factor[..., None] + jnp.einsum(
        "sqhgn,snhd->sqhgd",
        weights.astype(jnp.bfloat16),
        block_values,
        preferred_element_type=jnp.float32,
    )
    return (running, new_top, total_now)


def backward_block(
    queries, attention_gradient, log_total, delta, key_value_block, allowed, score_scale
):
    sequence_count, count_of_keys = (key_value_block.shape[1], key_value_block.shape[2])
    block_keys = key_value_block[0].reshape(
        sequence_count, count_of_keys, KEY_VALUE_HEADS, HEAD_SIZE
    )
    block_values = key_value_block[1].reshape(
        sequence_count, count_of_keys, KEY_VALUE_HEADS, HEAD_SIZE
    )
    mask_wide = allowed[:, :, None, None, :]
    scores = (
        jnp.einsum("sqhgd,snhd->sqhgn", queries, block_keys, preferred_element_type=jnp.float32)
        * score_scale
    )
    probabilities = jnp.where(mask_wide, jnp.exp(scores - log_total[..., None]), 0.0)
    value_gradient = jnp.einsum(
        "sqhgn,sqhgd->snhd",
        probabilities.astype(jnp.bfloat16),
        attention_gradient,
        preferred_element_type=jnp.float32,
    )
    grad_probs = jnp.einsum(
        "sqhgd,snhd->sqhgn", attention_gradient, block_values, preferred_element_type=jnp.float32
    )
    grad_scores = (probabilities * (grad_probs - delta[..., None])).astype(jnp.bfloat16)
    grad_queries = (
        jnp.einsum("sqhgn,snhd->sqhgd", grad_scores, block_keys, preferred_element_type=jnp.float32)
        * score_scale
    )
    key_gradient = (
        jnp.einsum("sqhgn,sqhgd->snhd", grad_scores, queries, preferred_element_type=jnp.float32)
        * score_scale
    )
    grad_pair = jnp.stack(
        [
            key_gradient.reshape(sequence_count, count_of_keys, KEY_VALUE_HEADS * HEAD_SIZE),
            value_gradient.reshape(sequence_count, count_of_keys, KEY_VALUE_HEADS * HEAD_SIZE),
        ]
    )
    return (grad_queries, grad_pair)


def sum_feed(grad_w_gate_up, grad_w_down, count_of_shards):
    return lax.psum_scatter(
        pack([grad_w_gate_up, grad_w_down], count_of_shards),
        ("ctx", "fsdp"),
        scatter_dimension=0,
        tiled=True,
    )


def local(tokens, cotangent, stretch_order, doc_lengths, master, first_moment, second_moment):
    cycle_size = lax.axis_size("ctx")
    ctx_index = lax.axis_index("ctx")
    count_of_shards = cycle_size * lax.axis_size("fsdp")
    sequence_count, count_of_rows, _ = tokens.shape
    seq_length = count_of_rows * cycle_size
    query_groups = QUERY_HEADS // KEY_VALUE_HEADS
    score_scale = HEAD_SIZE ** (-0.5)
    gathered = lax.all_gather(master.astype(jnp.bfloat16), ("ctx", "fsdp"), axis=0, tiled=True)
    w_qkv, w_out, w_gate_up, w_down, gain_column = unpack(gathered, count_of_shards)
    gains = gain_column.reshape(-1).astype(jnp.float32)
    g_attn = gains[:MODEL_WIDTH]
    g_mlp = gains[MODEL_WIDTH : 2 * MODEL_WIDTH]
    g_query = gains[2 * MODEL_WIDTH : 2 * MODEL_WIDTH + HEAD_SIZE]
    g_key = gains[2 * MODEL_WIDTH + HEAD_SIZE :]
    query_pos = slot_positions(stretch_order, ctx_index * count_of_rows, count_of_rows)
    query_doc, relative = documents(query_pos, doc_lengths)
    cosine_table, sine_values = rope_tables(relative)
    x_in = tokens.astype(jnp.float32)
    normed_one = rms_norm(x_in, g_attn).astype(jnp.bfloat16)
    projected_output = jnp.einsum(
        "sqd,de->sqe", normed_one, w_qkv, preferred_element_type=jnp.float32
    )
    query_raw = projected_output[:, :, : QUERY_HEADS * HEAD_SIZE].reshape(
        sequence_count, count_of_rows, QUERY_HEADS, HEAD_SIZE
    )
    unrotated_keys = projected_output[
        :, :, QUERY_HEADS * HEAD_SIZE : (QUERY_HEADS + KEY_VALUE_HEADS) * HEAD_SIZE
    ].reshape(sequence_count, count_of_rows, KEY_VALUE_HEADS, HEAD_SIZE)
    unprojected_values = projected_output[:, :, (QUERY_HEADS + KEY_VALUE_HEADS) * HEAD_SIZE :]
    queries = (
        rotate(rms_norm(query_raw, g_query), cosine_table, sine_values)
        .astype(jnp.bfloat16)
        .reshape(sequence_count, count_of_rows, KEY_VALUE_HEADS, query_groups, HEAD_SIZE)
    )
    keys_rot = rotate(rms_norm(unrotated_keys, g_key), cosine_table, sine_values).reshape(
        sequence_count, count_of_rows, KEY_VALUE_HEADS * HEAD_SIZE
    )
    kv_local = jnp.stack([keys_rot, unprojected_values]).astype(jnp.bfloat16)
    statistic_shape = (sequence_count, count_of_rows, KEY_VALUE_HEADS, query_groups)
    initial = (
        jnp.zeros(statistic_shape + (HEAD_SIZE,), jnp.float32),
        jnp.full(statistic_shape, MASKED, jnp.float32),
        jnp.zeros(statistic_shape, jnp.float32),
    )
    state = initial
    piece = lax.all_gather(kv_local, "ctx", axis=2, tiled=True)
    key_total = piece.shape[2]

    def key_step(inner, block_index):
        first_row = block_index * count_of_rows
        key_value_block = lax.dynamic_slice_in_dim(piece, first_row, count_of_rows, 2)
        allowed = key_mask(
            stretch_order, doc_lengths, query_pos, query_doc, first_row, count_of_rows
        )
        return (attend_block(inner, queries, key_value_block, allowed, score_scale), None)

    state, _ = lax.scan(key_step, state, jnp.arange(key_total // count_of_rows, dtype=jnp.int32))
    running, top_now, total_now = state
    attn = running / total_now[..., None]
    log_total = top_now + jnp.log(total_now)
    attn_low = attn.reshape(sequence_count, count_of_rows, QUERY_HEADS * HEAD_SIZE).astype(
        jnp.bfloat16
    )
    resid = x_in + jnp.einsum("sqa,ad->sqd", attn_low, w_out, preferred_element_type=jnp.float32)
    normed_two = rms_norm(resid, g_mlp).astype(jnp.bfloat16)
    gate_up = jnp.einsum("sqd,de->sqe", normed_two, w_gate_up, preferred_element_type=jnp.float32)
    gate = gate_up[:, :, :FEED_WIDTH]
    up_part = gate_up[:, :, FEED_WIDTH:]
    sigmoid_gate = jax.nn.sigmoid(gate)
    hidden = (gate * sigmoid_gate * up_part).astype(jnp.bfloat16)
    mlp_out = jnp.einsum("sqf,fd->sqd", hidden, w_down, preferred_element_type=jnp.float32)
    layer_out = (resid + mlp_out).astype(jnp.bfloat16)
    again = lax.all_gather(master.astype(jnp.bfloat16), ("ctx", "fsdp"), axis=0, tiled=True)
    w_qkv, w_out, w_gate_up, w_down, _ = unpack(again, count_of_shards)
    grad_w_down = jnp.einsum("sqf,sqd->fd", hidden, cotangent, preferred_element_type=jnp.float32)
    grad_hidden = jnp.einsum("sqd,fd->sqf", cotangent, w_down, preferred_element_type=jnp.float32)
    grad_gate = grad_hidden * up_part * sigmoid_gate * (1.0 + gate * (1.0 - sigmoid_gate))
    grad_up = grad_hidden * gate * sigmoid_gate
    grad_gate_up = jnp.concatenate([grad_gate, grad_up], axis=-1).astype(jnp.bfloat16)
    grad_w_gate_up = jnp.einsum(
        "sqd,sqe->de", normed_two, grad_gate_up, preferred_element_type=jnp.float32
    )
    grad_normed_two = jnp.einsum(
        "sqe,de->sqd", grad_gate_up, w_gate_up, preferred_element_type=jnp.float32
    )
    back_two, mlp_gain_terms = norm_back(resid, grad_normed_two, g_mlp)
    grad_resid = cotangent.astype(jnp.float32) + back_two
    grad_branch = grad_resid.astype(jnp.bfloat16)
    grad_w_out = jnp.einsum(
        "sqa,sqd->ad", attn_low, grad_branch, preferred_element_type=jnp.float32
    )
    attention_gradient = jnp.einsum(
        "sqd,ad->sqa", grad_branch, w_out, preferred_element_type=jnp.float32
    ).astype(jnp.bfloat16)
    attention_head_gradient = attention_gradient.reshape(
        sequence_count, count_of_rows, KEY_VALUE_HEADS, query_groups, HEAD_SIZE
    )
    delta = jnp.sum(attention_head_gradient.astype(jnp.float32) * attn, axis=-1)

    def grads_from(turn_index, kv_now, key_value_gradients, grad_queries):
        source_dev = (ctx_index - turn_index) % cycle_size
        allowed = key_mask(
            stretch_order,
            doc_lengths,
            query_pos,
            query_doc,
            source_dev * count_of_rows,
            count_of_rows,
        )
        part_queries, part_pair = backward_block(
            queries, attention_head_gradient, log_total, delta, kv_now, allowed, score_scale
        )
        return (key_value_gradients + part_pair, grad_queries + part_queries)

    def pass_grads(key_value_gradients):
        return from_behind(key_value_gradients.astype(jnp.bfloat16), "ctx", 1).astype(
            key_value_gradients.dtype
        )

    def turn_step(turn_index, state):
        kv_now, key_value_gradients, grad_queries = state
        key_value_gradients, grad_queries = grads_from(
            turn_index, kv_now, key_value_gradients, grad_queries
        )
        kv_now = from_behind(kv_now, "ctx", 1)
        key_value_gradients = pass_grads(key_value_gradients)
        return (kv_now, key_value_gradients, grad_queries)

    start_state = (
        kv_local,
        jnp.zeros(kv_local.shape, jnp.float32),
        jnp.zeros(statistic_shape + (HEAD_SIZE,), jnp.float32),
    )
    kv_now, key_value_gradients, grad_queries = lax.fori_loop(
        0, cycle_size - 1, turn_step, start_state
    )
    key_value_gradients, grad_queries = grads_from(
        cycle_size - 1, kv_now, key_value_gradients, grad_queries
    )
    key_value_gradients = pass_grads(key_value_gradients)
    grad_query_rot = rotate_back(
        grad_queries.reshape(sequence_count, count_of_rows, QUERY_HEADS, HEAD_SIZE),
        cosine_table,
        sine_values,
    )
    grad_key_rot = rotate_back(
        key_value_gradients[0].reshape(sequence_count, count_of_rows, KEY_VALUE_HEADS, HEAD_SIZE),
        cosine_table,
        sine_values,
    )
    grad_query_raw, query_gain_terms = norm_back(query_raw, grad_query_rot, g_query)
    unrotated_key_gradient, key_gain_terms = norm_back(unrotated_keys, grad_key_rot, g_key)
    grad_projected = jnp.concatenate(
        [
            grad_query_raw.reshape(sequence_count, count_of_rows, QUERY_HEADS * HEAD_SIZE),
            unrotated_key_gradient.reshape(
                sequence_count, count_of_rows, KEY_VALUE_HEADS * HEAD_SIZE
            ),
            key_value_gradients[1],
        ],
        axis=-1,
    ).astype(jnp.bfloat16)
    grad_w_qkv = jnp.einsum(
        "sqd,sqe->de", normed_one, grad_projected, preferred_element_type=jnp.float32
    )
    grad_normed_one = jnp.einsum(
        "sqe,de->sqd", grad_projected, w_qkv, preferred_element_type=jnp.float32
    )
    back_one, attn_gain_terms = norm_back(x_in, grad_normed_one, g_attn)
    input_grad = (grad_resid + back_one).astype(jnp.bfloat16)
    grad_gains = jnp.concatenate(
        [
            jnp.sum(attn_gain_terms, axis=(0, 1)),
            jnp.sum(mlp_gain_terms, axis=(0, 1)),
            jnp.sum(query_gain_terms, axis=(0, 1, 2)),
            jnp.sum(key_gain_terms, axis=(0, 1, 2)),
        ]
    ).reshape(-1, 1)
    mlp_share = sum_feed(grad_w_gate_up, grad_w_down, count_of_shards)
    late_share = lax.psum_scatter(
        pack([grad_w_qkv, grad_w_out, grad_gains], count_of_shards),
        ("ctx", "fsdp"),
        scatter_dimension=0,
        tiled=True,
    )
    head_span = (
        MODEL_WIDTH // count_of_shards * (QUERY_HEADS + 2 * KEY_VALUE_HEADS) * HEAD_SIZE
        + QUERY_HEADS * HEAD_SIZE // count_of_shards * MODEL_WIDTH
    )
    grad = jnp.concatenate([late_share[:head_span], mlp_share, late_share[head_span:]])
    step_rate, decay_value = rate_rows(count_of_shards, seq_length)
    new_first = BETA_ONE * first_moment + (1.0 - BETA_ONE) * grad
    new_second = BETA_TWO * second_moment + (1.0 - BETA_TWO) * grad * grad
    normalized = (
        new_first
        / (1.0 - BETA_ONE**STEP)
        / (jnp.sqrt(new_second / (1.0 - BETA_TWO**STEP)) + ADAM_EPS)
    )
    new_master = master - step_rate * (normalized + decay_value * master)
    return (layer_out, input_grad, new_master, new_first, new_second)


def solution(mesh):
    placed = (
        P("fsdp", "ctx", None),
        P("fsdp", "ctx", None),
        P(),
        P("fsdp", None),
        P(("ctx", "fsdp")),
        P(("ctx", "fsdp")),
        P(("ctx", "fsdp")),
    )
    return jax.shard_map(
        local,
        mesh=mesh,
        in_specs=placed,
        out_specs=(
            P("fsdp", "ctx", None),
            P("fsdp", "ctx", None),
            P(("ctx", "fsdp")),
            P(("ctx", "fsdp")),
            P(("ctx", "fsdp")),
        ),
        check_vma=False,
    )
```

profile of v0, /device:TPU:0, one launch (start us, length us, event | category | flops | bytes accessed | tf_op | source)
XLA Modules:
  0.0 2090.7 jit_solution(8948685709211337413)
XLA Ops:
  8.9 10.3 broadcast.1489
  19.2 16.1 dynamic-update-slice
  43.1 470.9 %all-reduce.7.cloned.1.call-done = bf16[15730944]{0:T(1024)(128)(2,1)} async-done(((bf16[15730944]{0:T(1024)(128)(2,1)}), bf16[15730944]{0:T(1024)(128)(2,1)}) %all-reduce.7.cloned.1.call-update) | async-done | bytes 31461904
  514.0 77.9 %reshape.1920 = bf16[32,491592]{1,0:T(8,128)(2,1)} reshape(bf16[15730944]{0:T(1024)(128)(2,1)} %all-reduce.7.cloned.1.call-done) | data formatting | bytes 62923776 | tf_op jit(solution)/shard_map/reshape | solution.py:40
  591.9 7.2 slice.186
  601.0 8.9 reshape.1922
  636.5 10.5 slice.198
  658.9 7.2 reshape.1930
  666.2 12.1 reshape.1928
  684.5 54.2 %while.38 = (s32[]{:T(128)}, f32[1,128,8,2,128]{1,4,3,2,0:T(8,128)S(1)}, f32[1,128,8,2]{1,3,2,0:T(2,128)}, f32[1,128,8,2]{1,3,2,0:T(2,128)}, s32[1,128]{1,0:T(1,...) while((s32[]{:T(128)}, ...), condition=%wide.region_12.13_spmd.clone, body=%wide.region_7.12_spmd.clone.sunk | while | flops 137435392 | bytes 10786759 | solution.py:275
  743.7 6.6 convolution_bitcast_fusion.3
  754.5 7.2 fusion.89
  768.8 151.2 %while.39 = (s32[]{:T(128)}, bf16[2,1,128,1024]{2,3,1,0:T(8,128)(2,1)}, f32[2,1,128,1024]{2,3,1,0:T(8,128)}, f32[1,128,8,2,128]{4,1,3,2,0:T(8,128)}, s32[1,128]{...) while((s32[]{:T(128)}, ...), condition=%wide.region_19.20_spmd.clone, body=%wide.region_16.19_spmd.clone.sunk | while | flops 339667200 | bytes 33871928 | solution.py:352
  777.0 7.8 collective-permute-done.1
  797.7 8.7 collective-permute-done.1
  818.6 9.3 collective-permute-done.1
  840.2 9.3 collective-permute-done.1
  861.8 9.3 collective-permute-done.1
  883.4 9.3 collective-permute-done.1
  904.9 9.3 collective-permute-done.1
  940.8 10.5 fusion.55
  965.1 7.6 reshape.1943
  979.1 10.0 reshape.1947
  989.0 26.4 %reshape.1946 = f32[32,196608]{1,0:T(8,128)} reshape(f32[1024,6144]{1,0:T(8,128)} %fusion.55) | data formatting | bytes 50331648 | tf_op jit(solution)/shard_map/reshape | solution.py:52
  1015.4 24.9 %maximum_bitcast_fusion = f32[4,2304,8,128]{3,2,1,0:T(8,128)} fusion(f32[32,98304]{1,0:T(8,128)} %reshape.1947, f32[32,196608]{1,0:T(8,128)} %reshape.1946), kind=kLoop, calls=%fused_computation.73 | loop fusion | flops 9437184 | bytes 75497472
  1040.3 33.5 %copy.279 = f32[4,2304,8,128]{3,1,2,0:T(8,128)} copy(f32[4,2304,8,128]{3,2,1,0:T(8,128)} %maximum_bitcast_fusion) | data formatting | bytes 75497472
  1084.3 7.1 fusion.72
  1091.4 8.3 fusion.97
  1100.5 12.3 reshape.1942
  1112.7 20.5 pad_maximum_fusion
  1133.2 31.1 %reshape.1945 = f32[6293760]{0:T(1024)} reshape(f32[32,196680]{1,0:T(8,128)} %pad_maximum_fusion) | data formatting | bytes 50350080 | tf_op jit(solution)/shard_map/reshape | solution.py:53
  1176.9 897.0 %all-reduce.9.cloned.1.call-done = (f32[6293760]{0:T(1024)}, f32[9437184]{0:T(1024)}) async-done(((f32[6293760]{0:T(1024)}, f32[9437184]{0:T(1024)}), (f32[6293760]{0:T(1024)}, f32[9437184]{0:T(1024)})) %all-reduce.9.cloned.1.call-update) | async-done | bytes 62923792
  (690 shorter events, 281.5 us)
Async XLA Ops:
  7.2 506.8 %all-reduce.7.cloned.1.call-start = ((), (), s32[]{:S(2)}) async-start(), calls=%async_computation.1 | async-start | bytes 62926848
  35.3 649.2 %all-gather.2.cloned.1.call-start = ((), (), s32[]{:S(2)}) async-start(), calls=%async_computation | async-start | bytes 4718592 | tf_op jit(solution)/shard_map/all_gather | solution.py:264
  38.1 553.8 %copy-start.87 = (s32[128]{0:T(128)}, s32[128]{0:T(128)S(1)}, u32[]{:S(2)}) copy-start(s32[128]{0:T(128)S(1)} %get-tuple-element.810) | copy-start | bytes 1540
  38.1 586.6 %copy-start.73 = (s32[128]{0:T(128)}, s32[128]{0:T(128)S(1)}, u32[]{:S(2)}) copy-start(s32[128]{0:T(128)S(1)} %get-tuple-element.1031) | copy-start | bytes 1540
  40.9 550.9 %copy-start.55 = (f32[128,128]{1,0:T(8,128)}, f32[128,128]{1,0:T(8,128)S(1)}, u32[]{:S(2)}) copy-start(f32[128,128]{1,0:T(8,128)S(1)} %copy.200) | copy-start | bytes 196612
  42.0 581.5 %copy-start.53 = (f32[128,128]{1,0:T(8,128)}, f32[128,128]{1,0:T(8,128)S(1)}, u32[]{:S(2)}) copy-start(f32[128,128]{1,0:T(8,128)S(1)} %copy.199) | copy-start | bytes 196612
  43.1 566.7 %copy-start.81 = (f32[128]{0:T(128)}, f32[128]{0:T(128)S(1)}, u32[]{:S(2)}) copy-start(f32[128]{0:T(128)S(1)} %add_rsqrt_fusion.3) | copy-start | bytes 1540
  622.5 1451.4 %all-reduce.9.cloned.1.call-start = ((), (), s32[]{:S(2)}) async-start(), calls=%async_computation.2 | async-start | bytes 125853696
  649.2 34.2 %copy-start.7 = (f32[1,128,2048]{1,2,0:T(8,128)}, f32[1,128,2048]{1,2,0:T(8,128)S(1)}, u32[]{:S(2)}) copy-start(f32[1,128,2048]{1,2,0:T(8,128)S(1)} %copy.255) | copy-start | bytes 3145732
  649.4 34.1 %copy-start.71 = (f32[128,16]{0,1:T(8,128)}, f32[128,16]{0,1:T(8,128)S(1)}, u32[]{:S(2)}) copy-start(f32[128,16]{0,1:T(8,128)S(1)} %add_rsqrt_fusion.1) | copy-start | bytes 24580
  768.8 152.3 %copy-start.75 = (pred[128,128]{0,1:T(8,128)(4,1)S(1)}, pred[128,128]{0,1:T(8,128)(4,1)}, u32[]{:S(2)}) copy-start(pred[128,128]{0,1:T(8,128)(4,1)} %compare_and_fusion.2) | copy-start | bytes 49156
  775.0 9.8 collective-permute-start.1
  775.0 15.4 collective-permute-start
  796.6 9.8 collective-permute-start.1
  796.6 15.4 collective-permute-start
  818.1 9.8 collective-permute-start.1
  818.1 15.4 collective-permute-start
  839.7 9.8 collective-permute-start.1
  839.7 15.4 collective-permute-start
  861.3 9.8 collective-permute-start.1
  861.3 15.4 collective-permute-start
  882.9 9.8 collective-permute-start.1
  882.9 15.4 collective-permute-start
  904.4 9.8 collective-permute-start.1
  904.4 15.4 collective-permute-start
  958.2 117.2 %collective-permute-start.2 = (bf16[2,1,128,1024]{3,2,1,0:T(8,128)(2,1)}, bf16[2,1,128,1024]{3,2,1,0:T(8,128)(2,1)S(1)}, u32[]{:S(2)}, u32[]{:S(2)}) collective-permute-start(bf16[2,1,128,1024]{3,2,1,0:T(8,128)(2,1)} %fusion.54), channel_id=1, source_target_pairs={{0,4},{4,8},{8,12},{12,16},{16,20},{20,24},{24,28},{28,0},{1,5},{5... | collective-permute-start | bytes 1572872 | tf_op jit(solution)/shard_map/ppermute | solution.py:26
  1040.3 33.6 %copy-start.34 = (f32[1,128,2048]{2,1,0:T(8,128)S(1)}, f32[1,128,2048]{2,1,0:T(8,128)}, u32[]{:S(2)}) copy-start(f32[1,128,2048]{2,1,0:T(8,128)} %mul.991) | copy-start | bytes 3145732
  1040.3 33.6 %copy-start.35 = (f32[1,128,2048]{2,1,0:T(8,128)S(1)}, f32[1,128,2048]{2,1,0:T(8,128)}, u32[]{:S(2)}) copy-start(f32[1,128,2048]{2,1,0:T(8,128)} %mul.971) | copy-start | bytes 3145732
  1040.3 33.6 %copy-start.36 = (f32[1,128,2048]{2,1,0:T(8,128)S(1)}, f32[1,128,2048]{2,1,0:T(8,128)}, u32[]{:S(2)}) copy-start(f32[1,128,2048]{2,1,0:T(8,128)} %mul.1004) | copy-start | bytes 3145732
  1040.3 33.6 %copy-start.37 = (f32[1,128,2048]{2,1,0:T(8,128)S(1)}, f32[1,128,2048]{2,1,0:T(8,128)}, u32[]{:S(2)}) copy-start(f32[1,128,2048]{2,1,0:T(8,128)} %concatenate.138) | copy-start | bytes 3145732
  1040.3 33.6 %copy-start.78 = (f32[2048]{0:T(1024)S(1)}, f32[2048]{0:T(1024)}, u32[]{:S(2)}) copy-start(f32[2048]{0:T(1024)} %broadcast_bitcast_fusion) | copy-start | bytes 24580
  1176.9 900.7 %copy-start.24 = (f32[491592]{0:T(1024)S(1)}, f32[491592]{0:T(1024)}, u32[]{:S(2)}) copy-start(f32[491592]{0:T(1024)} %param.15) | copy-start | bytes 5899108
  (130 other events, 586.8 us)
Sparse Core Ops, SparseCore 0:
  35.4 478.5 all-reduce.6
  622.6 35.2 all-gather.1
  1164.4 909.4 all-reduce.8
where the time goes:
time: 2100 us; the launch traced here: 2090 us
  waiting for transfers between devices  1460 us (70%)
  local copies, waits for them, and re-layouts  386 us (18%)
  other arithmetic  128 us (6%)
  matrix products  96.7 us (5%)
    unnamed x5, waiting for transfers between devices  1370 us
    ppermute x15, waiting for transfers between devices, from_behind(): return lax.ppermute(x, axis, [(i, (i + by) % peers) for i in range(peers)])  87.8 us
    reshape x1, local copies, waits for them, and re-layouts, unpack(): param_table = flat_params.reshape(count_of_shards, -1)  77.9 us
    unnamed x198, local copies, waits for them, and re-layouts  76.4 us
    reshape x4, local copies, waits for them, and re-layouts, pack(): matrix.reshape(count_of_shards, -1)  56.2 us
  transfers between devices with their start and end apart: 18, of which 16 were waited for; matrix products, arithmetic and copies ran while one was open for 10% of the time, Pallas kernels for 0%

commit v1 on v0

--- a/solution.py
+++ b/solution.py
@@ -1,6 +1,10 @@
+import functools
+
 import jax
 import jax.numpy as jnp
 from jax import lax
+from jax.experimental import pallas as pl
+from jax.experimental.pallas import tpu as pltpu
 from jax.sharding import PartitionSpec as P
 
 MODEL_WIDTH = 1024
@@ -206,12 +210,9 @@
     return (grad_queries, grad_pair)
 
 
-def sum_feed(grad_w_gate_up, grad_w_down, count_of_shards):
+def summed(part, count_of_shards):
     return lax.psum_scatter(
-        pack([grad_w_gate_up, grad_w_down], count_of_shards),
-        ("ctx", "fsdp"),
-        scatter_dimension=0,
-        tiled=True,
+        part.reshape(-1), ("ctx", "fsdp"), scatter_dimension=0, tiled=True
     )
 
 
@@ -288,8 +289,6 @@
     hidden = (gate * sigmoid_gate * up_part).astype(jnp.bfloat16)
     mlp_out = jnp.einsum("sqf,fd->sqd", hidden, w_down, preferred_element_type=jnp.float32)
     layer_out = (resid + mlp_out).astype(jnp.bfloat16)
-    again = lax.all_gather(master.astype(jnp.bfloat16), ("ctx", "fsdp"), axis=0, tiled=True)
-    w_qkv, w_out, w_gate_up, w_down, _ = unpack(again, count_of_shards)
     grad_w_down = jnp.einsum("sqf,sqd->fd", hidden, cotangent, preferred_element_type=jnp.float32)
     grad_hidden = jnp.einsum("sqd,fd->sqf", cotangent, w_down, preferred_element_type=jnp.float32)
     grad_gate = grad_hidden * up_part * sigmoid_gate * (1.0 + gate * (1.0 - sigmoid_gate))
@@ -394,19 +393,831 @@
             jnp.sum(key_gain_terms, axis=(0, 1, 2)),
         ]
     ).reshape(-1, 1)
-    mlp_share = sum_feed(grad_w_gate_up, grad_w_down, count_of_shards)
-    late_share = lax.psum_scatter(
-        pack([grad_w_qkv, grad_w_out, grad_gains], count_of_shards),
-        ("ctx", "fsdp"),
-        scatter_dimension=0,
-        tiled=True,
-    )
-    head_span = (
-        MODEL_WIDTH // count_of_shards * (QUERY_HEADS + 2 * KEY_VALUE_HEADS) * HEAD_SIZE
-        + QUERY_HEADS * HEAD_SIZE // count_of_shards * MODEL_WIDTH
-    )
-    grad = jnp.concatenate([late_share[:head_span], mlp_share, late_share[head_span:]])
-    step_rate, decay_value = rate_rows(count_of_shards, seq_length)
+    grad = jnp.concatenate(
+        [
+            summed(part, count_of_shards)
+            for part in (grad_w_qkv, grad_w_out, grad_w_gate_up, grad_w_down, grad_gains)
+        ]
+    )
+    new_master, new_first, new_second = adam(
+        grad, master, first_moment, second_moment, count_of_shards, seq_length
+    )
+    return (layer_out, input_grad, new_master, new_first, new_second)
+
+
+MESH = pl.DeviceIdType.MESH
+F32 = jnp.float32
+BF16 = jnp.bfloat16
+CTX = 8
+CHIPS = 4
+GROUP = QUERY_HEADS // KEY_VALUE_HEADS
+QCOLS = GROUP * HEAD_SIZE
+PCOLS = QCOLS + 2 * HEAD_SIZE
+HID = FEED_WIDTH // CTX
+GAIN_WIDTH = 2 * MODEL_WIDTH + 2 * HEAD_SIZE
+TILE = 256
+
+
+def dot(a, b, dims=((1,), (0,))):
+    return lax.dot_general(a, b, (dims, ((), ())), preferred_element_type=F32)
+
+
+NT = ((1,), (1,))
+TN = ((0,), (0,))
+
+
+def layer_kernel(
+    zsize,
+    x_ref,
+    cot_ref,
+    wq_in,
+    wo_in,
+    wgu_in,
+    wd_in,
+    gains_in,
+    cos_ref,
+    sin_ref,
+    kpos_ref,
+    qpos_ref,
+    qstart_ref,
+    out_ref,
+    xgrad_ref,
+    gq_ref,
+    go_ref,
+    ggu_ref,
+    gd_ref,
+    gg_ref,
+    n1,
+    cot,
+    n2,
+    gb,
+    wq,
+    wo,
+    wgu,
+    wd,
+    qraw,
+    kraw,
+    q_s,
+    k_s,
+    v_s,
+    kt_s,
+    vt_s,
+    probs,
+    attn,
+    attn_low,
+    hidden,
+    ggu,
+    gattn,
+    dq_s,
+    dk_s,
+    dv_s,
+    gp,
+    psnd,
+    prcv,
+    csnd,
+    crcv,
+    own,
+    acc,
+    resid_s,
+    gresid_s,
+    gwq,
+    gwo,
+    gwgu,
+    gwd,
+    lwq,
+    lwo,
+    lwgu,
+    lwd,
+    asq,
+    asg,
+    arg_,
+    gz,
+    gpl,
+    gains,
+    hz,
+    hpl,
+    hrow,
+    ag_s,
+    ag_r,
+    rs_ps,
+    rs_pr,
+    rs_cs,
+    rs_cr,
+    a2a_s,
+    a2a_r,
+    zg_s,
+    zg_r,
+    g_s,
+    g_r,
+    loc,
+):
+    c = lax.axis_index("ctx")
+    z = lax.axis_index("fsdp")
+    core = c % 2
+    chip = c // 2
+    cx = chip % 2
+    cy = chip // 2
+    slot = core * CHIPS + chip
+    sib = c + 1 - 2 * core
+    tiles = n1.shape[0] * n1.shape[1] // TILE
+    rows = n1.shape[1]
+    half = CHIPS * rows
+
+    def chip_at(i):
+        return ((cy + i // 2) % 2) * 2 + (cx + i % 2) % 2
+
+    def rcopy(src, dst, ssem, rsem, to_c, to_z):
+        return pltpu.make_async_remote_copy(
+            src_ref=src,
+            dst_ref=dst,
+            send_sem=ssem,
+            recv_sem=rsem,
+            device_id=(to_c, to_z),
+            device_id_type=MESH,
+        )
+
+    def loop(lo, hi, body):
+        def step(i, carry):
+            body(i)
+            return carry
+
+        lax.fori_loop(lo, hi, step, 0)
+
+    barrier = pltpu.get_barrier_semaphore()
+
+    def greet_plane(i):
+        pl.semaphore_signal(
+            barrier, inc=1, device_id=((c + i) % CTX, z), device_id_type=MESH
+        )
+
+    def greet_z(i):
+        pl.semaphore_signal(
+            barrier, inc=1, device_id=(c, (z + i) % zsize), device_id_type=MESH
+        )
+
+    loop(1, CTX, greet_plane)
+    loop(1, zsize, greet_z)
+    pl.semaphore_wait(barrier, CTX - 1 + zsize - 1)
+
+    def ag_direct(n, buf, i):
+        if i == 0:
+            return rcopy(buf.at[slot], buf.at[slot], ag_s.at[n, 0], ag_r.at[n, 0], sib, z)
+        return rcopy(
+            buf.at[slot],
+            buf.at[slot],
+            ag_s.at[n, i],
+            ag_r.at[n, i],
+            chip_at(i) * 2 + core,
+            z,
+        )
+
+    def ag_landed(n, buf, i):
+        there = core * CHIPS + chip_at(i)
+        return rcopy(buf.at[there], buf.at[there], ag_s.at[n, i], ag_r.at[n, i], sib, z)
+
+    def ag_forward(n, buf, i):
+        there = core * CHIPS + chip_at(i)
+        return rcopy(buf.at[there], buf.at[there], ag_s.at[n, 3 + i], ag_r.at[n, 3 + i], sib, z)
+
+    def ag_forwarded(n, buf, i):
+        there = (1 - core) * CHIPS + chip_at(i)
+        return rcopy(buf.at[there], buf.at[there], ag_s.at[n, 3 + i], ag_r.at[n, 3 + i], sib, z)
+
+    def ag_start(n, buf):
+        for i in (3, 1, 2, 0):
+            ag_direct(n, buf, i).start()
+
+    def ag_pass(n, buf):
+        for i in (1, 2, 3):
+            ag_landed(n, buf, i).wait_recv()
+            ag_forward(n, buf, i).start()
+
+    def ag_finish(n, buf):
+        other = (1 - core) * CHIPS + chip
+        rcopy(buf.at[other], buf.at[other], ag_s.at[n, 0], ag_r.at[n, 0], sib, z).wait_recv()
+        for i in (1, 2, 3):
+            ag_forwarded(n, buf, i).wait_recv()
+
+    def ag_drain(n, buf):
+        for i in range(4):
+            ag_direct(n, buf, i).wait_send()
+        for i in (1, 2, 3):
+            ag_forward(n, buf, i).wait_send()
+
+    def rs_pair(r):
+        return rcopy(psnd, prcv.at[r], rs_ps.at[r], rs_pr.at[r], sib, z)
+
+    def rs_chip(r, i):
+        return rcopy(
+            csnd.at[i - 1],
+            crcv.at[r, i - 1],
+            rs_cs.at[r, i - 1],
+            rs_cr.at[r, i - 1],
+            chip_at(i) * 2 + core,
+            z,
+        )
+
+    def rs_start(r, part):
+        if r > 0:
+            rs_pair(r - 1).wait_send()
+
+        def give(n):
+            cols = pl.ds(pl.multiple_of(n * TILE, TILE), TILE)
+            psnd[:, :, cols] = part(1 - core, n).astype(BF16).reshape(CHIPS, rows, TILE)
+
+        def keep(n):
+            cols = pl.ds(pl.multiple_of(n * TILE, TILE), TILE)
+            own[:, :, cols] = part(core, n).reshape(CHIPS, rows, TILE)
+
+        loop(0, MODEL_WIDTH // TILE, give)
+        rs_pair(r).start()
+        loop(0, MODEL_WIDTH // TILE, keep)
+        if r > 0:
+            for i in (1, 2, 3):
+                rs_chip(r - 1, i).wait_send()
+        rs_pair(r).wait_recv()
+        for i in (3, 1, 2):
+            there = chip_at(i)
+            csnd[i - 1] = (own[there] + prcv[r, there].astype(F32)).astype(BF16)
+            rs_chip(r, i).start()
+        acc[r] = own[chip] + prcv[r, chip].astype(F32)
+
+    def rs_finish(r):
+        total = acc[r]
+        for i in (1, 2, 3):
+            rs_chip(r, i).wait_recv()
+            total = total + crcv[r, i - 1].astype(F32)
+        return total
+
+    def a2a(n, src, dst_of, i):
+        to = (c + i) % CTX
+        return rcopy(src.at[to], dst_of(c), a2a_s.at[n, i], a2a_r.at[n, i], to, z)
+
+    def a2a_landed(n, dst_of, i):
+        frm = (c + CTX - i) % CTX
+        return rcopy(dst_of(frm), dst_of(frm), a2a_s.at[n, i], a2a_r.at[n, i], sib, z)
+
+    def a2a_start(n, src, dst_of):
+        loop(1, CTX, lambda i: a2a(n, src, dst_of, i).start())
+
+    def a2a_wait(n, dst_of):
+        loop(1, CTX, lambda i: a2a_landed(n, dst_of, i).wait_recv())
+
+    def a2a_drain(n, src, dst_of):
+        loop(1, CTX, lambda i: a2a(n, src, dst_of, i).wait_send())
+
+    def zg(n, src, dst_of, i):
+        return rcopy(src, dst_of(z), zg_s.at[n, i], zg_r.at[n, i], c, (z + i) % zsize)
+
+    def zg_landed(n, dst_of, i):
+        there = dst_of((z + zsize - i) % zsize)
+        return rcopy(there, there, zg_s.at[n, i], zg_r.at[n, i], sib, z)
+
+    def zg_start(n, src, dst_of):
+        for i in range(1, zsize):
+            zg(n, src, dst_of, i).start()
+
+    def zg_wait(n, dst_of):
+        for i in range(1, zsize):
+            zg_landed(n, dst_of, i).wait_recv()
+
+    def zg_drain(n, src, dst_of):
+        for i in range(1, zsize):
+            zg(n, src, dst_of, i).wait_send()
+
+    def zr(n, src_of, land, i):
+        to = (z + i) % zsize
+        return rcopy(src_of(to), land.at[i - 1], zg_s.at[n, i], zg_r.at[n, i], c, to)
+
+    def zr_start(n, src_of, land):
+        for i in range(1, zsize):
+            zr(n, src_of, land, i).start()
+
+    def zr_finish(n, src_of, land):
+        total = src_of(z)[...].astype(F32)
+        for i in range(1, zsize):
+            zr(n, src_of, land, i).wait_recv()
+            total = total + land[i - 1].astype(F32)
+        return total
+
+    def zr_drain(n, src_of, land):
+        for i in range(1, zsize):
+            zr(n, src_of, land, i).wait_send()
+
+    def row_z(n, src, land, i):
+        return rcopy(src, land.at[z], g_s.at[n, i], g_r.at[n, i], c, (z + i) % zsize)
+
+    def row_plane(n, src, land, i):
+        return rcopy(
+            src, land.at[c], g_s.at[n, zsize + i], g_r.at[n, zsize + i], (c + i) % CTX, z
+        )
+
+    def row_z_wait(n, land):
+        def one(i):
+            there = land.at[(z + zsize - i) % zsize]
+            rcopy(there, there, g_s.at[n, i], g_r.at[n, i], sib, z).wait_recv()
+
+        loop(1, zsize, one)
+
+    def row_plane_wait(n, land):
+        def one(i):
+            there = land.at[(c + CTX - i) % CTX]
+            rcopy(there, there, g_s.at[n, zsize + i], g_r.at[n, zsize + i], sib, z).wait_recv()
+
+        loop(1, CTX, one)
+
+    wq_at = lambda j: wq.at[j, z]
+    wgu_at = lambda j: wgu.at[j, z]
+    wq_z = lambda j: wq.at[:, j]
+    wgu_z = lambda j: wgu.at[:, j]
+    wo_z = lambda j: wo.at[j]
+    wd_z = lambda j: wd.at[j]
+
+    gz[z] = gains_in[...]
+    loop(1, zsize, lambda i: row_z(0, gains_in, gz, i).start())
+    a2a_start(0, wq_in, wq_at)
+    wq[c, z] = wq_in[c]
+    wo[z] = wo_in[...]
+    wd[z] = wd_in[...]
+    wgu[c, z] = wgu_in[c]
+    cot[slot] = cot_ref[...]
+
+    row_z_wait(0, gz)
+    gpl[c] = jnp.sum(gz[...], axis=0)
+    loop(1, CTX, lambda i: row_plane(0, gpl.at[c], gpl, i).start())
+
+    a2a_wait(0, wq_at)
+    zg_start(0, wq_z(z), wq_z)
+    zg_start(1, wo_in, wo_z)
+    a2a_start(1, wgu_in, wgu_at)
+
+    row_plane_wait(0, gpl)
+    gains[...] = jnp.sum(gpl[...], axis=0)
+    g_attn = gains[:, :MODEL_WIDTH]
+    x_own = x_ref[...].astype(F32)
+    s_one = lax.rsqrt(jnp.mean(x_own * x_own, axis=-1, keepdims=True) + NORM_EPS)
+    n1[slot] = (x_own * s_one * g_attn).astype(BF16)
+    ag_start(0, n1)
+    a2a_wait(1, wgu_at)
+    ag_pass(0, n1)
+    ag_finish(0, n1)
+    ag_start(1, cot)
+    zg_wait(0, wq_z)
+    zg_start(2, wgu_z(z), wgu_z)
+
+    g_query = gains[:, 2 * MODEL_WIDTH : 2 * MODEL_WIDTH + HEAD_SIZE]
+    g_key = gains[:, 2 * MODEL_WIDTH + HEAD_SIZE :]
+
+    def tile_rows(t):
+        return pl.ds(pl.multiple_of(t * TILE, TILE), TILE)
+
+    def two(buf, t):
+        return buf[pl.ds(t * (TILE // rows), TILE // rows)].reshape(TILE, buf.shape[-1])
+
+    def turned(v):
+        return pltpu.roll(v, HEAD_SIZE // 2, 1)
+
+    def project(t):
+        at = tile_rows(t)
+        cosine, sine = cos_ref[at, :], sin_ref[at, :]
+
+        def normed(raw, gain):
+            scale = lax.rsqrt(jnp.mean(raw * raw, axis=-1, keepdims=True) + NORM_EPS)
+            y = raw * scale * gain
+            return y * cosine + turned(y) * sine
+
+        out = dot(two(n1, t), wq[...].reshape(MODEL_WIDTH, PCOLS))
+        for h in range(GROUP):
+            raw = out[:, h * HEAD_SIZE : (h + 1) * HEAD_SIZE]
+            qraw[at, h * HEAD_SIZE : (h + 1) * HEAD_SIZE] = raw
+            q_s[h, at, :] = normed(raw, g_query).astype(BF16)
+        raw = out[:, QCOLS : QCOLS + HEAD_SIZE]
+        kraw[at, :] = raw
+        keys = normed(raw, g_key)
+        values = out[:, QCOLS + HEAD_SIZE :]
+        k_s[at, :] = keys.astype(BF16)
+        v_s[at, :] = values.astype(BF16)
+        kt_s[:, at] = keys.T.astype(BF16)
+        vt_s[:, at] = values.T.astype(BF16)
+
+    loop(0, tiles, project)
+    ag_pass(1, cot)
+
+    scale = HEAD_SIZE ** (-0.5)
+
+    def attend(t):
+        at = tile_rows(t)
+        kpos = kpos_ref[...]
+        kept = (kpos <= qpos_ref[:, at]) & (kpos >= qstart_ref[:, at])
+        for h in range(GROUP):
+            scores = jnp.where(kept, dot(k_s[...], q_s[h, at, :], NT) * scale, MASKED)
+            weights = jnp.exp(scores - jnp.max(scores, axis=0, keepdims=True))
+            share = 1.0 / jnp.sum(weights, axis=0, keepdims=True)
+            low = (weights * share).astype(BF16)
+            probs[h, t] = low
+            mixed = dot(vt_s[...], low).T
+            attn[at, h * HEAD_SIZE : (h + 1) * HEAD_SIZE] = mixed
+            attn_low[at, h * HEAD_SIZE : (h + 1) * HEAD_SIZE] = mixed.astype(BF16)
+
+    loop(0, tiles, attend)
+
+    zg_wait(1, wo_z)
+    zg_start(3, wd_in, wd_z)
+
+    def n_cols(n):
+        return pl.ds(pl.multiple_of(n * TILE, TILE), TILE)
+
+    def half_rows(which):
+        return pl.ds(pl.multiple_of(which * half, half), half)
+
+    def half_slots(buf, which):
+        return buf[pl.ds(which * CHIPS, CHIPS)].reshape(half, buf.shape[-1])
+
+    def out_part(which, n):
+        return dot(
+            attn_low[half_rows(which), :], wo[:, :, n_cols(n)].reshape(QCOLS, TILE)
+        )
+
+    rs_start(0, out_part)
+    ag_finish(1, cot)
+    resid = x_ref[...].astype(F32) + rs_finish(0)
+    resid_s[...] = resid
+    g_mlp = gains[:, MODEL_WIDTH : 2 * MODEL_WIDTH]
+    s_two = lax.rsqrt(jnp.mean(resid * resid, axis=-1, keepdims=True) + NORM_EPS)
+    n2[slot] = (resid * s_two * g_mlp).astype(BF16)
+    ag_start(2, n2)
+    ag_pass(2, n2)
+    ag_finish(2, n2)
+
+    zg_wait(2, wgu_z)
+    zg_wait(3, wd_z)
+
+    def feed(t):
+        at = tile_rows(t)
+        both = dot(two(n2, t), wgu[...].reshape(MODEL_WIDTH, 2 * HID))
+        ghid = dot(two(cot, t), wd[...].reshape(HID, MODEL_WIDTH), NT)
+        gate, up = both[:, :HID], both[:, HID:]
+        sig = 1.0 / (1.0 + jnp.exp(-gate))
+        silu = gate * sig
+        hidden[at, :] = (silu * up).astype(BF16)
+        ggu[at, :HID] = (ghid * up * sig * (1.0 + gate * (1.0 - sig))).astype(BF16)
+        ggu[at, HID:] = (ghid * silu).astype(BF16)
+
+    loop(0, tiles, feed)
+
+    def back_two_part(which, n):
+        per = MODEL_WIDTH // CTX
+        there = wgu[pl.ds(n * (TILE // per), TILE // per)].reshape(TILE, 2 * HID)
+        return dot(ggu[half_rows(which), :], there, NT)
+
+    rs_start(1, back_two_part)
+
+    def down_grad(n):
+        there = cot[:, :, n_cols(n)].reshape(2 * half, TILE)
+        gwd[:, :, n_cols(n)] = (
+            dot(hidden[...], there, TN).astype(BF16).reshape(zsize, HID // zsize, TILE)
+        )
+
+    loop(0, MODEL_WIDTH // TILE, down_grad)
+    gwd_z = lambda j: gwd.at[j]
+    zr_start(4, gwd_z, lwd)
+
+    def gate_up_grad(n):
+        per = MODEL_WIDTH // CTX
+        there = n2[:, :, n_cols(n)].reshape(2 * half, TILE)
+        gwgu[pl.ds(n * (TILE // per), TILE // per)] = (
+            dot(there, ggu[...], TN)
+            .astype(BF16)
+            .reshape(TILE // per, zsize, per // zsize, 2 * HID)
+        )
+
+    loop(0, MODEL_WIDTH // TILE, gate_up_grad)
+    gwgu_z = lambda j: gwgu.at[:, j]
+    zr_start(5, gwgu_z, lwgu)
+
+    def norm_back(values, grads, gain):
+        factor = lax.rsqrt(jnp.mean(values * values, axis=-1, keepdims=True) + NORM_EPS)
+        unit = values * factor
+        scaled = grads * gain
+        inner = jnp.mean(scaled * unit, axis=-1, keepdims=True)
+        return factor * (scaled - unit * inner), jnp.sum(grads * unit, axis=0, keepdims=True)
+
+    back, terms = norm_back(resid_s[...], rs_finish(1), g_mlp)
+    hrow[:, MODEL_WIDTH : 2 * MODEL_WIDTH] = terms
+    gresid = cot_ref[...].astype(F32) + back
+    gresid_s[...] = gresid
+    gb[slot] = gresid.astype(BF16)
+    ag_start(3, gb)
+
+    def down_part(which, n):
+        return dot(hidden[half_rows(which), :], wd[:, :, n_cols(n)].reshape(HID, TILE))
+
+    ag_pass(3, gb)
+    rs_start(2, down_part)
+    ag_finish(3, gb)
+
+    def attn_grad(t):
+        gattn[tile_rows(t), :] = dot(
+            two(gb, t), wo[...].reshape(QCOLS, MODEL_WIDTH), NT
+        ).astype(BF16)
+
+    loop(0, tiles, attn_grad)
+    dk_s[...] = jnp.zeros_like(dk_s)
+    dv_s[...] = jnp.zeros_like(dv_s)
+
+    def attend_back(t):
+        at = tile_rows(t)
+        for h in range(GROUP):
+            head = slice(h * HEAD_SIZE, (h + 1) * HEAD_SIZE)
+            grads = gattn[at, head]
+            delta = jnp.sum((grads.astype(F32) * attn[at, head]).T, axis=0, keepdims=True)
+            low = probs[h, t]
+            gprobs = dot(v_s[...], grads, NT)
+            gscores = (low.astype(F32) * (gprobs - delta)).astype(BF16)
+            dv_s[...] += dot(low, grads)
+            dk_s[...] += dot(gscores, q_s[h, at, :])
+            dq_s[at, head] = dot(kt_s[...], gscores).T
+
+    loop(0, tiles, attend_back)
+
+    def out_grad(n):
+        there = gb[:, :, n_cols(n)].reshape(2 * half, TILE)
+        gwo[:, :, n_cols(n)] = (
+            dot(attn_low[...], there, TN).astype(BF16).reshape(zsize, QCOLS // zsize, TILE)
+        )
+
+    loop(0, MODEL_WIDTH // TILE, out_grad)
+    gwo_z = lambda j: gwo.at[j]
+    zr_start(6, gwo_z, lwo)
+
+    hrow[:, 2 * MODEL_WIDTH :] = jnp.zeros((1, 2 * HEAD_SIZE), F32)
+
+    def project_back(t):
+        at = tile_rows(t)
+        cosine, sine = cos_ref[at, :], sin_ref[at, :]
+
+        def one(raw, grads, gain):
+            grads = grads * scale
+            grads = grads * cosine - turned(grads) * sine
+            return norm_back(raw, grads, gain)
+
+        lo = 2 * MODEL_WIDTH
+        for h in range(GROUP):
+            head = slice(h * HEAD_SIZE, (h + 1) * HEAD_SIZE)
+            back, terms = one(qraw[at, head], dq_s[at, head], g_query)
+            gp[at, head] = back.astype(BF16)
+            hrow[:, lo : lo + HEAD_SIZE] += terms
+        back, terms = one(kraw[at, :], dk_s[at, :], g_key)
+        gp[at, QCOLS : QCOLS + HEAD_SIZE] = back.astype(BF16)
+        hrow[:, lo + HEAD_SIZE :] += terms
+        gp[at, QCOLS + HEAD_SIZE :] = dv_s[at, :].astype(BF16)
+
+    loop(0, tiles, project_back)
+
+    def qkv_grad(n):
+        per = MODEL_WIDTH // CTX
+        there = n1[:, :, n_cols(n)].reshape(2 * half, TILE)
+        gwq[pl.ds(n * (TILE // per), TILE // per)] = (
+            dot(there, gp[...], TN)
+            .astype(BF16)
+            .reshape(TILE // per, zsize, per // zsize, PCOLS)
+        )
+
+    loop(0, MODEL_WIDTH // TILE, qkv_grad)
+    gwq_z = lambda j: gwq.at[:, j]
+    zr_start(7, gwq_z, lwq)
+
+    def back_one_part(which, n):
+        per = MODEL_WIDTH // CTX
+        there = wq[pl.ds(n * (TILE // per), TILE // per)].reshape(TILE, PCOLS)
+        return dot(gp[half_rows(which), :], there, NT)
+
+    out_ref[...] = (resid_s[...] + rs_finish(2)).astype(BF16)
+    rs_start(3, back_one_part)
+
+    gd_ref[...] = zr_finish(4, gwd_z, lwd)
+    asg[...] = zr_finish(5, gwgu_z, lwgu).astype(BF16)
+    arg_at = lambda j: arg_.at[j]
+    a2a_start(2, asg, arg_at)
+    arg_[c] = asg[c]
+
+    back, terms = norm_back(x_ref[...].astype(F32), rs_finish(3), gains[:, :MODEL_WIDTH])
+    xgrad_ref[...] = (gresid_s[...] + back).astype(BF16)
+    hrow[:, :MODEL_WIDTH] = terms
+    hz[z] = hrow[...]
+    loop(1, zsize, lambda i: row_z(1, hrow, hz, i).start())
+    go_ref[...] = zr_finish(6, gwo_z, lwo)
+    row_z_wait(1, hz)
+    hpl[c] = jnp.sum(hz[...], axis=0)
+    loop(1, CTX, lambda i: row_plane(1, hpl.at[c], hpl, i).start())
+    a2a_wait(2, arg_at)
+    ggu_ref[...] = arg_[...].astype(F32)
+    row_plane_wait(1, hpl)
+    gg_ref[...] = jnp.sum(hpl[...], axis=0)
+
+    asq[...] = zr_finish(7, gwq_z, lwq).astype(BF16)
+    gq_at = lambda j: gq_ref.at[j]
+    a2a_start(3, asq, gq_at)
+    gq_ref[c] = asq[c]
+    a2a_wait(3, gq_at)
+
+    for n, buf in enumerate((n1, cot, n2, gb)):
+        ag_drain(n, buf)
+    rs_pair(3).wait_send()
+    for i in (1, 2, 3):
+        rs_chip(3, i).wait_send()
+    a2a_drain(0, wq_in, wq_at)
+    a2a_drain(1, wgu_in, wgu_at)
+    a2a_drain(2, asg, arg_at)
+    a2a_drain(3, asq, gq_at)
+    zg_drain(0, wq_z(z), wq_z)
+    zg_drain(1, wo_in, wo_z)
+    zg_drain(2, wgu_z(z), wgu_z)
+    zg_drain(3, wd_in, wd_z)
+    zr_drain(4, gwd_z, lwd)
+    zr_drain(5, gwgu_z, lwgu)
+    zr_drain(6, gwo_z, lwo)
+    zr_drain(7, gwq_z, lwq)
+    loop(1, zsize, lambda i: row_z(0, gains_in, gz, i).wait_send())
+    loop(1, CTX, lambda i: row_plane(0, gpl.at[c], gpl, i).wait_send())
+    loop(1, zsize, lambda i: row_z(1, hrow, hz, i).wait_send())
+    loop(1, CTX, lambda i: row_plane(1, hpl.at[c], hpl, i).wait_send())
+
+
+def layer_call(zsize, rows, *operands):
+    length = CTX * rows
+    tiles = length // TILE
+    width = MODEL_WIDTH
+    per = width // CTX // zsize
+    vm = pltpu.VMEM
+    dma = pltpu.SemaphoreType.DMA
+    shape = jax.ShapeDtypeStruct
+    full = vm((CTX, rows, width), BF16)
+    scratch = [
+        full,
+        full,
+        full,
+        full,
+        vm((CTX, zsize, per, PCOLS), BF16),
+        vm((zsize, QCOLS // zsize, width), BF16),
+        vm((CTX, zsize, per, 2 * HID), BF16),
+        vm((zsize, HID // zsize, width), BF16),
+        vm((length, QCOLS), F32),
+        vm((length, HEAD_SIZE), F32),
+        vm((GROUP, length, HEAD_SIZE), BF16),
+        vm((length, HEAD_SIZE), BF16),
+        vm((length, HEAD_SIZE), BF16),
+        vm((HEAD_SIZE, length), BF16),
+        vm((HEAD_SIZE, length), BF16),
+        vm((GROUP, tiles, length, TILE), BF16),
+        vm((length, QCOLS), F32),
+        vm((length, QCOLS), BF16),
+        vm((length, HID), BF16),
+        vm((length, 2 * HID), BF16),
+        vm((length, QCOLS), BF16),
+        vm((length, QCOLS), F32),
+        vm((length, HEAD_SIZE), F32),
+        vm((length, HEAD_SIZE), F32),
+        vm((length, PCOLS), BF16),
+        vm((CHIPS, rows, width), BF16),
+        vm((4, CHIPS, rows, width), BF16),
+        vm((CHIPS - 1, rows, width), BF16),
+        vm((4, CHIPS - 1, rows, width), BF16),
+        vm((CHIPS, rows, width), F32),
+        vm((4, rows, width), F32),
+        vm((rows, width), F32),
+        vm((rows, width), F32),
+        vm((CTX, zsize, per, PCOLS), BF16),
+        vm((zsize, QCOLS // zsize, width), BF16),
+        vm((CTX, zsize, per, 2 * HID), BF16),
+        vm((zsize, HID // zsize, width), BF16),
+        vm((zsize - 1, CTX, per, PCOLS), BF16),
+        vm((zsize - 1, QCOLS // zsize, width), BF16),
+        vm((zsize - 1, CTX, per, 2 * HID), BF16),
+        vm((zsize - 1, HID // zsize, width), BF16),
+        vm((CTX, per, PCOLS), BF16),
+        vm((CTX, per, 2 * HID), BF16),
+        vm((CTX, per, 2 * HID), BF16),
+        vm((zsize, 1, GAIN_WIDTH), F32),
+        vm((CTX, 1, GAIN_WIDTH), F32),
+        vm((1, GAIN_WIDTH), F32),
+        vm((zsize, 1, GAIN_WIDTH), F32),
+        vm((CTX, 1, GAIN_WIDTH), F32),
+        vm((1, GAIN_WIDTH), F32),
+        dma((4, 7)),
+        dma((4, 7)),
+        dma((4,)),
+        dma((4,)),
+        dma((4, 3)),
+        dma((4, 3)),
+        dma((4, CTX)),
+        dma((4, CTX)),
+        dma((8, zsize)),
+        dma((8, zsize)),
+        dma((2, zsize + CTX)),
+        dma((2, zsize + CTX)),
+        dma((4,)),
+    ]
+    return pl.pallas_call(
+        functools.partial(layer_kernel, zsize),
+        out_shape=(
+            shape((rows, width), BF16),
+            shape((rows, width), BF16),
+            shape((CTX, per, PCOLS), BF16),
+            shape((QCOLS // zsize, width), F32),
+            shape((CTX, per, 2 * HID), F32),
+            shape((HID // zsize, width), F32),
+            shape((1, GAIN_WIDTH), F32),
+        ),
+        in_specs=[pl.BlockSpec(memory_space=pltpu.VMEM)] * len(operands),
+        out_specs=[pl.BlockSpec(memory_space=pltpu.VMEM)] * 7,
+        scratch_shapes=scratch,
+        compiler_params=pltpu.CompilerParams(
+            collective_id=1, has_side_effects=True, vmem_limit_bytes=62 << 20
+        ),
+        name="layer",
+    )(*operands)
+
+
+def local_planes(tokens, cotangent, stretch_order, doc_lengths, master, first_moment, second_moment):
+    cycle_size = lax.axis_size("ctx")
+    zsize = lax.axis_size("fsdp")
+    shards = cycle_size * zsize
+    j = lax.axis_index("ctx") * zsize + lax.axis_index("fsdp")
+    _, rows, width = tokens.shape
+    length = rows * cycle_size
+    spans = [r // shards * w for r, w in segment_shapes()]
+    ends = [sum(spans[: i + 1]) for i in range(5)]
+    low = master.astype(BF16)
+    per = width // shards
+    kv = KEY_VALUE_HEADS * HEAD_SIZE
+    seg = low[: ends[0]].reshape(per, -1)
+    wq_in = jnp.concatenate(
+        [
+            seg[:, : 2 * kv].reshape(per, CTX, QCOLS),
+            seg[:, 2 * kv : 3 * kv].reshape(per, CTX, HEAD_SIZE),
+            seg[:, 3 * kv :].reshape(per, CTX, HEAD_SIZE),
+        ],
+        axis=2,
+    ).transpose(1, 0, 2)
+    wo_in = low[ends[0] : ends[1]].reshape(-1, width)
+    seg = low[ends[1] : ends[2]].reshape(per, 2, CTX, HID)
+    wgu_in = seg.transpose(2, 0, 1, 3).reshape(CTX, per, 2 * HID)
+    wd_in = low[ends[2] : ends[3]].reshape(-1, width)
+    own_gains = low[ends[3] :].astype(F32)
+    gains_in = lax.dynamic_update_slice(
+        jnp.zeros((1, GAIN_WIDTH), F32), own_gains[None, :], (0, j * spans[4])
+    )
+
+    def slots(v):
+        return v.reshape(CHIPS, 2, rows).transpose(1, 0, 2).reshape(length)
+
+    pos = slot_positions(stretch_order, 0, length)
+    _, relative = documents(pos, doc_lengths)
+    pos, relative = slots(pos), slots(relative[0])
+    cosine, sine = rope_tables(relative)
+    sine = jnp.concatenate([-sine[:, : HEAD_SIZE // 2], sine[:, HEAD_SIZE // 2 :]], axis=1)
+    out, xgrad, gq, go, ggu, gd, gg = layer_call(
+        zsize,
+        rows,
+        tokens[0],
+        cotangent[0],
+        wq_in,
+        wo_in,
+        wgu_in,
+        wd_in,
+        gains_in,
+        cosine,
+        sine,
+        pos[:, None],
+        pos[None, :],
+        (pos - relative)[None, :],
+    )
+    gq = gq.astype(F32)
+    gq_rows = jnp.concatenate(
+        [
+            gq[:, :, :QCOLS].transpose(1, 0, 2).reshape(per, -1),
+            gq[:, :, QCOLS : QCOLS + HEAD_SIZE].transpose(1, 0, 2).reshape(per, -1),
+            gq[:, :, QCOLS + HEAD_SIZE :].transpose(1, 0, 2).reshape(per, -1),
+        ],
+        axis=1,
+    )
+    ggu_rows = ggu.reshape(CTX, per, 2, HID).transpose(1, 2, 0, 3)
+    grad = jnp.concatenate(
+        [
+            gq_rows.reshape(-1),
+            go.reshape(-1),
+            ggu_rows.reshape(-1),
+            gd.reshape(-1),
+            lax.dynamic_slice(gg, (0, j * spans[4]), (1, spans[4])).reshape(-1),
+        ]
+    )
+    new = adam(grad, master, first_moment, second_moment, shards, length)
+    return (out[None], xgrad[None], *new)
+
+
+def adam(grad, master, first_moment, second_moment, shards, length):
+    step_rate, decay_value = rate_rows(shards, length)
     new_first = BETA_ONE * first_moment + (1.0 - BETA_ONE) * grad
     new_second = BETA_TWO * second_moment + (1.0 - BETA_TWO) * grad * grad
     normalized = (
@@ -415,7 +1226,7 @@
         / (jnp.sqrt(new_second / (1.0 - BETA_TWO**STEP)) + ADAM_EPS)
     )
     new_master = master - step_rate * (normalized + decay_value * master)
-    return (layer_out, input_grad, new_master, new_first, new_second)
+    return new_master, new_first, new_second
 
 
 def solution(mesh):
@@ -428,8 +1239,9 @@
         P(("ctx", "fsdp")),
         P(("ctx", "fsdp")),
     )
+    plane = mesh.shape["ctx"] == CTX and KEY_VALUE_HEADS == CTX
     return jax.shard_map(
-        local,
+        local_planes if plane else local,
         mesh=mesh,
         in_specs=placed,
         out_specs=(

time: 2100 us -> 232 us (0.11)
  waiting for transfers between devices: 1460 us -> 0 us
  local copies, waits for them, and re-layouts: 386 us -> 12.6 us
  Pallas kernels: 0 us -> 203 us
  other arithmetic: 128 us -> 13.3 us
  matrix products: 96.7 us -> 0 us
    unnamed x5 -> x0, waiting for transfers between devices: 1370 us -> none
    pallas_call x0 -> x1, Pallas kernels: none -> 203 us  [layer_call(): pl.pallas_call(functools.partial(layer_kernel, zsize), out_shape=(shape((...]
    reshape x13, local copies, waits for them, and re-layouts: 200 us -> 3.81 us  [the longest x1 1.01 us: local_planes(): wgu_in = seg.transpose(2, 0, 1, 3).reshape(CTX, per, 2 * HID)]
    dot_general x68 -> x0, matrix products: 96.7 us -> none  [the longest x1 10.5 us: local(): jnp.einsum('sqd,sqe->de', normed_two, grad_gate_up, preferred_element_typ...]
    ppermute x15 -> x0, waiting for transfers between devices: 87.8 us -> none  [from_behind(): return lax.ppermute(x, axis, [(i, (i + by) % peers) for i in range(peers)])]
    unnamed x198 -> x36, local copies, waits for them, and re-layouts: 76.4 us -> 6.35 us
    slice x27 -> x5, local copies, waits for them, and re-layouts: 42.7 us -> 0.08 us  [the longest x1 0.03 us: local_planes(): seg = low[ends[1]:ends[2]].reshape(per, 2, CTX, HID)]
    convert_element_type x21 -> x2, other arithmetic: 28.9 us -> 2.64 us  [the longest x1 1.64 us: local_planes(): low = master.astype(BF16)]
  transfers between devices with their start and end apart: 18 -> 0, of which waited for: 16 -> 0; matrix products, arithmetic and copies ran while one was open for 10% -> 0% of each run, Pallas kernels for 0% -> 0%
where the time goes in v1:
time: 232 us; the launch traced here: 230 us
  Pallas kernels  203 us (88%)
  other arithmetic  13.3 us (6%)
  local copies, waits for them, and re-layouts  12.6 us (5%)
    pallas_call x1, Pallas kernels, layer_call(): pl.pallas_call(functools.partial(layer_kernel, zsize), out_shape=(shape((...  203 us
    unnamed x36, local copies, waits for them, and re-layouts  6.35 us

profile of v1, /device:TPU:0, one launch (start us, length us, event | category | flops | bytes accessed | tf_op | source)
XLA Modules:
  0.0 230.4 jit_solution(1522148480052996841)
XLA Ops:
  0.6 0.8 reduce_window_sum.11
  1.5 0.7 subtract_bitcast_fusion
  2.1 0.7 select_reduce_fusion
  3.0 0.1 fusion.2
  3.1 0.6 sub.31.qstart_ref
  3.7 1.0 copy.56.kpos_ref
  4.7 1.6 convert_element_type.28
  6.4 0.2 dynamic_update_slice.3.gains_in
  6.6 0.7 reshape.260.wo_in
  7.3 0.8 reshape.263.wd_in
  8.2 0.1 reshape.256
  8.3 0.2 reshape.261
  8.5 0.3 copy.53
  8.8 1.0 reshape.262.wgu_in
  9.9 0.7 maximum_bitcast_fusion.1.wq_in
  10.6 1.9 fusion.1
  12.5 1.3 pad_maximum_fusion
  13.8 203.4 %layer.1 = (bf16[128,1024]{1,0:T(8,128)(2,1)}, bf16[128,1024]{1,0:T(8,128)(2,1)}, bf16[8,32,512]{2,1,0:T(8,128)(2,1)}, f32[64,1024]{1,0:T(8,128)}, f32[8,32,768]...) custom-call(bf16[128,1024]{1,0:T(8,128)(2,1)} %bitcast.84, bf16[128,1024]{1,0:T(8,128)(2,1)} %bitcast.85, ...), custom_call_target="tpu_custom_call" | custom-call | tf_op jit(solution)/shard_map/layer/pallas_call | solution.py:1121
  217.3 1.0 copy.68
  218.3 1.1 copy.69
  219.4 1.0 convert_element_type.32
  220.6 0.1 copy.67
  220.7 0.9 copy-done.3
  221.5 0.4 reshape.270
  222.0 0.5 copy.80
  222.7 0.9 constant_dynamic-update-slice_fusion.1
  223.9 0.2 copy-done.2
  224.1 0.6 copy-done.1
  224.7 0.6 copy-done
  225.3 3.6 %multiply_subtract_fusion = (f32[491592]{0:T(1024)}, f32[491592]{0:T(1024)}, f32[491592]{0:T(1024)}) fusion(f32[491592]{0:T(1024)S(1)} %copy-done, f32[491592]{0:T(1024)S(1)} %get-tuple-element.38, f32[491592]{0:T(1024)S(1)} %get-tuple-element.39, f32[491592]{0:T(1024)S(1)} %constant_dynamic-update-slice_fusion.1, f32[491592]{0:T(1024)S(1)} %copy-done.1, ...), kind=kLoop, calls=%fused_computation.3 | loop fusion | flops 6882288 | bytes 17697312 | tf_op jit(solution)/shard_map/sub | solution.py:1228
  229.0 0.7 copy.99
  229.7 0.7 copy.100
  (48 shorter events, 0.9 us)
Async XLA Ops:
  3.1 4.2 %copy-start.6 = (s32[4,2,128]{2,0,1:T(4,128)}, s32[4,2,128]{2,0,1:T(4,128)S(1)}, u32[]{:S(2)}) copy-start(s32[4,2,128]{2,0,1:T(4,128)S(1)} %get-tuple-element.24) | copy-start | bytes 12292
  6.6 2.2 copy-start.7
  220.4 1.1 copy-start.3
  222.6 1.6 copy-start.2
  222.6 2.1 copy-start.1
  222.7 2.6 %copy-start = (f32[491592]{0:T(1024)S(1)}, f32[491592]{0:T(1024)}, u32[]{:S(2)}) copy-start(f32[491592]{0:T(1024)} %param.11) | copy-start | bytes 5899108
  225.3 3.6 %copy-start.5 = (bf16[128,1024]{1,0:T(8,128)(2,1)S(1)}, bf16[128,1024]{1,0:T(8,128)(2,1)}, u32[]{:S(2)}) copy-start(bf16[128,1024]{1,0:T(8,128)(2,1)} %get-tuple-element.12) | copy-start | bytes 786436
  225.3 4.3 %copy-start.4 = (bf16[128,1024]{1,0:T(8,128)(2,1)S(1)}, bf16[128,1024]{1,0:T(8,128)(2,1)}, u32[]{:S(2)}) copy-start(bf16[128,1024]{1,0:T(8,128)(2,1)} %get-tuple-element.13) | copy-start | bytes 786436

commit v2 on v1

--- a/solution.py
+++ b/solution.py
@@ -1,4 +1,4 @@
-import functools
+import math
 
 import jax
 import jax.numpy as jnp
@@ -55,23 +55,6 @@
     return jnp.concatenate(
         [matrix.reshape(count_of_shards, -1) for matrix in matrices], axis=1
     ).reshape(-1)
-
-
-def rate_rows(count_of_shards, seq_length):
-    settings = [
-        (MODEL_WIDTH ** (-0.5), DECAY_RATE),
-        ((seq_length / (3.0 * QUERY_HEADS * HEAD_SIZE)) ** 0.5, DECAY_RATE),
-        (MODEL_WIDTH ** (-0.5), DECAY_RATE),
-        (FEED_WIDTH ** (-0.5), DECAY_RATE),
-        (0.2, 0.0),
-    ]
-    step_parts = []
-    decay_parts = []
-    for (row_total, column_total), (step_rate, decay_value) in zip(segment_shapes(), settings):
-        shard_span = row_total // count_of_shards * column_total
-        step_parts.append(jnp.full((shard_span,), step_rate, jnp.float32))
-        decay_parts.append(jnp.full((shard_span,), decay_value, jnp.float32))
-    return (jnp.concatenate(step_parts), jnp.concatenate(decay_parts))
 
 
 def slot_positions(stretch_order, first_row, count_of_rows):
@@ -427,26 +410,26 @@
 
 
 def layer_kernel(
-    zsize,
-    x_ref,
-    cot_ref,
+    order_ref,
+    doc_ref,
+    x_hbm,
+    cot_hbm,
+    master_hbm,
+    out_ref,
+    xgrad_ref,
+    lin_ref,
+    flat,
+    flat_gains,
+    lines,
     wq_in,
-    wo_in,
     wgu_in,
-    wd_in,
     gains_in,
     cos_ref,
     sin_ref,
     kpos_ref,
     qpos_ref,
     qstart_ref,
-    out_ref,
-    xgrad_ref,
-    gq_ref,
-    go_ref,
-    ggu_ref,
-    gd_ref,
-    gg_ref,
+    xg,
     n1,
     cot,
     n2,
@@ -468,7 +451,6 @@
     hidden,
     ggu,
     gattn,
-    dq_s,
     dk_s,
     dv_s,
     gp,
@@ -490,7 +472,12 @@
     lwd,
     asq,
     asg,
+    arq,
     arg_,
+    sum_sq,
+    sum_o,
+    sum_d,
+    sum_gu,
     gz,
     gpl,
     gains,
@@ -507,6 +494,8 @@
     a2a_r,
     zg_s,
     zg_r,
+    zr_s,
+    zr_r,
     g_s,
     g_r,
     loc,
@@ -543,6 +532,24 @@
 
         lax.fori_loop(lo, hi, step, 0)
 
+    spans = [r // (4 * CTX) * w for r, w in segment_shapes()]
+    ends = [sum(spans[: i + 1]) for i in range(5)]
+    tail = ends[3]
+    fetch = [
+        pltpu.make_async_copy(
+            master_hbm.at[pl.ds(0, ends[1])], flat.at[pl.ds(0, ends[1])], loc.at[0]
+        ),
+        pltpu.make_async_copy(master_hbm.at[pl.ds(tail, spans[4])], flat_gains, loc.at[3]),
+        pltpu.make_async_copy(
+            master_hbm.at[pl.ds(ends[1], tail - ends[1])],
+            flat.at[pl.ds(ends[1], tail - ends[1])],
+            loc.at[4],
+        ),
+        pltpu.make_async_copy(x_hbm.at[0], xg.at[slot], loc.at[1]),
+        pltpu.make_async_copy(cot_hbm.at[0], cot.at[slot], loc.at[2]),
+    ]
+    for copy in fetch:
+        copy.start()
     barrier = pltpu.get_barrier_semaphore()
 
     def greet_plane(i):
@@ -552,102 +559,208 @@
 
     def greet_z(i):
         pl.semaphore_signal(
-            barrier, inc=1, device_id=(c, (z + i) % zsize), device_id_type=MESH
+            barrier, inc=1, device_id=(c, (z + i) % 4), device_id_type=MESH
         )
 
     loop(1, CTX, greet_plane)
-    loop(1, zsize, greet_z)
-    pl.semaphore_wait(barrier, CTX - 1 + zsize - 1)
-
-    def ag_direct(n, buf, i):
-        if i == 0:
-            return rcopy(buf.at[slot], buf.at[slot], ag_s.at[n, 0], ag_r.at[n, 0], sib, z)
-        return rcopy(
-            buf.at[slot],
-            buf.at[slot],
-            ag_s.at[n, i],
-            ag_r.at[n, i],
-            chip_at(i) * 2 + core,
-            z,
-        )
-
-    def ag_landed(n, buf, i):
-        there = core * CHIPS + chip_at(i)
-        return rcopy(buf.at[there], buf.at[there], ag_s.at[n, i], ag_r.at[n, i], sib, z)
-
-    def ag_forward(n, buf, i):
-        there = core * CHIPS + chip_at(i)
-        return rcopy(buf.at[there], buf.at[there], ag_s.at[n, 3 + i], ag_r.at[n, 3 + i], sib, z)
-
-    def ag_forwarded(n, buf, i):
-        there = (1 - core) * CHIPS + chip_at(i)
-        return rcopy(buf.at[there], buf.at[there], ag_s.at[n, 3 + i], ag_r.at[n, 3 + i], sib, z)
+    loop(1, 4, greet_z)
+
+    def to_lines(i):
+        lines[pl.ds(pl.multiple_of(i * 128, 128), 128), :] = flat[
+            pl.ds(pl.multiple_of(i * 128 * 128, 128 * 128), 128 * 128)
+        ].reshape(128, 128)
+
+    def qkv_group(j, part):
+        return (GROUP * j + part) if part < GROUP else KEY_VALUE_HEADS * part + j
+
+    def feed_group(j, part):
+        per = HID // 128
+        return j * per + part if part < per else CTX * per + j * per + part - per
+
+    def line_rows(first, group, groups, count):
+        return pl.ds(first // 128 + group, count, stride=groups)
+
+    per_run = wq_in.shape[1]
+    fetch[0].wait()
+    fetch[1].wait()
+    loop(0, ends[1] // (128 * 128), to_lines)
+    for g in range(MODEL_WIDTH // 128):
+        wo[z, :, g * 128 : (g + 1) * 128] = lines[
+            line_rows(ends[0], g, MODEL_WIDTH // 128, wo.shape[1]), :
+        ].astype(BF16)
+    qkv_groups = CTX * PCOLS // 128
+    for j in range(CTX):
+        for part in range(PCOLS // 128):
+            wq_in[j, :, part * 128 : (part + 1) * 128] = lines[
+                line_rows(0, qkv_group(j, part), qkv_groups, per_run), :
+            ].astype(BF16)
+    own_gains = flat_gains[...].reshape(1, spans[4]).astype(BF16).astype(F32)
+    gains_in[...] = pltpu.roll(
+        jnp.concatenate([own_gains, jnp.zeros((1, GAIN_WIDTH - spans[4]), F32)], axis=1),
+        spans[4] * (4 * c + z),
+        1,
+    )
+
+    fetch[2].wait()
+    loop(ends[2] // (128 * 128), ends[3] // (128 * 128), to_lines)
+    for g in range(MODEL_WIDTH // 128):
+        wd[z, :, g * 128 : (g + 1) * 128] = lines[
+            line_rows(ends[2], g, MODEL_WIDTH // 128, wd.shape[1]), :
+        ].astype(BF16)
+    pl.semaphore_wait(barrier, CTX - 1 + 4 - 1)
+
+    mid = rows // 2
+    XN, YN, ACROSS = 1, 2, 3
+    whole, top, bottom = pl.ds(0, rows), pl.ds(0, mid), pl.ds(mid, mid)
+
+    def ag_piece(n, buf, k):
+        origin, part, to = (
+            (0, whole, sib),
+            (0, top, XN),
+            (0, bottom, XN),
+            (0, bottom, YN),
+            (0, top, YN),
+            (XN, top, YN),
+            (YN, bottom, XN),
+            (XN, whole, sib),
+            (YN, whole, sib),
+            (ACROSS, top, sib),
+            (ACROSS, bottom, sib),
+        )[k]
+        there = buf.at[core * CHIPS + chip_at(origin), part]
+        target = sib if to is sib else chip_at(to) * 2 + core
+        return rcopy(there, there, ag_s.at[n, k], ag_r.at[n, k], target, z)
+
+    def ag_landed(n, buf, k):
+        origin, part, own_core = (
+            (0, whole, False),
+            (XN, top, True),
+            (XN, bottom, True),
+            (YN, bottom, True),
+            (YN, top, True),
+            (ACROSS, top, True),
+            (ACROSS, bottom, True),
+            (XN, whole, False),
+            (YN, whole, False),
+            (ACROSS, top, False),
+            (ACROSS, bottom, False),
+        )[k]
+        which = core if own_core else 1 - core
+        there = buf.at[which * CHIPS + chip_at(origin), part]
+        return rcopy(there, there, ag_s.at[n, k], ag_r.at[n, k], sib, z)
 
     def ag_start(n, buf):
-        for i in (3, 1, 2, 0):
-            ag_direct(n, buf, i).start()
-
-    def ag_pass(n, buf):
-        for i in (1, 2, 3):
-            ag_landed(n, buf, i).wait_recv()
-            ag_forward(n, buf, i).start()
+        for k in (1, 3, 2, 4, 0):
+            ag_piece(n, buf, k).start()
+
+    def ag_pass_near(n, buf):
+        for landed, onward in ((1, 5), (3, 6), (2, 7), (4, 8)):
+            ag_landed(n, buf, landed).wait_recv()
+            ag_piece(n, buf, onward).start()
+
+    def ag_pass_across(n, buf):
+        for landed, onward in ((5, 9), (6, 10)):
+            ag_landed(n, buf, landed).wait_recv()
+            ag_piece(n, buf, onward).start()
+
+    def ag_finish_near(n, buf):
+        for k in (0, 7):
+            ag_landed(n, buf, k).wait_recv()
 
     def ag_finish(n, buf):
-        other = (1 - core) * CHIPS + chip
-        rcopy(buf.at[other], buf.at[other], ag_s.at[n, 0], ag_r.at[n, 0], sib, z).wait_recv()
-        for i in (1, 2, 3):
-            ag_forwarded(n, buf, i).wait_recv()
+        for k in (8, 9, 10):
+            ag_landed(n, buf, k).wait_recv()
 
     def ag_drain(n, buf):
-        for i in range(4):
-            ag_direct(n, buf, i).wait_send()
-        for i in (1, 2, 3):
-            ag_forward(n, buf, i).wait_send()
-
-    def rs_pair(r):
-        return rcopy(psnd, prcv.at[r], rs_ps.at[r], rs_pr.at[r], sib, z)
-
-    def rs_chip(r, i):
-        return rcopy(
-            csnd.at[i - 1],
-            crcv.at[r, i - 1],
-            rs_cs.at[r, i - 1],
-            rs_cr.at[r, i - 1],
-            chip_at(i) * 2 + core,
-            z,
-        )
-
-    def rs_start(r, part):
-        if r > 0:
-            rs_pair(r - 1).wait_send()
-
-        def give(n):
+        for k in range(11):
+            ag_piece(n, buf, k).wait_send()
+
+    def gathered_tiles(n, buf, body, between=None):
+        ag_pass_near(n, buf)
+        ag_finish_near(n, buf)
+        loop(0, 2, lambda k: body(2 * k + cy))
+        if between is not None:
+            between()
+        ag_pass_across(n, buf)
+        ag_finish(n, buf)
+        loop(0, 2, lambda k: body(2 * k + 1 - cy))
+
+    wide = MODEL_WIDTH // 2
+
+    def rs_pair(r, h):
+        return rcopy(psnd.at[r % 2, h], prcv.at[r % 2, h], rs_ps.at[r, h], rs_pr.at[r, h], sib, z)
+
+    def rs_chip(r, k):
+        to = chip_at((XN, XN, YN, YN, YN, XN)[k]) * 2 + core
+        return rcopy(csnd.at[r % 2, k], crcv.at[r % 2, k], rs_cs.at[r, k], rs_cr.at[r, k], to, z)
+
+    def rs_give(r, part, h):
+        def one(n):
+            out = part(1 - core, h * (wide // TILE) + n).astype(BF16)
             cols = pl.ds(pl.multiple_of(n * TILE, TILE), TILE)
-            psnd[:, :, cols] = part(1 - core, n).astype(BF16).reshape(CHIPS, rows, TILE)
-
-        def keep(n):
+            psnd[r % 2, h, :, :, cols] = out.reshape(CHIPS, rows, TILE)
+
+        loop(0, wide // TILE, one)
+        rs_pair(r, h).start()
+
+    def rs_keep(r, part, h):
+        def one(n):
+            out = part(core, h * (wide // TILE) + n)
             cols = pl.ds(pl.multiple_of(n * TILE, TILE), TILE)
-            own[:, :, cols] = part(core, n).reshape(CHIPS, rows, TILE)
-
-        loop(0, MODEL_WIDTH // TILE, give)
-        rs_pair(r).start()
-        loop(0, MODEL_WIDTH // TILE, keep)
-        if r > 0:
-            for i in (1, 2, 3):
-                rs_chip(r - 1, i).wait_send()
-        rs_pair(r).wait_recv()
-        for i in (3, 1, 2):
-            there = chip_at(i)
-            csnd[i - 1] = (own[there] + prcv[r, there].astype(F32)).astype(BF16)
-            rs_chip(r, i).start()
-        acc[r] = own[chip] + prcv[r, chip].astype(F32)
+            own[h, :, :, cols] = out.reshape(CHIPS, rows, TILE)
+
+        loop(0, wide // TILE, one)
+
+    def pair_sum(r, h, i):
+        return own[h, chip_at(i)] + prcv[r % 2, h, chip_at(i)].astype(F32)
+
+    def rs_send(r, h):
+        rs_pair(r, h).wait_recv()
+        csnd[r % 2, 2 * h] = pair_sum(r, h, ACROSS).astype(BF16)
+        rs_chip(r, 2 * h).start()
+        csnd[r % 2, 2 * h + 1] = pair_sum(r, h, (XN, YN)[h]).astype(BF16)
+        rs_chip(r, 2 * h + 1).start()
+        acc[r % 2, :, h * wide : (h + 1) * wide] = pair_sum(r, h, 0)
+
+    def rs_begin(r, part):
+        if r > 1:
+            rs_drain(r - 2)
+        for h in range(2):
+            rs_give(r, part, h)
+            rs_keep(r, part, h)
+            rs_send(r, h)
+
+    def rs_compute(r, part):
+        if r > 1:
+            rs_drain(r - 2)
+        for h in range(2):
+            rs_give(r, part, h)
+        for h in range(2):
+            rs_keep(r, part, h)
+
+    def rs_drain(r):
+        for h in range(2):
+            rs_pair(r, h).wait_send()
+        for k in range(6):
+            rs_chip(r, k).wait_send()
+
+    def rs_relay(r):
+        for h, second in ((0, YN), (1, XN)):
+            rs_chip(r, 2 * h).wait_recv()
+            csnd[r % 2, 4 + h] = (pair_sum(r, h, second) + crcv[r % 2, 2 * h].astype(F32)).astype(BF16)
+            rs_chip(r, 4 + h).start()
 
     def rs_finish(r):
-        total = acc[r]
-        for i in (1, 2, 3):
-            rs_chip(r, i).wait_recv()
-            total = total + crcv[r, i - 1].astype(F32)
-        return total
+        halves = []
+        for h in range(2):
+            rs_chip(r, 2 * h + 1).wait_recv()
+            rs_chip(r, 4 + h).wait_recv()
+            halves.append(
+                acc[r % 2, :, h * wide : (h + 1) * wide]
+                + crcv[r % 2, 2 * h + 1].astype(F32)
+                + crcv[r % 2, 4 + h].astype(F32)
+            )
+        return jnp.concatenate(halves, axis=1)
 
     def a2a(n, src, dst_of, i):
         to = (c + i) % CTX
@@ -660,110 +773,245 @@
     def a2a_start(n, src, dst_of):
         loop(1, CTX, lambda i: a2a(n, src, dst_of, i).start())
 
+    def a2a_half(n, src, dst_of, h):
+        def one(i):
+            pl.when((c + i) % CTX // (CTX // 2) == h)(a2a(n, src, dst_of, i).start)
+
+        loop(1, CTX, one)
+
     def a2a_wait(n, dst_of):
         loop(1, CTX, lambda i: a2a_landed(n, dst_of, i).wait_recv())
 
     def a2a_drain(n, src, dst_of):
         loop(1, CTX, lambda i: a2a(n, src, dst_of, i).wait_send())
 
-    def zg(n, src, dst_of, i):
-        return rcopy(src, dst_of(z), zg_s.at[n, i], zg_r.at[n, i], c, (z + i) % zsize)
-
-    def zg_landed(n, dst_of, i):
-        there = dst_of((z + zsize - i) % zsize)
-        return rcopy(there, there, zg_s.at[n, i], zg_r.at[n, i], sib, z)
-
-    def zg_start(n, src, dst_of):
-        for i in range(1, zsize):
-            zg(n, src, dst_of, i).start()
-
-    def zg_wait(n, dst_of):
-        for i in range(1, zsize):
-            zg_landed(n, dst_of, i).wait_recv()
-
-    def zg_drain(n, src, dst_of):
-        for i in range(1, zsize):
-            zg(n, src, dst_of, i).wait_send()
-
-    def zr(n, src_of, land, i):
-        to = (z + i) % zsize
-        return rcopy(src_of(to), land.at[i - 1], zg_s.at[n, i], zg_r.at[n, i], c, to)
-
-    def zr_start(n, src_of, land):
-        for i in range(1, zsize):
-            zr(n, src_of, land, i).start()
-
-    def zr_finish(n, src_of, land):
-        total = src_of(z)[...].astype(F32)
-        for i in range(1, zsize):
-            zr(n, src_of, land, i).wait_recv()
-            total = total + land[i - 1].astype(F32)
-        return total
-
-    def zr_drain(n, src_of, land):
-        for i in range(1, zsize):
-            zr(n, src_of, land, i).wait_send()
+    inner = (z == 1) | (z == 2)
+    outer = jnp.logical_not(inner)
+    far = 3 * (2 - z)
+
+    def zg(n, of, j, to, sem):
+        return rcopy(of(j), of(j), zg_s.at[n, sem], zg_r.at[n, j], c, to)
+
+    def zg_own(n, of):
+        return (
+            (z < 3, zg(n, of, z, z + 1, 4)),
+            (z > 0, zg(n, of, z, z - 1, 5)),
+        )
+
+    def zg_onward(n, of):
+        return (
+            zg(n, of, z - 1, z + 1, 0),
+            zg(n, of, z + 1, z - 1, 1),
+            zg(n, of, far, 3 * (z - 1), 2),
+        )
+
+    def zg_start(n, of):
+        for there, copy in zg_own(n, of):
+            pl.when(there)(copy.start)
+
+    def zg_near(n, of):
+        def run():
+            for k, j in ((0, z - 1), (1, z + 1)):
+                zg(n, of, j, z, 0).wait_recv()
+                zg_onward(n, of)[k].start()
+
+        pl.when(inner)(run)
+
+    def zg_far(n, of):
+        def run():
+            zg(n, of, far, z, 0).wait_recv()
+            zg_onward(n, of)[2].start()
+
+        pl.when(inner)(run)
+
+    def zg_wait(n, of):
+        def run():
+            for i in (1, 2, 3):
+                zg(n, of, (z + i) % 4, z, 0).wait_recv()
+
+        pl.when(outer)(run)
+
+    def zg_drain(n, of):
+        for there, copy in zg_own(n, of):
+            pl.when(there)(copy.wait_send)
+
+        def run():
+            for copy in zg_onward(n, of):
+                copy.wait_send()
+
+        pl.when(inner)(run)
+
+    def zr(n, of, land, d, to, spot):
+        return rcopy(of(d), land(spot), zr_s.at[n, d], zr_r.at[n, spot], c, to)
+
+    def zr_add(n, of, land, d):
+        rcopy(land(d), land(d), zr_s.at[n, d], zr_r.at[n, d], sib, z).wait_recv()
+        mine = of(d)
+        mine[...] = (mine[...].astype(F32) + land(d)[...].astype(F32)).astype(BF16)
+
+    ENDS = ((0, 3, 1, 3), (3, 0, 2, 0), (0, 2, 1, 2), (3, 1, 2, 1), (0, 1, 1, 1), (3, 2, 2, 4))
+    FIRST = ((1, 3, 2, 3), (2, 0, 1, 0))
+    SECOND = ((1, 2, 2, 2), (2, 1, 1, 4), (1, 0, 0, 4), (2, 3, 3, 3))
+
+    def zr_start(n, of, land):
+        for device, d, to, spot in ENDS:
+            pl.when(z == device)(zr(n, of, land, d, to, spot).start)
+
+    def zr_pass(n, of, land, steps):
+        for device, d, to, spot in steps:
+
+            def run(d=d, to=to, spot=spot):
+                zr_add(n, of, land, d)
+                zr(n, of, land, d, to, spot).start()
+
+            pl.when(z == device)(run)
+
+    def zr_first(n, of, land):
+        zr_pass(n, of, land, FIRST)
+
+    def zr_second(n, of, land):
+        zr_pass(n, of, land, SECOND)
+
+    def zr_finish(n, of, land, total):
+        total[...] = of(z)[...].astype(F32)
+
+        def add(spot):
+            rcopy(land(spot), land(spot), zr_s.at[n, 0], zr_r.at[n, spot], sib, z).wait_recv()
+            total[...] += land(spot)[...].astype(F32)
+
+        pl.when(z > 0)(lambda: add(z))
+        pl.when(z < 3)(lambda: add(4))
+
+    def zr_drain(n, of, land):
+        for device, d, to, spot in ENDS + FIRST + SECOND:
+            pl.when(z == device)(zr(n, of, land, d, to, spot).wait_send)
 
     def row_z(n, src, land, i):
-        return rcopy(src, land.at[z], g_s.at[n, i], g_r.at[n, i], c, (z + i) % zsize)
+        return rcopy(src, land.at[z], g_s.at[n, i], g_r.at[n, i], c, (z + i) % 4)
 
     def row_plane(n, src, land, i):
         return rcopy(
-            src, land.at[c], g_s.at[n, zsize + i], g_r.at[n, zsize + i], (c + i) % CTX, z
+            src, land.at[c], g_s.at[n, 4 + i], g_r.at[n, 4 + i], (c + i) % CTX, z
         )
 
     def row_z_wait(n, land):
         def one(i):
-            there = land.at[(z + zsize - i) % zsize]
+            there = land.at[(z + 4 - i) % 4]
             rcopy(there, there, g_s.at[n, i], g_r.at[n, i], sib, z).wait_recv()
 
-        loop(1, zsize, one)
+        loop(1, 4, one)
 
     def row_plane_wait(n, land):
         def one(i):
             there = land.at[(c + CTX - i) % CTX]
-            rcopy(there, there, g_s.at[n, zsize + i], g_r.at[n, zsize + i], sib, z).wait_recv()
+            rcopy(there, there, g_s.at[n, 4 + i], g_r.at[n, 4 + i], sib, z).wait_recv()
 
         loop(1, CTX, one)
+
+    def halves(ref):
+        half_of = lambda h: lambda j: ref.at[pl.ds(h * (CTX // 2), CTX // 2), j]
+        return half_of(0), half_of(1)
+
+    def land_halves(ref):
+        half_of = lambda h: lambda j: ref.at[j, pl.ds(h * (CTX // 2), CTX // 2)]
+        return half_of(0), half_of(1)
 
     wq_at = lambda j: wq.at[j, z]
     wgu_at = lambda j: wgu.at[j, z]
-    wq_z = lambda j: wq.at[:, j]
-    wgu_z = lambda j: wgu.at[:, j]
-    wo_z = lambda j: wo.at[j]
-    wd_z = lambda j: wd.at[j]
-
+    g_q = (0, lambda j: wq.at[:, j])
+    g_o = (1, lambda j: wo.at[j])
+    g_gu1, g_gu2 = ((2 + h, of) for h, of in enumerate(halves(wgu)))
+    g_d = (4, lambda j: wd.at[j])
+    r_d = (0, lambda j: gwd.at[j], lambda j: lwd.at[j])
+    r_gu1, r_gu2 = (
+        (1 + h, *both) for h, both in enumerate(zip(halves(gwgu), land_halves(lwgu)))
+    )
+    r_o = (3, lambda j: gwo.at[j], lambda j: lwo.at[j])
+    r_q1, r_q2 = (
+        (4 + h, *both) for h, both in enumerate(zip(halves(gwq), land_halves(lwq)))
+    )
+
+    lines[pl.ds(tail // 128, 8), :] = jnp.zeros((8, 128), F32)
     gz[z] = gains_in[...]
-    loop(1, zsize, lambda i: row_z(0, gains_in, gz, i).start())
+    loop(1, 4, lambda i: row_z(0, gains_in, gz, i).start())
     a2a_start(0, wq_in, wq_at)
+    zg_start(*g_o)
+    fetch[3].wait()
+    ag_start(0, xg)
+
+    def share(frm):
+        there = wq.at[frm, z]
+        for k, to, here in ((4, z + 1, z < 3), (5, z - 1, z > 0)):
+            pl.when(here)(rcopy(there, there, zg_s.at[0, k], zg_r.at[0, z], c, to).start)
+
+    def share_landed(i):
+        a2a_landed(0, wq_at, i).wait_recv()
+        share((c + CTX - i) % CTX)
+
     wq[c, z] = wq_in[c]
-    wo[z] = wo_in[...]
-    wd[z] = wd_in[...]
-    wgu[c, z] = wgu_in[c]
-    cot[slot] = cot_ref[...]
-
+    share(c)
+    loop(ends[1] // (128 * 128), ends[2] // (128 * 128), to_lines)
+    feed_groups = 2 * FEED_WIDTH // 128
+    for j in range(CTX):
+        for part in range(2 * HID // 128):
+            wgu_in[j, :, part * 128 : (part + 1) * 128] = lines[
+                line_rows(ends[1], feed_group(j, part), feed_groups, per_run), :
+            ].astype(BF16)
+    loop(1, CTX, share_landed)
     row_z_wait(0, gz)
     gpl[c] = jnp.sum(gz[...], axis=0)
     loop(1, CTX, lambda i: row_plane(0, gpl.at[c], gpl, i).start())
-
-    a2a_wait(0, wq_at)
-    zg_start(0, wq_z(z), wq_z)
-    zg_start(1, wo_in, wo_z)
+    wgu[c, z] = wgu_in[c]
+    zg_near(*g_o)
+    fetch[4].wait()
+    doc_ends = [doc_ref[0, 0]]
+    for j in range(1, doc_ref.shape[1] - 1):
+        doc_ends.append(doc_ends[-1] + doc_ref[0, j])
+
+    def doc_start(pos):
+        start = jnp.zeros_like(pos)
+        for end in doc_ends:
+            start = jnp.where(pos >= end, end, start)
+        return start
+
+    def tables(s):
+        first = 2 * (2 * (s % CHIPS) + s // CHIPS)
+        lead = order_ref[first] * STRETCH
+        trail = order_ref[first + 1] * STRETCH - STRETCH
+        at = pl.ds(pl.multiple_of(s * rows, rows), rows)
+
+        def positions(shape, axis):
+            index = lax.broadcasted_iota(jnp.int32, shape, axis)
+            return index + jnp.where(index < STRETCH, lead, trail)
+
+        across = positions((1, rows), 1)
+        qpos_ref[:, at] = across
+        qstart_ref[:, at] = doc_start(across)
+        down = positions((rows, HEAD_SIZE), 0)
+        kpos_ref[at, :] = down
+        lane = lax.broadcasted_iota(jnp.int32, (1, HEAD_SIZE), 1)
+        upper = lane >= HEAD_SIZE // 2
+        index = jnp.where(upper, lane - HEAD_SIZE // 2, lane).astype(F32)
+        frequency = jnp.exp(index * (-2.0 / HEAD_SIZE * math.log(ROPE_BASE)))
+        angles = (down - doc_start(down)).astype(F32) * frequency
+        sine = jnp.sin(angles)
+        cos_ref[at, :] = jnp.cos(angles)
+        sin_ref[at, :] = jnp.where(upper, sine, -sine)
+
+    loop(0, CTX, tables)
+    ag_pass_near(0, xg)
+    zg_near(*g_q)
+    zg_far(*g_o)
+    ag_finish_near(0, xg)
+    ag_pass_across(0, xg)
+    ag_finish(0, xg)
     a2a_start(1, wgu_in, wgu_at)
-
+    ag_start(1, cot)
+    zg_far(*g_q)
     row_plane_wait(0, gpl)
     gains[...] = jnp.sum(gpl[...], axis=0)
     g_attn = gains[:, :MODEL_WIDTH]
-    x_own = x_ref[...].astype(F32)
-    s_one = lax.rsqrt(jnp.mean(x_own * x_own, axis=-1, keepdims=True) + NORM_EPS)
-    n1[slot] = (x_own * s_one * g_attn).astype(BF16)
-    ag_start(0, n1)
-    a2a_wait(1, wgu_at)
-    ag_pass(0, n1)
-    ag_finish(0, n1)
-    ag_start(1, cot)
-    zg_wait(0, wq_z)
-    zg_start(2, wgu_z(z), wgu_z)
+    zg_wait(*g_q)
 
     g_query = gains[:, 2 * MODEL_WIDTH : 2 * MODEL_WIDTH + HEAD_SIZE]
     g_key = gains[:, 2 * MODEL_WIDTH + HEAD_SIZE :]
@@ -786,7 +1034,13 @@
             y = raw * scale * gain
             return y * cosine + turned(y) * sine
 
-        out = dot(two(n1, t), wq[...].reshape(MODEL_WIDTH, PCOLS))
+        x_tile = two(xg, t).astype(F32)
+        x_scale = lax.rsqrt(jnp.mean(x_tile * x_tile, axis=-1, keepdims=True) + NORM_EPS)
+        normed_one = (x_tile * x_scale * g_attn).astype(BF16)
+        n1[pl.ds(t * (TILE // rows), TILE // rows)] = normed_one.reshape(
+            TILE // rows, rows, MODEL_WIDTH
+        )
+        out = dot(normed_one, wq[...].reshape(MODEL_WIDTH, PCOLS))
         for h in range(GROUP):
             raw = out[:, h * HEAD_SIZE : (h + 1) * HEAD_SIZE]
             qraw[at, h * HEAD_SIZE : (h + 1) * HEAD_SIZE] = raw
@@ -801,13 +1055,15 @@
         vt_s[:, at] = values.T.astype(BF16)
 
     loop(0, tiles, project)
-    ag_pass(1, cot)
-
+    a2a_wait(1, wgu_at)
+    zg_start(*g_gu1)
+    zg_start(*g_gu2)
+    zg_start(*g_d)
     scale = HEAD_SIZE ** (-0.5)
 
     def attend(t):
         at = tile_rows(t)
-        kpos = kpos_ref[...]
+        kpos = jnp.concatenate([kpos_ref[...]] * (TILE // HEAD_SIZE), axis=1)
         kept = (kpos <= qpos_ref[:, at]) & (kpos >= qstart_ref[:, at])
         for h in range(GROUP):
             scores = jnp.where(kept, dot(k_s[...], q_s[h, at, :], NT) * scale, MASKED)
@@ -819,10 +1075,12 @@
             attn[at, h * HEAD_SIZE : (h + 1) * HEAD_SIZE] = mixed
             attn_low[at, h * HEAD_SIZE : (h + 1) * HEAD_SIZE] = mixed.astype(BF16)
 
-    loop(0, tiles, attend)
-
-    zg_wait(1, wo_z)
-    zg_start(3, wd_in, wd_z)
+    loop(0, tiles // 2, attend)
+    ag_pass_near(1, cot)
+    loop(tiles // 2, tiles, attend)
+
+    zg_wait(*g_o)
+    ag_pass_across(1, cot)
 
     def n_cols(n):
         return pl.ds(pl.multiple_of(n * TILE, TILE), TILE)
@@ -838,49 +1096,65 @@
             attn_low[half_rows(which), :], wo[:, :, n_cols(n)].reshape(QCOLS, TILE)
         )
 
-    rs_start(0, out_part)
-    ag_finish(1, cot)
-    resid = x_ref[...].astype(F32) + rs_finish(0)
+    rs_begin(0, out_part)
+    zg_near(*g_gu1)
+    rs_relay(0)
+    zg_near(*g_gu2)
+    resid = xg[slot].astype(F32) + rs_finish(0)
     resid_s[...] = resid
     g_mlp = gains[:, MODEL_WIDTH : 2 * MODEL_WIDTH]
     s_two = lax.rsqrt(jnp.mean(resid * resid, axis=-1, keepdims=True) + NORM_EPS)
     n2[slot] = (resid * s_two * g_mlp).astype(BF16)
     ag_start(2, n2)
-    ag_pass(2, n2)
+    ag_finish_near(1, cot)
+    ag_finish(1, cot)
+    zg_far(*g_gu1)
+    zg_near(*g_d)
+    ag_pass_near(2, n2)
+    ag_finish_near(2, n2)
+    zg_far(*g_gu2)
+    ag_pass_across(2, n2)
     ag_finish(2, n2)
-
-    zg_wait(2, wgu_z)
-    zg_wait(3, wd_z)
+    zg_far(*g_d)
+    zg_wait(*g_gu1)
+    zg_wait(*g_gu2)
 
     def feed(t):
         at = tile_rows(t)
         both = dot(two(n2, t), wgu[...].reshape(MODEL_WIDTH, 2 * HID))
-        ghid = dot(two(cot, t), wd[...].reshape(HID, MODEL_WIDTH), NT)
         gate, up = both[:, :HID], both[:, HID:]
         sig = 1.0 / (1.0 + jnp.exp(-gate))
         silu = gate * sig
         hidden[at, :] = (silu * up).astype(BF16)
-        ggu[at, :HID] = (ghid * up * sig * (1.0 + gate * (1.0 - sig))).astype(BF16)
-        ggu[at, HID:] = (ghid * silu).astype(BF16)
+        ggu[at, :HID] = (up * sig * (1.0 + gate * (1.0 - sig))).astype(BF16)
+        ggu[at, HID:] = silu.astype(BF16)
 
     loop(0, tiles, feed)
+
+    def down_grad(n):
+        there = cot[:, :, n_cols(n)].reshape(2 * half, TILE)
+        gwd[:, :, n_cols(n)] = (
+            dot(hidden[...], there, TN).astype(BF16).reshape(4, HID // 4, TILE)
+        )
+
+    loop(0, MODEL_WIDTH // TILE, down_grad)
+    zr_start(*r_d)
+    zg_wait(*g_d)
+
+    def feed_back(t):
+        at = tile_rows(t)
+        ghid = dot(two(cot, t), wd[...].reshape(HID, MODEL_WIDTH), NT)
+        ggu[at, :HID] = (ghid * ggu[at, :HID].astype(F32)).astype(BF16)
+        ggu[at, HID:] = (ghid * ggu[at, HID:].astype(F32)).astype(BF16)
+
+    loop(0, tiles, feed_back)
 
     def back_two_part(which, n):
         per = MODEL_WIDTH // CTX
         there = wgu[pl.ds(n * (TILE // per), TILE // per)].reshape(TILE, 2 * HID)
         return dot(ggu[half_rows(which), :], there, NT)
 
-    rs_start(1, back_two_part)
-
-    def down_grad(n):
-        there = cot[:, :, n_cols(n)].reshape(2 * half, TILE)
-        gwd[:, :, n_cols(n)] = (
-            dot(hidden[...], there, TN).astype(BF16).reshape(zsize, HID // zsize, TILE)
-        )
-
-    loop(0, MODEL_WIDTH // TILE, down_grad)
-    gwd_z = lambda j: gwd.at[j]
-    zr_start(4, gwd_z, lwd)
+    rs_begin(1, back_two_part)
 
     def gate_up_grad(n):
         per = MODEL_WIDTH // CTX
@@ -888,12 +1162,16 @@
         gwgu[pl.ds(n * (TILE // per), TILE // per)] = (
             dot(there, ggu[...], TN)
             .astype(BF16)
-            .reshape(TILE // per, zsize, per // zsize, 2 * HID)
-        )
-
-    loop(0, MODEL_WIDTH // TILE, gate_up_grad)
-    gwgu_z = lambda j: gwgu.at[:, j]
-    zr_start(5, gwgu_z, lwgu)
+            .reshape(TILE // per, 4, per // 4, 2 * HID)
+        )
+
+    loop(0, MODEL_WIDTH // TILE // 2, gate_up_grad)
+    zr_start(*r_gu1)
+    loop(MODEL_WIDTH // TILE // 2, MODEL_WIDTH // TILE, gate_up_grad)
+    zr_start(*r_gu2)
+    zr_first(*r_d)
+    rs_relay(1)
+
 
     def norm_back(values, grads, gain):
         factor = lax.rsqrt(jnp.mean(values * values, axis=-1, keepdims=True) + NORM_EPS)
@@ -904,24 +1182,25 @@
 
     back, terms = norm_back(resid_s[...], rs_finish(1), g_mlp)
     hrow[:, MODEL_WIDTH : 2 * MODEL_WIDTH] = terms
-    gresid = cot_ref[...].astype(F32) + back
+    gresid = cot[slot].astype(F32) + back
     gresid_s[...] = gresid
     gb[slot] = gresid.astype(BF16)
-    ag_start(3, gb)
-
     def down_part(which, n):
         return dot(hidden[half_rows(which), :], wd[:, :, n_cols(n)].reshape(HID, TILE))
 
-    ag_pass(3, gb)
-    rs_start(2, down_part)
-    ag_finish(3, gb)
+    ag_start(3, gb)
+    rs_compute(2, down_part)
+    zr_second(*r_d)
 
     def attn_grad(t):
         gattn[tile_rows(t), :] = dot(
             two(gb, t), wo[...].reshape(QCOLS, MODEL_WIDTH), NT
         ).astype(BF16)
 
-    loop(0, tiles, attn_grad)
+    gathered_tiles(3, gb, attn_grad, lambda: zr_first(*r_gu1))
+    rs_send(2, 0)
+    rs_send(2, 1)
+
     dk_s[...] = jnp.zeros_like(dk_s)
     dv_s[...] = jnp.zeros_like(dv_s)
 
@@ -936,19 +1215,13 @@
             gscores = (low.astype(F32) * (gprobs - delta)).astype(BF16)
             dv_s[...] += dot(low, grads)
             dk_s[...] += dot(gscores, q_s[h, at, :])
-            dq_s[at, head] = dot(kt_s[...], gscores).T
-
-    loop(0, tiles, attend_back)
-
-    def out_grad(n):
-        there = gb[:, :, n_cols(n)].reshape(2 * half, TILE)
-        gwo[:, :, n_cols(n)] = (
-            dot(attn_low[...], there, TN).astype(BF16).reshape(zsize, QCOLS // zsize, TILE)
-        )
-
-    loop(0, MODEL_WIDTH // TILE, out_grad)
-    gwo_z = lambda j: gwo.at[j]
-    zr_start(6, gwo_z, lwo)
+            attn[at, head] = dot(kt_s[...], gscores).T
+
+    loop(0, tiles // 2, attend_back)
+    zr_second(*r_gu1)
+    loop(tiles // 2, tiles, attend_back)
+    rs_relay(2)
+    zr_first(*r_gu2)
 
     hrow[:, 2 * MODEL_WIDTH :] = jnp.zeros((1, 2 * HEAD_SIZE), F32)
 
@@ -964,7 +1237,7 @@
         lo = 2 * MODEL_WIDTH
         for h in range(GROUP):
             head = slice(h * HEAD_SIZE, (h + 1) * HEAD_SIZE)
-            back, terms = one(qraw[at, head], dq_s[at, head], g_query)
+            back, terms = one(qraw[at, head], attn[at, head], g_query)
             gp[at, head] = back.astype(BF16)
             hrow[:, lo : lo + HEAD_SIZE] += terms
         back, terms = one(kraw[at, :], dk_s[at, :], g_key)
@@ -980,88 +1253,153 @@
         gwq[pl.ds(n * (TILE // per), TILE // per)] = (
             dot(there, gp[...], TN)
             .astype(BF16)
-            .reshape(TILE // per, zsize, per // zsize, PCOLS)
-        )
-
-    loop(0, MODEL_WIDTH // TILE, qkv_grad)
-    gwq_z = lambda j: gwq.at[:, j]
-    zr_start(7, gwq_z, lwq)
+            .reshape(TILE // per, 4, per // 4, PCOLS)
+        )
+
+    loop(0, MODEL_WIDTH // TILE // 2, qkv_grad)
+    zr_start(*r_q1)
+    loop(MODEL_WIDTH // TILE // 2, MODEL_WIDTH // TILE, qkv_grad)
+    zr_start(*r_q2)
+    zr_second(*r_gu2)
 
     def back_one_part(which, n):
         per = MODEL_WIDTH // CTX
         there = wq[pl.ds(n * (TILE // per), TILE // per)].reshape(TILE, PCOLS)
         return dot(gp[half_rows(which), :], there, NT)
 
-    out_ref[...] = (resid_s[...] + rs_finish(2)).astype(BF16)
-    rs_start(3, back_one_part)
-
-    gd_ref[...] = zr_finish(4, gwd_z, lwd)
-    asg[...] = zr_finish(5, gwgu_z, lwgu).astype(BF16)
+    rs_begin(3, back_one_part)
+    zr_first(*r_q1)
+
+    def out_grad(n):
+        there = gb[:, :, n_cols(n)].reshape(2 * half, TILE)
+        gwo[:, :, n_cols(n)] = (
+            dot(attn_low[...], there, TN).astype(BF16).reshape(4, QCOLS // 4, TILE)
+        )
+
+    loop(0, MODEL_WIDTH // TILE, out_grad)
+    zr_start(*r_o)
+    zr_first(*r_q2)
+    rs_relay(3)
+    zr_second(*r_q1)
+    zr_finish(*r_d, sum_d)
+    for g in range(MODEL_WIDTH // 128):
+        lines[line_rows(ends[2], g, MODEL_WIDTH // 128, sum_d.shape[0]), :] = sum_d[
+            :, g * 128 : (g + 1) * 128
+        ]
+    zr_finish(*r_gu1, sum_gu.at[pl.ds(0, CTX // 2)])
+    zr_finish(*r_gu2, sum_gu.at[pl.ds(CTX // 2, CTX // 2)])
+    asg[...] = sum_gu[...].astype(BF16)
     arg_at = lambda j: arg_.at[j]
     a2a_start(2, asg, arg_at)
     arg_[c] = asg[c]
-
-    back, terms = norm_back(x_ref[...].astype(F32), rs_finish(3), gains[:, :MODEL_WIDTH])
-    xgrad_ref[...] = (gresid_s[...] + back).astype(BF16)
+    zr_second(*r_q2)
+    back, terms = norm_back(xg[slot].astype(F32), rs_finish(3), gains[:, :MODEL_WIDTH])
+    xgrad_ref[0] = (gresid_s[...] + back).astype(BF16)
     hrow[:, :MODEL_WIDTH] = terms
     hz[z] = hrow[...]
-    loop(1, zsize, lambda i: row_z(1, hrow, hz, i).start())
-    go_ref[...] = zr_finish(6, gwo_z, lwo)
+    loop(1, 4, lambda i: row_z(1, hrow, hz, i).start())
+    zr_first(*r_o)
+    out_ref[0] = (resid_s[...] + rs_finish(2)).astype(BF16)
+    arq_at = lambda j: arq.at[j]
+    first_half, second_half = pl.ds(0, CTX // 2), pl.ds(CTX // 2, CTX // 2)
+    zr_finish(*r_q1, sum_sq.at[first_half])
+    asq[first_half] = sum_sq[first_half].astype(BF16)
+    a2a_half(3, asq, arq_at, 0)
+    zr_finish(*r_q2, sum_sq.at[second_half])
+    asq[second_half] = sum_sq[second_half].astype(BF16)
+    a2a_half(3, asq, arq_at, 1)
+    arq[c] = asq[c]
+    zr_second(*r_o)
     row_z_wait(1, hz)
     hpl[c] = jnp.sum(hz[...], axis=0)
     loop(1, CTX, lambda i: row_plane(1, hpl.at[c], hpl, i).start())
     a2a_wait(2, arg_at)
-    ggu_ref[...] = arg_[...].astype(F32)
+    for j in range(CTX):
+        for part in range(2 * HID // 128):
+            lines[line_rows(ends[1], feed_group(j, part), feed_groups, per_run), :] = arg_[
+                j, :, part * 128 : (part + 1) * 128
+            ].astype(F32)
+    a2a_wait(3, arq_at)
+    for j in range(CTX):
+        for part in range(PCOLS // 128):
+            lines[line_rows(0, qkv_group(j, part), qkv_groups, per_run), :] = arq[
+                j, :, part * 128 : (part + 1) * 128
+            ].astype(F32)
+    split = ends[0] // 128, ends[1] // 128
+    stores = [
+        pltpu.make_async_copy(
+            lines.at[pl.ds(first, last - first)], lin_ref.at[pl.ds(first, last - first)], loc.at[k]
+        )
+        for k, (first, last) in enumerate(
+            ((0, split[0]), (split[1], tail // 128), split, (tail // 128, tail // 128 + 8))
+        )
+    ]
+    stores[0].start()
+    stores[1].start()
+    zr_finish(*r_o, sum_o)
+    for g in range(MODEL_WIDTH // 128):
+        lines[line_rows(ends[0], g, MODEL_WIDTH // 128, sum_o.shape[0]), :] = sum_o[
+            :, g * 128 : (g + 1) * 128
+        ]
+    stores[2].start()
     row_plane_wait(1, hpl)
-    gg_ref[...] = jnp.sum(hpl[...], axis=0)
-
-    asq[...] = zr_finish(7, gwq_z, lwq).astype(BF16)
-    gq_at = lambda j: gq_ref.at[j]
-    a2a_start(3, asq, gq_at)
-    gq_ref[c] = asq[c]
-    a2a_wait(3, gq_at)
-
-    for n, buf in enumerate((n1, cot, n2, gb)):
+    total = jnp.sum(hpl[...], axis=0)
+    lines[pl.ds(tail // 128, 1), :] = pltpu.roll(
+        total, GAIN_WIDTH - spans[4] * (4 * c + z), 1
+    )[:, :128]
+    stores[3].start()
+
+    for n, buf in enumerate((xg, cot, n2, gb)):
         ag_drain(n, buf)
-    rs_pair(3).wait_send()
-    for i in (1, 2, 3):
-        rs_chip(3, i).wait_send()
+    rs_drain(2)
+    rs_drain(3)
     a2a_drain(0, wq_in, wq_at)
     a2a_drain(1, wgu_in, wgu_at)
     a2a_drain(2, asg, arg_at)
-    a2a_drain(3, asq, gq_at)
-    zg_drain(0, wq_z(z), wq_z)
-    zg_drain(1, wo_in, wo_z)
-    zg_drain(2, wgu_z(z), wgu_z)
-    zg_drain(3, wd_in, wd_z)
-    zr_drain(4, gwd_z, lwd)
-    zr_drain(5, gwgu_z, lwgu)
-    zr_drain(6, gwo_z, lwo)
-    zr_drain(7, gwq_z, lwq)
-    loop(1, zsize, lambda i: row_z(0, gains_in, gz, i).wait_send())
+    a2a_drain(3, asq, arq_at)
+    for item in (g_q, g_o, g_gu1, g_gu2, g_d):
+        zg_drain(*item)
+    for item in (r_d, r_gu1, r_gu2, r_o, r_q1, r_q2):
+        zr_drain(*item)
+    loop(1, 4, lambda i: row_z(0, gains_in, gz, i).wait_send())
     loop(1, CTX, lambda i: row_plane(0, gpl.at[c], gpl, i).wait_send())
-    loop(1, zsize, lambda i: row_z(1, hrow, hz, i).wait_send())
+    loop(1, 4, lambda i: row_z(1, hrow, hz, i).wait_send())
     loop(1, CTX, lambda i: row_plane(1, hpl.at[c], hpl, i).wait_send())
-
-
-def layer_call(zsize, rows, *operands):
+    for copy in stores:
+        copy.wait()
+
+
+def layer_call(tokens, cotangent, stretch_order, doc_lengths, master):
+    _, rows, width = tokens.shape
     length = CTX * rows
     tiles = length // TILE
-    width = MODEL_WIDTH
-    per = width // CTX // zsize
+    per = width // CTX // 4
+    entries = master.shape[0] // 1024 * 1024
     vm = pltpu.VMEM
     dma = pltpu.SemaphoreType.DMA
     shape = jax.ShapeDtypeStruct
     full = vm((CTX, rows, width), BF16)
     scratch = [
+        vm((entries,), F32),
+        vm((master.shape[0] - entries,), F32),
+        vm((entries // 128 + 8, 128), F32),
+        vm((CTX, per, PCOLS), BF16),
+        vm((CTX, per, 2 * HID), BF16),
+        vm((1, GAIN_WIDTH), F32),
+        vm((length, HEAD_SIZE), F32),
+        vm((length, HEAD_SIZE), F32),
+        vm((length, HEAD_SIZE), jnp.int32),
+        vm((1, length), jnp.int32),
+        vm((1, length), jnp.int32),
         full,
         full,
         full,
         full,
-        vm((CTX, zsize, per, PCOLS), BF16),
-        vm((zsize, QCOLS // zsize, width), BF16),
-        vm((CTX, zsize, per, 2 * HID), BF16),
-        vm((zsize, HID // zsize, width), BF16),
+        full,
+        vm((CTX, 4, per, PCOLS), BF16),
+        vm((4, QCOLS // 4, width), BF16),
+        vm((CTX, 4, per, 2 * HID), BF16),
+        vm((4, HID // 4, width), BF16),
         vm((length, QCOLS), F32),
         vm((length, HEAD_SIZE), F32),
         vm((GROUP, length, HEAD_SIZE), BF16),
@@ -1075,149 +1413,112 @@
         vm((length, HID), BF16),
         vm((length, 2 * HID), BF16),
         vm((length, QCOLS), BF16),
-        vm((length, QCOLS), F32),
         vm((length, HEAD_SIZE), F32),
         vm((length, HEAD_SIZE), F32),
         vm((length, PCOLS), BF16),
-        vm((CHIPS, rows, width), BF16),
-        vm((4, CHIPS, rows, width), BF16),
-        vm((CHIPS - 1, rows, width), BF16),
-        vm((4, CHIPS - 1, rows, width), BF16),
-        vm((CHIPS, rows, width), F32),
-        vm((4, rows, width), F32),
+        vm((2, 2, CHIPS, rows, width // 2), BF16),
+        vm((2, 2, CHIPS, rows, width // 2), BF16),
+        vm((2, 6, rows, width // 2), BF16),
+        vm((2, 6, rows, width // 2), BF16),
+        vm((2, CHIPS, rows, width // 2), F32),
+        vm((2, rows, width), F32),
         vm((rows, width), F32),
         vm((rows, width), F32),
-        vm((CTX, zsize, per, PCOLS), BF16),
-        vm((zsize, QCOLS // zsize, width), BF16),
-        vm((CTX, zsize, per, 2 * HID), BF16),
-        vm((zsize, HID // zsize, width), BF16),
-        vm((zsize - 1, CTX, per, PCOLS), BF16),
-        vm((zsize - 1, QCOLS // zsize, width), BF16),
-        vm((zsize - 1, CTX, per, 2 * HID), BF16),
-        vm((zsize - 1, HID // zsize, width), BF16),
+        vm((CTX, 4, per, PCOLS), BF16),
+        vm((4, QCOLS // 4, width), BF16),
+        vm((CTX, 4, per, 2 * HID), BF16),
+        vm((4, HID // 4, width), BF16),
+        vm((5, CTX, per, PCOLS), BF16),
+        vm((5, QCOLS // 4, width), BF16),
+        vm((5, CTX, per, 2 * HID), BF16),
+        vm((5, HID // 4, width), BF16),
         vm((CTX, per, PCOLS), BF16),
         vm((CTX, per, 2 * HID), BF16),
+        vm((CTX, per, PCOLS), BF16),
         vm((CTX, per, 2 * HID), BF16),
-        vm((zsize, 1, GAIN_WIDTH), F32),
+        vm((CTX, per, PCOLS), F32),
+        vm((QCOLS // 4, width), F32),
+        vm((HID // 4, width), F32),
+        vm((CTX, per, 2 * HID), F32),
+        vm((4, 1, GAIN_WIDTH), F32),
         vm((CTX, 1, GAIN_WIDTH), F32),
         vm((1, GAIN_WIDTH), F32),
-        vm((zsize, 1, GAIN_WIDTH), F32),
+        vm((4, 1, GAIN_WIDTH), F32),
         vm((CTX, 1, GAIN_WIDTH), F32),
         vm((1, GAIN_WIDTH), F32),
-        dma((4, 7)),
-        dma((4, 7)),
-        dma((4,)),
-        dma((4,)),
-        dma((4, 3)),
-        dma((4, 3)),
+        dma((4, 11)),
+        dma((4, 11)),
+        dma((4, 2)),
+        dma((4, 2)),
+        dma((4, 6)),
+        dma((4, 6)),
         dma((4, CTX)),
         dma((4, CTX)),
-        dma((8, zsize)),
-        dma((8, zsize)),
-        dma((2, zsize + CTX)),
-        dma((2, zsize + CTX)),
-        dma((4,)),
+        dma((5, 6)),
+        dma((5, 4)),
+        dma((6, 4)),
+        dma((6, 5)),
+        dma((2, 4 + CTX)),
+        dma((2, 4 + CTX)),
+        dma((5,)),
     ]
+    smem = pl.BlockSpec(memory_space=pltpu.SMEM)
+    vmem = pl.BlockSpec(memory_space=pltpu.VMEM)
+    anywhere = pl.BlockSpec(memory_space=pl.ANY)
     return pl.pallas_call(
-        functools.partial(layer_kernel, zsize),
+        layer_kernel,
         out_shape=(
-            shape((rows, width), BF16),
-            shape((rows, width), BF16),
-            shape((CTX, per, PCOLS), BF16),
-            shape((QCOLS // zsize, width), F32),
-            shape((CTX, per, 2 * HID), F32),
-            shape((HID // zsize, width), F32),
-            shape((1, GAIN_WIDTH), F32),
+            shape((1, rows, width), BF16),
+            shape((1, rows, width), BF16),
+            shape((entries // 128 + 8, 128), F32),
         ),
-        in_specs=[pl.BlockSpec(memory_space=pltpu.VMEM)] * len(operands),
-        out_specs=[pl.BlockSpec(memory_space=pltpu.VMEM)] * 7,
+        in_specs=[smem, smem, anywhere, anywhere, anywhere],
+        out_specs=[vmem, vmem, anywhere],
         scratch_shapes=scratch,
         compiler_params=pltpu.CompilerParams(
-            collective_id=1, has_side_effects=True, vmem_limit_bytes=62 << 20
+            collective_id=1, has_side_effects=True, vmem_limit_bytes=63 << 20
         ),
         name="layer",
-    )(*operands)
+    )(stretch_order, doc_lengths, tokens, cotangent, master)
 
 
 def local_planes(tokens, cotangent, stretch_order, doc_lengths, master, first_moment, second_moment):
-    cycle_size = lax.axis_size("ctx")
-    zsize = lax.axis_size("fsdp")
-    shards = cycle_size * zsize
-    j = lax.axis_index("ctx") * zsize + lax.axis_index("fsdp")
-    _, rows, width = tokens.shape
-    length = rows * cycle_size
+    shards = lax.axis_size("ctx") * lax.axis_size("fsdp")
+    length = tokens.shape[1] * lax.axis_size("ctx")
+    out, xgrad, lines = layer_call(
+        tokens, cotangent, stretch_order, doc_lengths, master
+    )
+    grad = lines.reshape(-1)[: master.shape[0]]
+    new = adam(grad, master, first_moment, second_moment, shards, length)
+    return (out, xgrad, *new)
+
+
+def step_settings(length):
+    return [
+        (MODEL_WIDTH ** (-0.5), DECAY_RATE),
+        ((length / (3.0 * QUERY_HEADS * HEAD_SIZE)) ** 0.5, DECAY_RATE),
+        (MODEL_WIDTH ** (-0.5), DECAY_RATE),
+        (FEED_WIDTH ** (-0.5), DECAY_RATE),
+        (0.2, 0.0),
+    ]
+
+
+def rates(shards, length):
+    settings = step_settings(length)
     spans = [r // shards * w for r, w in segment_shapes()]
-    ends = [sum(spans[: i + 1]) for i in range(5)]
-    low = master.astype(BF16)
-    per = width // shards
-    kv = KEY_VALUE_HEADS * HEAD_SIZE
-    seg = low[: ends[0]].reshape(per, -1)
-    wq_in = jnp.concatenate(
-        [
-            seg[:, : 2 * kv].reshape(per, CTX, QCOLS),
-            seg[:, 2 * kv : 3 * kv].reshape(per, CTX, HEAD_SIZE),
-            seg[:, 3 * kv :].reshape(per, CTX, HEAD_SIZE),
-        ],
-        axis=2,
-    ).transpose(1, 0, 2)
-    wo_in = low[ends[0] : ends[1]].reshape(-1, width)
-    seg = low[ends[1] : ends[2]].reshape(per, 2, CTX, HID)
-    wgu_in = seg.transpose(2, 0, 1, 3).reshape(CTX, per, 2 * HID)
-    wd_in = low[ends[2] : ends[3]].reshape(-1, width)
-    own_gains = low[ends[3] :].astype(F32)
-    gains_in = lax.dynamic_update_slice(
-        jnp.zeros((1, GAIN_WIDTH), F32), own_gains[None, :], (0, j * spans[4])
-    )
-
-    def slots(v):
-        return v.reshape(CHIPS, 2, rows).transpose(1, 0, 2).reshape(length)
-
-    pos = slot_positions(stretch_order, 0, length)
-    _, relative = documents(pos, doc_lengths)
-    pos, relative = slots(pos), slots(relative[0])
-    cosine, sine = rope_tables(relative)
-    sine = jnp.concatenate([-sine[:, : HEAD_SIZE // 2], sine[:, HEAD_SIZE // 2 :]], axis=1)
-    out, xgrad, gq, go, ggu, gd, gg = layer_call(
-        zsize,
-        rows,
-        tokens[0],
-        cotangent[0],
-        wq_in,
-        wo_in,
-        wgu_in,
-        wd_in,
-        gains_in,
-        cosine,
-        sine,
-        pos[:, None],
-        pos[None, :],
-        (pos - relative)[None, :],
-    )
-    gq = gq.astype(F32)
-    gq_rows = jnp.concatenate(
-        [
-            gq[:, :, :QCOLS].transpose(1, 0, 2).reshape(per, -1),
-            gq[:, :, QCOLS : QCOLS + HEAD_SIZE].transpose(1, 0, 2).reshape(per, -1),
-            gq[:, :, QCOLS + HEAD_SIZE :].transpose(1, 0, 2).reshape(per, -1),
-        ],
-        axis=1,
-    )
-    ggu_rows = ggu.reshape(CTX, per, 2, HID).transpose(1, 2, 0, 3)
-    grad = jnp.concatenate(
-        [
-            gq_rows.reshape(-1),
-            go.reshape(-1),
-            ggu_rows.reshape(-1),
-            gd.reshape(-1),
-            lax.dynamic_slice(gg, (0, j * spans[4]), (1, spans[4])).reshape(-1),
-        ]
-    )
-    new = adam(grad, master, first_moment, second_moment, shards, length)
-    return (out[None], xgrad[None], *new)
+    index = lax.iota(jnp.int32, sum(spans))
+    step_rate = jnp.full(index.shape, settings[0][0], F32)
+    decay_value = jnp.full(index.shape, settings[0][1], F32)
+    first = 0
+    for span, (step, decay) in zip(spans, settings):
+        step_rate = jnp.where(index >= first, step, step_rate)
+        decay_value = jnp.where(index >= first, decay, decay_value)
+        first += span
+    return step_rate, decay_value
 
 
 def adam(grad, master, first_moment, second_moment, shards, length):
-    step_rate, decay_value = rate_rows(shards, length)
+    step_rate, decay_value = rates(shards, length)
     new_first = BETA_ONE * first_moment + (1.0 - BETA_ONE) * grad
     new_second = BETA_TWO * second_moment + (1.0 - BETA_TWO) * grad * grad
     normalized = (
@@ -1239,7 +1540,7 @@
         P(("ctx", "fsdp")),
         P(("ctx", "fsdp")),
     )
-    plane = mesh.shape["ctx"] == CTX and KEY_VALUE_HEADS == CTX
+    plane = mesh.shape["ctx"] == CTX == KEY_VALUE_HEADS and mesh.shape["fsdp"] == 4
     return jax.shard_map(
         local_planes if plane else local,
         mesh=mesh,

time: 232 us -> 160 us (0.69)
  Pallas kernels: 203 us -> 151 us
  local copies, waits for them, and re-layouts: 12.6 us -> 1.41 us
  other arithmetic: 13.3 us -> 6.98 us
    pallas_call x1, Pallas kernels: 203 us -> 151 us  [layer_call(): pl.pallas_call(layer_kernel, out_shape=(shape((1, rows, width), BF16), sh...]
    unnamed x36 -> x6, local copies, waits for them, and re-layouts: 6.35 us -> 1.41 us
    reshape x13 -> x0, local copies, waits for them, and re-layouts: 3.81 us -> none  [the longest x1 1.01 us: local_planes(): wgu_in = seg.transpose(2, 0, 1, 3).reshape(CTX, per, 2 * HID)]
    sub x1, other arithmetic: 3.63 us -> 6.98 us  [adam(): new_master = master - step_rate * (normalized + decay_value * master)]
    convert_element_type x3 -> x0, other arithmetic: 2.66 us -> none  [the longest x1 1.64 us: local_planes(): low = master.astype(BF16)]
where the time goes in v2:
time: 160 us
  Pallas kernels  151 us (94%)
  other arithmetic  6.98 us (4%)
    pallas_call x1, Pallas kernels, layer_call(): pl.pallas_call(layer_kernel, out_shape=(shape((1, rows, width), BF16), sh...  151 us
    sub x1, other arithmetic, adam(): new_master = master - step_rate * (normalized + decay_value * master)  6.98 us

profile of v2, /device:TPU:0, one launch (start us, length us, event | category | flops | bytes accessed | tf_op | source)
XLA Modules:
  0.0 159.8 jit_solution(3167508268349745860)
XLA Ops:
  0.6 150.7 %layer.1 = (bf16[1,128,1024]{2,1,0:T(8,128)(2,1)}, bf16[1,128,1024]{2,1,0:T(8,128)(2,1)}, f32[3848,128]{1,0:T(8,128)}) custom-call(s32[16]{0:T(128)} %order_ref.1, s32[1,3]{1,0:T(1,128)} %doc_ref.1, bf16[1,128,1024]{2,1,0:T(8,128)(2,1)} %x_hbm.1, bf16[1,128,1024]{2,1,0:T(8,128)(2,1)} %cot_hbm.1, f32[491592]{0:T(1024)} %master_hbm.1), custom_call_target="tpu_custom_call" | custom-call | tf_op jit(solution)/shard_map/layer/pallas_call | solution.py:1468
  151.4 0.0 copy-start.1
  151.4 0.0 copy-start
  151.4 7.0 %fusion.3 = (f32[491592]{0:T(1024)}, f32[491592]{0:T(1024)}, f32[491592]{0:T(1024)}) fusion(f32[491592]{0:T(1024)} %master_hbm.1, f32[492544]{0:T(1024)} %bitcast.1, f32[491592]{0:T(1024)} %param.12, f32[491592]{0:T(1024)} %param.13), kind=kLoop, calls=%fused_computation.9 | loop fusion | flops 11306616 | bytes 13764576 | tf_op jit(solution)/shard_map/sub | solution.py:1529
  158.4 0.0 copy-done.1
  158.4 0.7 copy.14
  159.1 0.0 copy-done
  159.1 0.7 copy.15
Async XLA Ops:
  151.4 7.0 %copy-start.1 = (bf16[1,128,1024]{2,1,0:T(8,128)(2,1)S(1)}, bf16[1,128,1024]{2,1,0:T(8,128)(2,1)}, u32[]{:S(2)}) copy-start(bf16[1,128,1024]{2,1,0:T(8,128)(2,1)} %get-tuple-element.19) | copy-start | bytes 786436
  151.4 7.7 %copy-start = (bf16[1,128,1024]{2,1,0:T(8,128)(2,1)S(1)}, bf16[1,128,1024]{2,1,0:T(8,128)(2,1)}, u32[]{:S(2)}) copy-start(bf16[1,128,1024]{2,1,0:T(8,128)(2,1)} %get-tuple-element.20) | copy-start | bytes 786436

commit v3 on v2

--- a/solution.py
+++ b/solution.py
@@ -399,6 +399,7 @@
 HID = FEED_WIDTH // CTX
 GAIN_WIDTH = 2 * MODEL_WIDTH + 2 * HEAD_SIZE
 TILE = 256
+WIDE = 512
 
 
 def dot(a, b, dims=((1,), (0,))):
@@ -410,15 +411,20 @@
 
 
 def layer_kernel(
-    order_ref,
-    doc_ref,
+    order_hbm,
+    doc_hbm,
     x_hbm,
     cot_hbm,
     master_hbm,
+    out_hbm,
+    xgrad_hbm,
+    lin_ref,
+    order_ref,
+    doc_ref,
     out_ref,
     xgrad_ref,
-    lin_ref,
     flat,
+    flat_down,
     flat_gains,
     lines,
     wq_in,
@@ -433,7 +439,7 @@
     n1,
     cot,
     n2,
-    gb,
+    x_own,
     wq,
     wo,
     wgu,
@@ -447,6 +453,7 @@
     vt_s,
     probs,
     attn,
+    shares,
     attn_low,
     hidden,
     ggu,
@@ -474,10 +481,6 @@
     asg,
     arq,
     arg_,
-    sum_sq,
-    sum_o,
-    sum_d,
-    sum_gu,
     gz,
     gpl,
     gains,
@@ -536,20 +539,19 @@
     ends = [sum(spans[: i + 1]) for i in range(5)]
     tail = ends[3]
     fetch = [
-        pltpu.make_async_copy(
-            master_hbm.at[pl.ds(0, ends[1])], flat.at[pl.ds(0, ends[1])], loc.at[0]
-        ),
+        pltpu.make_async_copy(master_hbm.at[pl.ds(0, ends[1])], flat, loc.at[0]),
         pltpu.make_async_copy(master_hbm.at[pl.ds(tail, spans[4])], flat_gains, loc.at[3]),
-        pltpu.make_async_copy(
-            master_hbm.at[pl.ds(ends[1], tail - ends[1])],
-            flat.at[pl.ds(ends[1], tail - ends[1])],
-            loc.at[4],
-        ),
+        pltpu.make_async_copy(master_hbm.at[pl.ds(ends[2], spans[3])], flat_down, loc.at[4]),
         pltpu.make_async_copy(x_hbm.at[0], xg.at[slot], loc.at[1]),
         pltpu.make_async_copy(cot_hbm.at[0], cot.at[slot], loc.at[2]),
+        pltpu.make_async_copy(order_hbm, order_ref, loc.at[5]),
+        pltpu.make_async_copy(doc_hbm, doc_ref, loc.at[6]),
     ]
     for copy in fetch:
         copy.start()
+    fetch_feed = pltpu.make_async_copy(
+        master_hbm.at[pl.ds(ends[1], spans[2])], flat, loc.at[0]
+    )
     barrier = pltpu.get_barrier_semaphore()
 
     def greet_plane(i):
@@ -565,10 +567,15 @@
     loop(1, CTX, greet_plane)
     loop(1, 4, greet_z)
 
-    def to_lines(i):
-        lines[pl.ds(pl.multiple_of(i * 128, 128), 128), :] = flat[
-            pl.ds(pl.multiple_of(i * 128 * 128, 128 * 128), 128 * 128)
-        ].reshape(128, 128)
+    def to_lines(src, first, last):
+        block = 128 * 128
+
+        def one(i):
+            lines[pl.ds(pl.multiple_of(first // 128 + i * 128, 128), 128), :] = src[
+                pl.ds(pl.multiple_of(i * block, block), block)
+            ].reshape(128, 128)
+
+        loop(0, (last - first) // block, one)
 
     def qkv_group(j, part):
         return (GROUP * j + part) if part < GROUP else KEY_VALUE_HEADS * part + j
@@ -580,10 +587,11 @@
     def line_rows(first, group, groups, count):
         return pl.ds(first // 128 + group, count, stride=groups)
 
-    per_run = wq_in.shape[1]
+    per_run = wq_in.shape[2]
     fetch[0].wait()
     fetch[1].wait()
-    loop(0, ends[1] // (128 * 128), to_lines)
+    to_lines(flat, 0, ends[1])
+    fetch_feed.start()
     for g in range(MODEL_WIDTH // 128):
         wo[z, :, g * 128 : (g + 1) * 128] = lines[
             line_rows(ends[0], g, MODEL_WIDTH // 128, wo.shape[1]), :
@@ -591,7 +599,7 @@
     qkv_groups = CTX * PCOLS // 128
     for j in range(CTX):
         for part in range(PCOLS // 128):
-            wq_in[j, :, part * 128 : (part + 1) * 128] = lines[
+            wq_in[part // 2, j, :, part % 2 * 128 : (part % 2 + 1) * 128] = lines[
                 line_rows(0, qkv_group(j, part), qkv_groups, per_run), :
             ].astype(BF16)
     own_gains = flat_gains[...].reshape(1, spans[4]).astype(BF16).astype(F32)
@@ -602,7 +610,7 @@
     )
 
     fetch[2].wait()
-    loop(ends[2] // (128 * 128), ends[3] // (128 * 128), to_lines)
+    to_lines(flat_down, ends[2], ends[3])
     for g in range(MODEL_WIDTH // 128):
         wd[z, :, g * 128 : (g + 1) * 128] = lines[
             line_rows(ends[2], g, MODEL_WIDTH // 128, wd.shape[1]), :
@@ -629,7 +637,7 @@
         )[k]
         there = buf.at[core * CHIPS + chip_at(origin), part]
         target = sib if to is sib else chip_at(to) * 2 + core
-        return rcopy(there, there, ag_s.at[n, k], ag_r.at[n, k], target, z)
+        return rcopy(there, there, ag_s.at[n], ag_r.at[n % 3, k], target, z)
 
     def ag_landed(n, buf, k):
         origin, part, own_core = (
@@ -647,7 +655,7 @@
         )[k]
         which = core if own_core else 1 - core
         there = buf.at[which * CHIPS + chip_at(origin), part]
-        return rcopy(there, there, ag_s.at[n, k], ag_r.at[n, k], sib, z)
+        return rcopy(there, there, ag_s.at[n], ag_r.at[n % 3, k], sib, z)
 
     def ag_start(n, buf):
         for k in (1, 3, 2, 4, 0):
@@ -672,8 +680,8 @@
             ag_landed(n, buf, k).wait_recv()
 
     def ag_drain(n, buf):
-        for k in range(11):
-            ag_piece(n, buf, k).wait_send()
+        seven = buf.at[pl.ds(0, 7)]
+        rcopy(seven, seven, ag_s.at[n], ag_r.at[0, 0], sib, z).wait_send()
 
     def gathered_tiles(n, buf, body, between=None):
         ag_pass_near(n, buf)
@@ -688,51 +696,43 @@
     wide = MODEL_WIDTH // 2
 
     def rs_pair(r, h):
-        return rcopy(psnd.at[r % 2, h], prcv.at[r % 2, h], rs_ps.at[r, h], rs_pr.at[r, h], sib, z)
+        return rcopy(psnd.at[h], prcv.at[r % 2, h], rs_ps.at[h], rs_pr.at[r % 2, h], sib, z)
 
     def rs_chip(r, k):
         to = chip_at((XN, XN, YN, YN, YN, XN)[k]) * 2 + core
-        return rcopy(csnd.at[r % 2, k], crcv.at[r % 2, k], rs_cs.at[r, k], rs_cr.at[r, k], to, z)
+        return rcopy(csnd.at[k], crcv.at[r % 2, k], rs_cs.at[k], rs_cr.at[r % 2, k], to, z)
 
     def rs_give(r, part, h):
-        def one(n):
-            out = part(1 - core, h * (wide // TILE) + n).astype(BF16)
-            cols = pl.ds(pl.multiple_of(n * TILE, TILE), TILE)
-            psnd[r % 2, h, :, :, cols] = out.reshape(CHIPS, rows, TILE)
-
-        loop(0, wide // TILE, one)
+        if r > 0:
+            rs_pair(r - 1, h).wait_send()
+        psnd[h] = part(1 - core, h).astype(BF16).reshape(CHIPS, rows, wide)
         rs_pair(r, h).start()
 
     def rs_keep(r, part, h):
-        def one(n):
-            out = part(core, h * (wide // TILE) + n)
-            cols = pl.ds(pl.multiple_of(n * TILE, TILE), TILE)
-            own[h, :, :, cols] = out.reshape(CHIPS, rows, TILE)
-
-        loop(0, wide // TILE, one)
+        own[h] = part(core, h).reshape(CHIPS, rows, wide)
 
     def pair_sum(r, h, i):
         return own[h, chip_at(i)] + prcv[r % 2, h, chip_at(i)].astype(F32)
 
     def rs_send(r, h):
         rs_pair(r, h).wait_recv()
-        csnd[r % 2, 2 * h] = pair_sum(r, h, ACROSS).astype(BF16)
+        if r > 0 and h == 0:
+            for k in range(6):
+                rs_chip(r - 1, k).wait_send()
+        csnd[2 * h] = pair_sum(r, h, ACROSS).astype(BF16)
         rs_chip(r, 2 * h).start()
-        csnd[r % 2, 2 * h + 1] = pair_sum(r, h, (XN, YN)[h]).astype(BF16)
+        csnd[2 * h + 1] = pair_sum(r, h, (XN, YN)[h]).astype(BF16)
         rs_chip(r, 2 * h + 1).start()
         acc[r % 2, :, h * wide : (h + 1) * wide] = pair_sum(r, h, 0)
 
     def rs_begin(r, part):
-        if r > 1:
-            rs_drain(r - 2)
         for h in range(2):
             rs_give(r, part, h)
+        for h in range(2):
             rs_keep(r, part, h)
             rs_send(r, h)
 
     def rs_compute(r, part):
-        if r > 1:
-            rs_drain(r - 2)
         for h in range(2):
             rs_give(r, part, h)
         for h in range(2):
@@ -747,7 +747,7 @@
     def rs_relay(r):
         for h, second in ((0, YN), (1, XN)):
             rs_chip(r, 2 * h).wait_recv()
-            csnd[r % 2, 4 + h] = (pair_sum(r, h, second) + crcv[r % 2, 2 * h].astype(F32)).astype(BF16)
+            csnd[4 + h] = (pair_sum(r, h, second) + crcv[r % 2, 2 * h].astype(F32)).astype(BF16)
             rs_chip(r, 4 + h).start()
 
     def rs_finish(r):
@@ -762,16 +762,16 @@
             )
         return jnp.concatenate(halves, axis=1)
 
-    def a2a(n, src, dst_of, i):
+    def a2a(n, src, dst_of, i, sem=0):
         to = (c + i) % CTX
-        return rcopy(src.at[to], dst_of(c), a2a_s.at[n, i], a2a_r.at[n, i], to, z)
+        return rcopy(src.at[to], dst_of(c), a2a_s.at[n], a2a_r.at[n, sem], to, z)
 
     def a2a_landed(n, dst_of, i):
         frm = (c + CTX - i) % CTX
-        return rcopy(dst_of(frm), dst_of(frm), a2a_s.at[n, i], a2a_r.at[n, i], sib, z)
-
-    def a2a_start(n, src, dst_of):
-        loop(1, CTX, lambda i: a2a(n, src, dst_of, i).start())
+        return rcopy(dst_of(frm), dst_of(frm), a2a_s.at[n], a2a_r.at[n, i - 1], sib, z)
+
+    def a2a_start(n, src, dst_of, apart=False):
+        loop(1, CTX, lambda i: a2a(n, src, dst_of, i, i - 1 if apart else 0).start())
 
     def a2a_half(n, src, dst_of, h):
         def one(i):
@@ -779,11 +779,13 @@
 
         loop(1, CTX, one)
 
-    def a2a_wait(n, dst_of):
-        loop(1, CTX, lambda i: a2a_landed(n, dst_of, i).wait_recv())
-
-    def a2a_drain(n, src, dst_of):
-        loop(1, CTX, lambda i: a2a(n, src, dst_of, i).wait_send())
+    def a2a_wait(n, dst):
+        seven = dst.at[pl.ds(0, CTX - 1)]
+        rcopy(seven, seven, a2a_s.at[n], a2a_r.at[n, 0], sib, z).wait_recv()
+
+    def a2a_drain(n, src):
+        seven = src.at[pl.ds(0, CTX - 1)]
+        rcopy(seven, seven, a2a_s.at[n], a2a_r.at[n, 0], sib, z).wait_send()
 
     inner = (z == 1) | (z == 2)
     outer = jnp.logical_not(inner)
@@ -794,28 +796,39 @@
 
     def zg_own(n, of):
         return (
-            (z < 3, zg(n, of, z, z + 1, 4)),
-            (z > 0, zg(n, of, z, z - 1, 5)),
+            (z < 3, zg(n, of, z, z + 1, 0)),
+            (z > 0, zg(n, of, z, z - 1, 0)),
         )
 
     def zg_onward(n, of):
         return (
-            zg(n, of, z - 1, z + 1, 0),
+            zg(n, of, z - 1, z + 1, 1),
             zg(n, of, z + 1, z - 1, 1),
-            zg(n, of, far, 3 * (z - 1), 2),
-        )
-
-    def zg_start(n, of):
+            zg(n, of, far, 3 * (z - 1), 1),
+        )
+
+    def zg_start(n, of, who=None):
         for there, copy in zg_own(n, of):
-            pl.when(there)(copy.start)
+            pl.when(there if who is None else there & who)(copy.start)
+
+    def zg_pass(n, of, k, when, j):
+        def run():
+            zg(n, of, j, z, 0).wait_recv()
+            zg_onward(n, of)[k].start()
+
+        pl.when(when)(run)
+
+    def zg_across(n, of):
+        zg_pass(n, of, 0, z == 1, z - 1)
+        zg_pass(n, of, 1, z == 2, z + 1)
+
+    def zg_back(n, of):
+        zg_pass(n, of, 1, z == 1, z + 1)
+        zg_pass(n, of, 0, z == 2, z - 1)
 
     def zg_near(n, of):
-        def run():
-            for k, j in ((0, z - 1), (1, z + 1)):
-                zg(n, of, j, z, 0).wait_recv()
-                zg_onward(n, of)[k].start()
-
-        pl.when(inner)(run)
+        zg_across(n, of)
+        zg_back(n, of)
 
     def zg_far(n, of):
         def run():
@@ -831,31 +844,42 @@
 
         pl.when(outer)(run)
 
-    def zg_drain(n, of):
-        for there, copy in zg_own(n, of):
-            pl.when(there)(copy.wait_send)
+    def zg_drain(n, some):
+        def sent(count, sem):
+            part = some(count)
+            rcopy(part, part, zg_s.at[n, sem], zg_r.at[n, 0], c, c).wait_send()
 
         def run():
-            for copy in zg_onward(n, of):
-                copy.wait_send()
+            sent(2, 0)
+            sent(3, 1)
 
         pl.when(inner)(run)
+        pl.when(outer)(lambda: sent(1, 0))
 
     def zr(n, of, land, d, to, spot):
-        return rcopy(of(d), land(spot), zr_s.at[n, d], zr_r.at[n, spot], c, to)
+        return rcopy(of(d), land(spot), zr_s.at[n], zr_r.at[n, spot], c, to)
 
     def zr_add(n, of, land, d):
-        rcopy(land(d), land(d), zr_s.at[n, d], zr_r.at[n, d], sib, z).wait_recv()
+        rcopy(land(d), land(d), zr_s.at[n], zr_r.at[n, d], sib, z).wait_recv()
         mine = of(d)
         mine[...] = (mine[...].astype(F32) + land(d)[...].astype(F32)).astype(BF16)
 
-    ENDS = ((0, 3, 1, 3), (3, 0, 2, 0), (0, 2, 1, 2), (3, 1, 2, 1), (0, 1, 1, 1), (3, 2, 2, 4))
+    ENDS = (
+        ((0, 3, 1, 3), (3, 0, 2, 0)),
+        ((0, 2, 1, 2), (3, 1, 2, 1)),
+        ((0, 1, 1, 1), (3, 2, 2, 4)),
+    )
     FIRST = ((1, 3, 2, 3), (2, 0, 1, 0))
     SECOND = ((1, 2, 2, 2), (2, 1, 1, 4), (1, 0, 0, 4), (2, 3, 3, 3))
 
-    def zr_start(n, of, land):
-        for device, d, to, spot in ENDS:
+    def zr_send(n, of, land, k):
+        for device, d, to, spot in ENDS[k]:
             pl.when(z == device)(zr(n, of, land, d, to, spot).start)
+
+    def zr_start(*items, part=range(3)):
+        for k in part:
+            for item in items:
+                zr_send(*item, k)
 
     def zr_pass(n, of, land, steps):
         for device, d, to, spot in steps:
@@ -872,41 +896,29 @@
     def zr_second(n, of, land):
         zr_pass(n, of, land, SECOND)
 
-    def zr_finish(n, of, land, total):
-        total[...] = of(z)[...].astype(F32)
-
-        def add(spot):
-            rcopy(land(spot), land(spot), zr_s.at[n, 0], zr_r.at[n, spot], sib, z).wait_recv()
-            total[...] += land(spot)[...].astype(F32)
-
-        pl.when(z > 0)(lambda: add(z))
-        pl.when(z < 3)(lambda: add(4))
-
-    def zr_drain(n, of, land):
-        for device, d, to, spot in ENDS + FIRST + SECOND:
-            pl.when(z == device)(zr(n, of, land, d, to, spot).wait_send)
+    def zr_finish(n, of, land):
+        def landed(spot):
+            rcopy(land(spot), land(spot), zr_s.at[n], zr_r.at[n, spot], sib, z).wait_recv()
+
+        pl.when(z > 0)(lambda: landed(z))
+        pl.when(z < 3)(lambda: landed(4))
+        return of(z)[...].astype(F32) + land(z)[...].astype(F32) + land(4)[...].astype(F32)
 
     def row_z(n, src, land, i):
-        return rcopy(src, land.at[z], g_s.at[n, i], g_r.at[n, i], c, (z + i) % 4)
+        return rcopy(src, land.at[z], g_s.at[n, 0], g_r.at[n, 0], c, (z + i) % 4)
 
     def row_plane(n, src, land, i):
-        return rcopy(
-            src, land.at[c], g_s.at[n, 4 + i], g_r.at[n, 4 + i], (c + i) % CTX, z
-        )
+        return rcopy(src, land.at[c], g_s.at[n, 1], g_r.at[n, 1], (c + i) % CTX, z)
+
+    def rows_of(n, land, k):
+        others = land.at[pl.ds(0, (3, CTX - 1)[k])]
+        return rcopy(others, others, g_s.at[n, k], g_r.at[n, k], sib, z)
 
     def row_z_wait(n, land):
-        def one(i):
-            there = land.at[(z + 4 - i) % 4]
-            rcopy(there, there, g_s.at[n, i], g_r.at[n, i], sib, z).wait_recv()
-
-        loop(1, 4, one)
+        rows_of(n, land, 0).wait_recv()
 
     def row_plane_wait(n, land):
-        def one(i):
-            there = land.at[(c + CTX - i) % CTX]
-            rcopy(there, there, g_s.at[n, 4 + i], g_r.at[n, 4 + i], sib, z).wait_recv()
-
-        loop(1, CTX, one)
+        rows_of(n, land, 1).wait_recv()
 
     def halves(ref):
         half_of = lambda h: lambda j: ref.at[pl.ds(h * (CTX // 2), CTX // 2), j]
@@ -916,9 +928,11 @@
         half_of = lambda h: lambda j: ref.at[j, pl.ds(h * (CTX // 2), CTX // 2)]
         return half_of(0), half_of(1)
 
-    wq_at = lambda j: wq.at[j, z]
+    wq_at = lambda j: wq.at[0, j, z]
+    wkv_at = lambda j: wq.at[1, j, z]
     wgu_at = lambda j: wgu.at[j, z]
-    g_q = (0, lambda j: wq.at[:, j])
+    g_q = (0, lambda j: wq.at[0, :, j])
+    g_kv = (5, lambda j: wq.at[1, :, j])
     g_o = (1, lambda j: wo.at[j])
     g_gu1, g_gu2 = ((2 + h, of) for h, of in enumerate(halves(wgu)))
     g_d = (4, lambda j: wd.at[j])
@@ -934,36 +948,44 @@
     lines[pl.ds(tail // 128, 8), :] = jnp.zeros((8, 128), F32)
     gz[z] = gains_in[...]
     loop(1, 4, lambda i: row_z(0, gains_in, gz, i).start())
-    a2a_start(0, wq_in, wq_at)
+    a2a_start(0, wq_in.at[0], wq_at, apart=True)
+    a2a_start(4, wq_in.at[1], wkv_at, apart=True)
     zg_start(*g_o)
-    fetch[3].wait()
-    ag_start(0, xg)
-
-    def share(frm):
-        there = wq.at[frm, z]
-        for k, to, here in ((4, z + 1, z < 3), (5, z - 1, z > 0)):
-            pl.when(here)(rcopy(there, there, zg_s.at[0, k], zg_r.at[0, z], c, to).start)
-
-    def share_landed(i):
-        a2a_landed(0, wq_at, i).wait_recv()
-        share((c + CTX - i) % CTX)
-
-    wq[c, z] = wq_in[c]
-    share(c)
-    loop(ends[1] // (128 * 128), ends[2] // (128 * 128), to_lines)
+
+    def share(part, frm):
+        there = wq.at[part, frm, z]
+        n = 5 * part
+        for to, here in ((z + 1, z < 3), (z - 1, z > 0)):
+            pl.when(here)(rcopy(there, there, zg_s.at[n, 0], zg_r.at[n, z], c, to).start)
+
+    def shares_landed(part, n, at):
+        def one(i):
+            a2a_landed(n, at, i).wait_recv()
+            share(part, (c + CTX - i) % CTX)
+
+        loop(1, CTX, one)
+
+    for part in range(2):
+        wq[part, c, z] = wq_in[part, c]
+        share(part, c)
+    fetch_feed.wait()
+    to_lines(flat, ends[1], ends[2])
     feed_groups = 2 * FEED_WIDTH // 128
     for j in range(CTX):
         for part in range(2 * HID // 128):
             wgu_in[j, :, part * 128 : (part + 1) * 128] = lines[
                 line_rows(ends[1], feed_group(j, part), feed_groups, per_run), :
             ].astype(BF16)
-    loop(1, CTX, share_landed)
+    fetch[3].wait()
+    ag_start(0, xg)
+    shares_landed(0, 0, wq_at)
+    shares_landed(1, 4, wkv_at)
     row_z_wait(0, gz)
     gpl[c] = jnp.sum(gz[...], axis=0)
     loop(1, CTX, lambda i: row_plane(0, gpl.at[c], gpl, i).start())
     wgu[c, z] = wgu_in[c]
-    zg_near(*g_o)
-    fetch[4].wait()
+    for copy in fetch[4:]:
+        copy.wait()
     doc_ends = [doc_ref[0, 0]]
     for j in range(1, doc_ref.shape[1] - 1):
         doc_ends.append(doc_ends[-1] + doc_ref[0, j])
@@ -998,20 +1020,43 @@
         cos_ref[at, :] = jnp.cos(angles)
         sin_ref[at, :] = jnp.where(upper, sine, -sine)
 
-    loop(0, CTX, tables)
+    loop(0, CTX // 2, tables)
+    for land in (lwq, lwo, lwgu, lwd):
+        for end, spot in ((0, 0), (3, 4)):
+
+            def blank(land=land, spot=spot):
+                land[spot] = jnp.zeros(land.shape[1:], BF16)
+
+            pl.when(z == end)(blank)
+    zg_near(*g_q)
+    loop(CTX // 2, CTX, tables)
     ag_pass_near(0, xg)
-    zg_near(*g_q)
-    zg_far(*g_o)
+    zg_near(*g_kv)
     ag_finish_near(0, xg)
     ag_pass_across(0, xg)
+    zg_far(*g_q)
     ag_finish(0, xg)
     a2a_start(1, wgu_in, wgu_at)
     ag_start(1, cot)
-    zg_far(*g_q)
+    zg_far(*g_kv)
+    zg_near(*g_o)
     row_plane_wait(0, gpl)
     gains[...] = jnp.sum(gpl[...], axis=0)
     g_attn = gains[:, :MODEL_WIDTH]
+    def normed(t):
+        at = pl.ds(t * (TILE // rows), TILE // rows)
+        x_tile = xg[at].astype(F32)
+        x_scale = lax.rsqrt(jnp.mean(x_tile * x_tile, axis=-1, keepdims=True) + NORM_EPS)
+        n1[at] = (x_tile * x_scale * g_attn.reshape(1, 1, MODEL_WIDTH)).astype(BF16)
+
+    loop(0, tiles, normed)
+    x_own[...] = xg[slot]
+    pl.when(outer)(lambda: a2a_wait(1, wgu_in))
+    zg_start(*g_gu1, outer)
+    zg_start(*g_gu2, outer)
+    zg_start(*g_d, outer)
     zg_wait(*g_q)
+    zg_wait(*g_kv)
 
     g_query = gains[:, 2 * MODEL_WIDTH : 2 * MODEL_WIDTH + HEAD_SIZE]
     g_key = gains[:, 2 * MODEL_WIDTH + HEAD_SIZE :]
@@ -1034,73 +1079,75 @@
             y = raw * scale * gain
             return y * cosine + turned(y) * sine
 
-        x_tile = two(xg, t).astype(F32)
-        x_scale = lax.rsqrt(jnp.mean(x_tile * x_tile, axis=-1, keepdims=True) + NORM_EPS)
-        normed_one = (x_tile * x_scale * g_attn).astype(BF16)
-        n1[pl.ds(t * (TILE // rows), TILE // rows)] = normed_one.reshape(
-            TILE // rows, rows, MODEL_WIDTH
-        )
-        out = dot(normed_one, wq[...].reshape(MODEL_WIDTH, PCOLS))
+        out = dot(two(n1, t), wq[0].reshape(MODEL_WIDTH, QCOLS))
+        both = dot(two(n1, t), wq[1].reshape(MODEL_WIDTH, 2 * HEAD_SIZE))
         for h in range(GROUP):
             raw = out[:, h * HEAD_SIZE : (h + 1) * HEAD_SIZE]
             qraw[at, h * HEAD_SIZE : (h + 1) * HEAD_SIZE] = raw
             q_s[h, at, :] = normed(raw, g_query).astype(BF16)
-        raw = out[:, QCOLS : QCOLS + HEAD_SIZE]
+        raw = both[:, :HEAD_SIZE]
         kraw[at, :] = raw
         keys = normed(raw, g_key)
-        values = out[:, QCOLS + HEAD_SIZE :]
+        values = both[:, HEAD_SIZE:]
         k_s[at, :] = keys.astype(BF16)
         v_s[at, :] = values.astype(BF16)
         kt_s[:, at] = keys.T.astype(BF16)
         vt_s[:, at] = values.T.astype(BF16)
 
     loop(0, tiles, project)
-    a2a_wait(1, wgu_at)
-    zg_start(*g_gu1)
-    zg_start(*g_gu2)
-    zg_start(*g_d)
+    ag_drain(0, xg)
+    zg_far(*g_o)
+    pl.when(inner)(lambda: a2a_wait(1, wgu_in))
+    zg_start(*g_gu1, inner)
+    zg_start(*g_gu2, inner)
+    def n_cols(n):
+        return pl.ds(pl.multiple_of(n * WIDE, WIDE), WIDE)
+
+    def half_rows(which):
+        return pl.ds(pl.multiple_of(which * half, half), half)
+
+    def half_slots(buf, which):
+        return buf[pl.ds(which * CHIPS, CHIPS)].reshape(half, buf.shape[-1])
+
+    def out_part(which, n):
+        return dot(
+            attn_low[half_rows(which), :], wo[:, :, n_cols(n)].reshape(QCOLS, WIDE)
+        )
+
     scale = HEAD_SIZE ** (-0.5)
 
     def attend(t):
-        at = tile_rows(t)
-        kpos = jnp.concatenate([kpos_ref[...]] * (TILE // HEAD_SIZE), axis=1)
+        at = half_rows(t)
+        kpos = jnp.concatenate([kpos_ref[...]] * (half // HEAD_SIZE), axis=1)
         kept = (kpos <= qpos_ref[:, at]) & (kpos >= qstart_ref[:, at])
         for h in range(GROUP):
             scores = jnp.where(kept, dot(k_s[...], q_s[h, at, :], NT) * scale, MASKED)
             weights = jnp.exp(scores - jnp.max(scores, axis=0, keepdims=True))
+            low = weights.astype(BF16)
+            probs[h, t] = low
             share = 1.0 / jnp.sum(weights, axis=0, keepdims=True)
-            low = (weights * share).astype(BF16)
-            probs[h, t] = low
-            mixed = dot(vt_s[...], low).T
-            attn[at, h * HEAD_SIZE : (h + 1) * HEAD_SIZE] = mixed
-            attn_low[at, h * HEAD_SIZE : (h + 1) * HEAD_SIZE] = mixed.astype(BF16)
-
-    loop(0, tiles // 2, attend)
+            shares[h, :, at] = share
+            mixed = dot(vt_s[...], low) * share
+            attn[h, :, at] = mixed
+            attn_low[at, h * HEAD_SIZE : (h + 1) * HEAD_SIZE] = mixed.T.astype(BF16)
+
+    attend(1 - core)
+    zg_across(*g_gu1)
+    zg_wait(*g_o)
+    rs_give(0, out_part, 0)
+    rs_give(0, out_part, 1)
     ag_pass_near(1, cot)
-    loop(tiles // 2, tiles, attend)
-
-    zg_wait(*g_o)
+    attend(core)
     ag_pass_across(1, cot)
-
-    def n_cols(n):
-        return pl.ds(pl.multiple_of(n * TILE, TILE), TILE)
-
-    def half_rows(which):
-        return pl.ds(pl.multiple_of(which * half, half), half)
-
-    def half_slots(buf, which):
-        return buf[pl.ds(which * CHIPS, CHIPS)].reshape(half, buf.shape[-1])
-
-    def out_part(which, n):
-        return dot(
-            attn_low[half_rows(which), :], wo[:, :, n_cols(n)].reshape(QCOLS, TILE)
-        )
-
-    rs_begin(0, out_part)
-    zg_near(*g_gu1)
+    for h in range(2):
+        rs_keep(0, out_part, h)
+        rs_send(0, h)
+    zg_across(*g_gu2)
+    zg_back(*g_gu1)
+    zg_back(*g_gu2)
     rs_relay(0)
-    zg_near(*g_gu2)
-    resid = xg[slot].astype(F32) + rs_finish(0)
+    zg_far(*g_gu1)
+    resid = x_own[...].astype(F32) + rs_finish(0)
     resid_s[...] = resid
     g_mlp = gains[:, MODEL_WIDTH : 2 * MODEL_WIDTH]
     s_two = lax.rsqrt(jnp.mean(resid * resid, axis=-1, keepdims=True) + NORM_EPS)
@@ -1108,11 +1155,12 @@
     ag_start(2, n2)
     ag_finish_near(1, cot)
     ag_finish(1, cot)
-    zg_far(*g_gu1)
-    zg_near(*g_d)
+    zg_far(*g_gu2)
+    zg_start(*g_d, inner)
+    zg_across(*g_d)
     ag_pass_near(2, n2)
     ag_finish_near(2, n2)
-    zg_far(*g_gu2)
+    zg_back(*g_d)
     ag_pass_across(2, n2)
     ag_finish(2, n2)
     zg_far(*g_d)
@@ -1132,13 +1180,13 @@
     loop(0, tiles, feed)
 
     def down_grad(n):
-        there = cot[:, :, n_cols(n)].reshape(2 * half, TILE)
+        there = cot[:, :, n_cols(n)].reshape(2 * half, WIDE)
         gwd[:, :, n_cols(n)] = (
-            dot(hidden[...], there, TN).astype(BF16).reshape(4, HID // 4, TILE)
-        )
-
-    loop(0, MODEL_WIDTH // TILE, down_grad)
-    zr_start(*r_d)
+            dot(hidden[...], there, TN).astype(BF16).reshape(4, HID // 4, WIDE)
+        )
+
+    loop(0, MODEL_WIDTH // WIDE, down_grad)
+    zr_start(r_d)
     zg_wait(*g_d)
 
     def feed_back(t):
@@ -1151,24 +1199,24 @@
 
     def back_two_part(which, n):
         per = MODEL_WIDTH // CTX
-        there = wgu[pl.ds(n * (TILE // per), TILE // per)].reshape(TILE, 2 * HID)
+        there = wgu[pl.ds(n * (WIDE // per), WIDE // per)].reshape(WIDE, 2 * HID)
         return dot(ggu[half_rows(which), :], there, NT)
 
     rs_begin(1, back_two_part)
 
     def gate_up_grad(n):
         per = MODEL_WIDTH // CTX
-        there = n2[:, :, n_cols(n)].reshape(2 * half, TILE)
-        gwgu[pl.ds(n * (TILE // per), TILE // per)] = (
+        there = n2[:, :, n_cols(n)].reshape(2 * half, WIDE)
+        gwgu[pl.ds(n * (WIDE // per), WIDE // per)] = (
             dot(there, ggu[...], TN)
             .astype(BF16)
-            .reshape(TILE // per, 4, per // 4, 2 * HID)
-        )
-
-    loop(0, MODEL_WIDTH // TILE // 2, gate_up_grad)
-    zr_start(*r_gu1)
-    loop(MODEL_WIDTH // TILE // 2, MODEL_WIDTH // TILE, gate_up_grad)
-    zr_start(*r_gu2)
+            .reshape(WIDE // per, 4, per // 4, 2 * HID)
+        )
+
+    gate_up_grad(0)
+    zr_start(r_gu1)
+    gate_up_grad(1)
+    zr_start(r_gu2)
     zr_first(*r_d)
     rs_relay(1)
 
@@ -1184,9 +1232,10 @@
     hrow[:, MODEL_WIDTH : 2 * MODEL_WIDTH] = terms
     gresid = cot[slot].astype(F32) + back
     gresid_s[...] = gresid
+    gb = xg
     gb[slot] = gresid.astype(BF16)
     def down_part(which, n):
-        return dot(hidden[half_rows(which), :], wd[:, :, n_cols(n)].reshape(HID, TILE))
+        return dot(hidden[half_rows(which), :], wd[:, :, n_cols(n)].reshape(HID, WIDE))
 
     ag_start(3, gb)
     rs_compute(2, down_part)
@@ -1201,125 +1250,128 @@
     rs_send(2, 0)
     rs_send(2, 1)
 
+    def out_grad(n):
+        there = gb[:, :, n_cols(n)].reshape(2 * half, WIDE)
+        gwo[:, :, n_cols(n)] = (
+            dot(attn_low[...], there, TN).astype(BF16).reshape(4, QCOLS // 4, WIDE)
+        )
+
+    loop(0, MODEL_WIDTH // WIDE, out_grad)
+    zr_start(r_o, part=(0, 1))
+
     dk_s[...] = jnp.zeros_like(dk_s)
     dv_s[...] = jnp.zeros_like(dv_s)
 
+    hrow[:, 2 * MODEL_WIDTH :] = jnp.zeros((1, 2 * HEAD_SIZE), F32)
+
+    def head_back(raw, grads, at, gain):
+        grads = grads * scale
+        grads = grads * cos_ref[at, :] - turned(grads) * sin_ref[at, :]
+        return norm_back(raw, grads, gain)
+
+    q_terms = pl.ds(2 * MODEL_WIDTH, HEAD_SIZE)
+    k_terms = pl.ds(2 * MODEL_WIDTH + HEAD_SIZE, HEAD_SIZE)
+
     def attend_back(t):
-        at = tile_rows(t)
+        at = pl.ds(t * half, half)
         for h in range(GROUP):
             head = slice(h * HEAD_SIZE, (h + 1) * HEAD_SIZE)
             grads = gattn[at, head]
-            delta = jnp.sum((grads.astype(F32) * attn[at, head]).T, axis=0, keepdims=True)
+            turned_grads = grads.astype(F32).T
+            share = shares[h, :, at]
+            delta = jnp.sum(turned_grads * attn[h, :, at], axis=0, keepdims=True)
             low = probs[h, t]
             gprobs = dot(v_s[...], grads, NT)
-            gscores = (low.astype(F32) * (gprobs - delta)).astype(BF16)
-            dv_s[...] += dot(low, grads)
+            gscores = (low.astype(F32) * ((gprobs - delta) * share)).astype(BF16)
+            dv_s[...] += dot(low, (turned_grads * share).T.astype(BF16))
             dk_s[...] += dot(gscores, q_s[h, at, :])
-            attn[at, head] = dot(kt_s[...], gscores).T
-
-    loop(0, tiles // 2, attend_back)
+            back, terms = head_back(qraw[at, head], dot(kt_s[...], gscores).T, at, g_query)
+            gp[at, head] = back.astype(BF16)
+            hrow[:, q_terms] += terms
+
+    attend_back(0)
     zr_second(*r_gu1)
-    loop(tiles // 2, tiles, attend_back)
+    attend_back(1)
     rs_relay(2)
     zr_first(*r_gu2)
 
-    hrow[:, 2 * MODEL_WIDTH :] = jnp.zeros((1, 2 * HEAD_SIZE), F32)
-
     def project_back(t):
         at = tile_rows(t)
-        cosine, sine = cos_ref[at, :], sin_ref[at, :]
-
-        def one(raw, grads, gain):
-            grads = grads * scale
-            grads = grads * cosine - turned(grads) * sine
-            return norm_back(raw, grads, gain)
-
-        lo = 2 * MODEL_WIDTH
-        for h in range(GROUP):
-            head = slice(h * HEAD_SIZE, (h + 1) * HEAD_SIZE)
-            back, terms = one(qraw[at, head], attn[at, head], g_query)
-            gp[at, head] = back.astype(BF16)
-            hrow[:, lo : lo + HEAD_SIZE] += terms
-        back, terms = one(kraw[at, :], dk_s[at, :], g_key)
+        back, terms = head_back(kraw[at, :], dk_s[at, :], at, g_key)
         gp[at, QCOLS : QCOLS + HEAD_SIZE] = back.astype(BF16)
-        hrow[:, lo + HEAD_SIZE :] += terms
+        hrow[:, k_terms] += terms
         gp[at, QCOLS + HEAD_SIZE :] = dv_s[at, :].astype(BF16)
 
     loop(0, tiles, project_back)
 
     def qkv_grad(n):
         per = MODEL_WIDTH // CTX
-        there = n1[:, :, n_cols(n)].reshape(2 * half, TILE)
-        gwq[pl.ds(n * (TILE // per), TILE // per)] = (
+        there = n1[:, :, n_cols(n)].reshape(2 * half, WIDE)
+        gwq[pl.ds(n * (WIDE // per), WIDE // per)] = (
             dot(there, gp[...], TN)
             .astype(BF16)
-            .reshape(TILE // per, 4, per // 4, PCOLS)
-        )
-
-    loop(0, MODEL_WIDTH // TILE // 2, qkv_grad)
-    zr_start(*r_q1)
-    loop(MODEL_WIDTH // TILE // 2, MODEL_WIDTH // TILE, qkv_grad)
-    zr_start(*r_q2)
-    zr_second(*r_gu2)
-
+            .reshape(WIDE // per, 4, per // 4, PCOLS)
+        )
+
+    qkv_grad(0)
+    qkv_grad(1)
+    zr_start(r_q1, r_q2, part=(0, 1))
     def back_one_part(which, n):
         per = MODEL_WIDTH // CTX
-        there = wq[pl.ds(n * (TILE // per), TILE // per)].reshape(TILE, PCOLS)
-        return dot(gp[half_rows(which), :], there, NT)
+        at = pl.ds(n * (WIDE // per), WIDE // per)
+        rows_at = half_rows(which)
+        return dot(gp[rows_at, :QCOLS], wq[0, at].reshape(WIDE, QCOLS), NT) + dot(
+            gp[rows_at, QCOLS:], wq[1, at].reshape(WIDE, 2 * HEAD_SIZE), NT
+        )
 
     rs_begin(3, back_one_part)
+    zr_second(*r_gu2)
+    rs_relay(3)
+    zr_first(*r_o)
     zr_first(*r_q1)
-
-    def out_grad(n):
-        there = gb[:, :, n_cols(n)].reshape(2 * half, TILE)
-        gwo[:, :, n_cols(n)] = (
-            dot(attn_low[...], there, TN).astype(BF16).reshape(4, QCOLS // 4, TILE)
-        )
-
-    loop(0, MODEL_WIDTH // TILE, out_grad)
-    zr_start(*r_o)
     zr_first(*r_q2)
-    rs_relay(3)
-    zr_second(*r_q1)
-    zr_finish(*r_d, sum_d)
+    zr_second(*r_o)
+    sum_d = zr_finish(*r_d)
     for g in range(MODEL_WIDTH // 128):
         lines[line_rows(ends[2], g, MODEL_WIDTH // 128, sum_d.shape[0]), :] = sum_d[
             :, g * 128 : (g + 1) * 128
         ]
-    zr_finish(*r_gu1, sum_gu.at[pl.ds(0, CTX // 2)])
-    zr_finish(*r_gu2, sum_gu.at[pl.ds(CTX // 2, CTX // 2)])
-    asg[...] = sum_gu[...].astype(BF16)
-    arg_at = lambda j: arg_.at[j]
-    a2a_start(2, asg, arg_at)
+    first_half, second_half = pl.ds(0, CTX // 2), pl.ds(CTX // 2, CTX // 2)
+    asg[first_half] = zr_finish(*r_gu1).astype(BF16)
+    asg[second_half] = zr_finish(*r_gu2).astype(BF16)
     arg_[c] = asg[c]
-    zr_second(*r_q2)
-    back, terms = norm_back(xg[slot].astype(F32), rs_finish(3), gains[:, :MODEL_WIDTH])
-    xgrad_ref[0] = (gresid_s[...] + back).astype(BF16)
+    zr_second(*r_q1)
+    back, terms = norm_back(x_own[...].astype(F32), rs_finish(3), gains[:, :MODEL_WIDTH])
+    xgrad_ref[...] = (gresid_s[...] + back).astype(BF16)
+    store_xgrad = pltpu.make_async_copy(xgrad_ref, xgrad_hbm.at[0], loc.at[5])
+    store_xgrad.start()
     hrow[:, :MODEL_WIDTH] = terms
     hz[z] = hrow[...]
     loop(1, 4, lambda i: row_z(1, hrow, hz, i).start())
-    zr_first(*r_o)
-    out_ref[0] = (resid_s[...] + rs_finish(2)).astype(BF16)
-    arq_at = lambda j: arq.at[j]
-    first_half, second_half = pl.ds(0, CTX // 2), pl.ds(CTX // 2, CTX // 2)
-    zr_finish(*r_q1, sum_sq.at[first_half])
-    asq[first_half] = sum_sq[first_half].astype(BF16)
-    a2a_half(3, asq, arq_at, 0)
-    zr_finish(*r_q2, sum_sq.at[second_half])
-    asq[second_half] = sum_sq[second_half].astype(BF16)
-    a2a_half(3, asq, arq_at, 1)
-    arq[c] = asq[c]
-    zr_second(*r_o)
+    zr_start(r_q1, r_q2, part=(2,))
+    zr_start(r_o, part=(2,))
+    arg_at = lambda j: arg_.at[j]
+    a2a_start(2, asg, arg_at)
+    zr_second(*r_q2)
+    out_ref[...] = (resid_s[...] + rs_finish(2)).astype(BF16)
+    store_out = pltpu.make_async_copy(out_ref, out_hbm.at[0], loc.at[6])
+    store_out.start()
     row_z_wait(1, hz)
     hpl[c] = jnp.sum(hz[...], axis=0)
     loop(1, CTX, lambda i: row_plane(1, hpl.at[c], hpl, i).start())
-    a2a_wait(2, arg_at)
+    arq_at = lambda j: arq.at[j]
+    asq[first_half] = zr_finish(*r_q1).astype(BF16)
+    a2a_half(3, asq, arq_at, 0)
+    asq[second_half] = zr_finish(*r_q2).astype(BF16)
+    a2a_half(3, asq, arq_at, 1)
+    arq[c] = asq[c]
+    a2a_wait(2, arg_)
     for j in range(CTX):
         for part in range(2 * HID // 128):
             lines[line_rows(ends[1], feed_group(j, part), feed_groups, per_run), :] = arg_[
                 j, :, part * 128 : (part + 1) * 128
             ].astype(F32)
-    a2a_wait(3, arq_at)
+    a2a_wait(3, arq)
     for j in range(CTX):
         for part in range(PCOLS // 128):
             lines[line_rows(0, qkv_group(j, part), qkv_groups, per_run), :] = arq[
@@ -1336,7 +1388,7 @@
     ]
     stores[0].start()
     stores[1].start()
-    zr_finish(*r_o, sum_o)
+    sum_o = zr_finish(*r_o)
     for g in range(MODEL_WIDTH // 128):
         lines[line_rows(ends[0], g, MODEL_WIDTH // 128, sum_o.shape[0]), :] = sum_o[
             :, g * 128 : (g + 1) * 128
@@ -1349,23 +1401,38 @@
     )[:, :128]
     stores[3].start()
 
-    for n, buf in enumerate((xg, cot, n2, gb)):
+    for n, buf in ((1, cot), (2, n2), (3, gb)):
         ag_drain(n, buf)
-    rs_drain(2)
     rs_drain(3)
-    a2a_drain(0, wq_in, wq_at)
-    a2a_drain(1, wgu_in, wgu_at)
-    a2a_drain(2, asg, arg_at)
-    a2a_drain(3, asq, arq_at)
-    for item in (g_q, g_o, g_gu1, g_gu2, g_d):
-        zg_drain(*item)
-    for item in (r_d, r_gu1, r_gu2, r_o, r_q1, r_q2):
-        zr_drain(*item)
-    loop(1, 4, lambda i: row_z(0, gains_in, gz, i).wait_send())
-    loop(1, CTX, lambda i: row_plane(0, gpl.at[c], gpl, i).wait_send())
-    loop(1, 4, lambda i: row_z(1, hrow, hz, i).wait_send())
-    loop(1, CTX, lambda i: row_plane(1, hpl.at[c], hpl, i).wait_send())
-    for copy in stores:
+    a2a_drain(0, wq_in.at[0])
+    a2a_drain(4, wq_in.at[1])
+    a2a_drain(1, wgu_in)
+    a2a_drain(2, asg)
+    a2a_drain(3, asq)
+    first_four = pl.ds(0, CTX // 2)
+    for n, some in (
+        (0, lambda count: wq.at[0, :, pl.ds(0, count)]),
+        (5, lambda count: wq.at[1, :, pl.ds(0, count)]),
+        (1, lambda count: wo.at[pl.ds(0, count)]),
+        (2, lambda count: wgu.at[first_four, pl.ds(0, count)]),
+        (3, lambda count: wgu.at[first_four, pl.ds(0, count)]),
+        (4, lambda count: wd.at[pl.ds(0, count)]),
+    ):
+        zg_drain(n, some)
+    three = pl.ds(0, 3)
+    for n, part in (
+        (0, lwd.at[three]),
+        (1, lwgu.at[three, first_four]),
+        (2, lwgu.at[three, first_four]),
+        (3, lwo.at[three]),
+        (4, lwq.at[three, first_four]),
+        (5, lwq.at[three, first_four]),
+    ):
+        rcopy(part, part, zr_s.at[n], zr_r.at[n, 0], sib, z).wait_send()
+    for n, lands in enumerate(((gz, gpl), (hz, hpl))):
+        for k, land in enumerate(lands):
+            rows_of(n, land, k).wait_send()
+    for copy in (store_out, store_xgrad, *stores):
         copy.wait()
 
 
@@ -1380,10 +1447,15 @@
     shape = jax.ShapeDtypeStruct
     full = vm((CTX, rows, width), BF16)
     scratch = [
-        vm((entries,), F32),
+        pltpu.SMEM(stretch_order.shape, jnp.int32),
+        pltpu.SMEM(doc_lengths.shape, jnp.int32),
+        vm((rows, width), BF16),
+        vm((rows, width), BF16),
+        vm((width * 4 * width // 32 + 2 * width * width // 32,), F32),
+        vm((FEED_WIDTH * width // 32,), F32),
         vm((master.shape[0] - entries,), F32),
         vm((entries // 128 + 8, 128), F32),
-        vm((CTX, per, PCOLS), BF16),
+        vm((2, CTX, per, QCOLS), BF16),
         vm((CTX, per, 2 * HID), BF16),
         vm((1, GAIN_WIDTH), F32),
         vm((length, HEAD_SIZE), F32),
@@ -1395,8 +1467,8 @@
         full,
         full,
         full,
-        full,
-        vm((CTX, 4, per, PCOLS), BF16),
+        vm((rows, width), BF16),
+        vm((2, CTX, 4, per, QCOLS), BF16),
         vm((4, QCOLS // 4, width), BF16),
         vm((CTX, 4, per, 2 * HID), BF16),
         vm((4, HID // 4, width), BF16),
@@ -1407,8 +1479,9 @@
         vm((length, HEAD_SIZE), BF16),
         vm((HEAD_SIZE, length), BF16),
         vm((HEAD_SIZE, length), BF16),
-        vm((GROUP, tiles, length, TILE), BF16),
-        vm((length, QCOLS), F32),
+        vm((GROUP, 2, length, length // 2), BF16),
+        vm((GROUP, HEAD_SIZE, length), F32),
+        vm((GROUP, 1, length), F32),
         vm((length, QCOLS), BF16),
         vm((length, HID), BF16),
         vm((length, 2 * HID), BF16),
@@ -1416,9 +1489,9 @@
         vm((length, HEAD_SIZE), F32),
         vm((length, HEAD_SIZE), F32),
         vm((length, PCOLS), BF16),
+        vm((2, CHIPS, rows, width // 2), BF16),
         vm((2, 2, CHIPS, rows, width // 2), BF16),
-        vm((2, 2, CHIPS, rows, width // 2), BF16),
-        vm((2, 6, rows, width // 2), BF16),
+        vm((6, rows, width // 2), BF16),
         vm((2, 6, rows, width // 2), BF16),
         vm((2, CHIPS, rows, width // 2), F32),
         vm((2, rows, width), F32),
@@ -1436,34 +1509,28 @@
         vm((CTX, per, 2 * HID), BF16),
         vm((CTX, per, PCOLS), BF16),
         vm((CTX, per, 2 * HID), BF16),
-        vm((CTX, per, PCOLS), F32),
-        vm((QCOLS // 4, width), F32),
-        vm((HID // 4, width), F32),
-        vm((CTX, per, 2 * HID), F32),
         vm((4, 1, GAIN_WIDTH), F32),
         vm((CTX, 1, GAIN_WIDTH), F32),
         vm((1, GAIN_WIDTH), F32),
         vm((4, 1, GAIN_WIDTH), F32),
         vm((CTX, 1, GAIN_WIDTH), F32),
         vm((1, GAIN_WIDTH), F32),
-        dma((4, 11)),
-        dma((4, 11)),
-        dma((4, 2)),
-        dma((4, 2)),
-        dma((4, 6)),
-        dma((4, 6)),
-        dma((4, CTX)),
-        dma((4, CTX)),
-        dma((5, 6)),
-        dma((5, 4)),
+        dma((4,)),
+        dma((3, 11)),
+        dma((2,)),
+        dma((2, 2)),
+        dma((6,)),
+        dma((2, 6)),
+        dma((5,)),
+        dma((5, CTX - 1)),
+        dma((6, 2)),
         dma((6, 4)),
+        dma((6,)),
         dma((6, 5)),
-        dma((2, 4 + CTX)),
-        dma((2, 4 + CTX)),
-        dma((5,)),
+        dma((2, 2)),
+        dma((2, 2)),
+        dma((8,)),
     ]
-    smem = pl.BlockSpec(memory_space=pltpu.SMEM)
-    vmem = pl.BlockSpec(memory_space=pltpu.VMEM)
     anywhere = pl.BlockSpec(memory_space=pl.ANY)
     return pl.pallas_call(
         layer_kernel,
@@ -1472,8 +1539,8 @@
             shape((1, rows, width), BF16),
             shape((entries // 128 + 8, 128), F32),
         ),
-        in_specs=[smem, smem, anywhere, anywhere, anywhere],
-        out_specs=[vmem, vmem, anywhere],
+        in_specs=[anywhere] * 5,
+        out_specs=[anywhere] * 3,
         scratch_shapes=scratch,
         compiler_params=pltpu.CompilerParams(
             collective_id=1, has_side_effects=True, vmem_limit_bytes=63 << 20

time: 160 us -> 145 us (0.906)
  Pallas kernels: 151 us -> 136 us
    pallas_call x1, Pallas kernels: 151 us -> 136 us  [layer_call(): pl.pallas_call(layer_kernel, out_shape=(shape((1, rows, width), BF16), sh...]
where the time goes in v3:
time: 145 us
  Pallas kernels  136 us (94%)
  other arithmetic  6.98 us (5%)
    pallas_call x1, Pallas kernels, layer_call(): pl.pallas_call(layer_kernel, out_shape=(shape((1, rows, width), BF16), sh...  136 us
    sub x1, other arithmetic, adam(): new_master = master - step_rate * (normalized + decay_value * master)  6.98 us

profile of v3, /device:TPU:0, one launch (start us, length us, event | category | flops | bytes accessed | tf_op | source)
XLA Modules:
  0.0 144.6 jit_solution(7675253171557636753)
XLA Ops:
  0.6 135.5 %layer.1 = (bf16[1,128,1024]{2,1,0:T(8,128)(2,1)}, bf16[1,128,1024]{2,1,0:T(8,128)(2,1)}, f32[3848,128]{1,0:T(8,128)}) custom-call(s32[16]{0:T(128)} %order_hbm.1, s32[1,3]{1,0:T(1,128)} %doc_hbm.1, bf16[1,128,1024]{2,1,0:T(8,128)(2,1)} %x_hbm.1, bf16[1,128,1024]{2,1,0:T(8,128)(2,1)} %cot_hbm.1, f32[491592]{0:T(1024)} %master_hbm.1), custom_call_target="tpu_custom_call" | custom-call | tf_op jit(solution)/shard_map/layer/pallas_call | solution.py:1535
  136.2 0.0 copy-start.1
  136.2 0.0 copy-start
  136.2 7.0 %fusion.3 = (f32[491592]{0:T(1024)}, f32[491592]{0:T(1024)}, f32[491592]{0:T(1024)}) fusion(f32[491592]{0:T(1024)} %master_hbm.1, f32[492544]{0:T(1024)} %bitcast.1, f32[491592]{0:T(1024)} %param.12, f32[491592]{0:T(1024)} %param.13), kind=kLoop, calls=%fused_computation.9 | loop fusion | flops 11306616 | bytes 13764576 | tf_op jit(solution)/shard_map/sub | solution.py:1596
  143.2 0.0 copy-done.1
  143.2 0.7 copy.14
  143.9 0.0 copy-done
  143.9 0.7 copy.15
Async XLA Ops:
  136.2 7.0 %copy-start.1 = (bf16[1,128,1024]{2,1,0:T(8,128)(2,1)S(1)}, bf16[1,128,1024]{2,1,0:T(8,128)(2,1)}, u32[]{:S(2)}) copy-start(bf16[1,128,1024]{2,1,0:T(8,128)(2,1)} %get-tuple-element.19) | copy-start | bytes 786436
  136.2 7.7 %copy-start = (bf16[1,128,1024]{2,1,0:T(8,128)(2,1)S(1)}, bf16[1,128,1024]{2,1,0:T(8,128)(2,1)}, u32[]{:S(2)}) copy-start(bf16[1,128,1024]{2,1,0:T(8,128)(2,1)} %get-tuple-element.20) | copy-start | bytes 786436

commit v4 on v3

--- a/solution.py
+++ b/solution.py
@@ -1,3 +1,4 @@
+import functools
 import math
 
 import jax
@@ -621,6 +622,8 @@
     XN, YN, ACROSS = 1, 2, 3
     whole, top, bottom = pl.ds(0, rows), pl.ds(0, mid), pl.ds(mid, mid)
 
+    AG_SEM = (0, 1, 2, 3, 4, 5, 6, 0, 7, 7, 7)
+
     def ag_piece(n, buf, k):
         origin, part, to = (
             (0, whole, sib),
@@ -637,7 +640,7 @@
         )[k]
         there = buf.at[core * CHIPS + chip_at(origin), part]
         target = sib if to is sib else chip_at(to) * 2 + core
-        return rcopy(there, there, ag_s.at[n], ag_r.at[n % 3, k], target, z)
+        return rcopy(there, there, ag_s.at[n], ag_r.at[n % 3, AG_SEM[k]], target, z)
 
     def ag_landed(n, buf, k):
         origin, part, own_core = (
@@ -655,7 +658,7 @@
         )[k]
         which = core if own_core else 1 - core
         there = buf.at[which * CHIPS + chip_at(origin), part]
-        return rcopy(there, there, ag_s.at[n], ag_r.at[n % 3, k], sib, z)
+        return rcopy(there, there, ag_s.at[n], ag_r.at[n % 3, AG_SEM[k]], sib, z)
 
     def ag_start(n, buf):
         for k in (1, 3, 2, 4, 0):
@@ -671,24 +674,27 @@
             ag_landed(n, buf, landed).wait_recv()
             ag_piece(n, buf, onward).start()
 
+    def ag_handed(n, buf, sem):
+        two_rows = buf.at[pl.ds(0, 2)]
+        rcopy(two_rows, two_rows, ag_s.at[n], ag_r.at[n % 3, sem], sib, z).wait_recv()
+
     def ag_finish_near(n, buf):
-        for k in (0, 7):
-            ag_landed(n, buf, k).wait_recv()
+        ag_handed(n, buf, 0)
 
     def ag_finish(n, buf):
-        for k in (8, 9, 10):
-            ag_landed(n, buf, k).wait_recv()
+        ag_handed(n, buf, 7)
 
     def ag_drain(n, buf):
         seven = buf.at[pl.ds(0, 7)]
         rcopy(seven, seven, ag_s.at[n], ag_r.at[0, 0], sib, z).wait_send()
 
-    def gathered_tiles(n, buf, body, between=None):
+    def gathered_tiles(n, buf, body, between, before=None):
         ag_pass_near(n, buf)
         ag_finish_near(n, buf)
+        if before is not None:
+            before()
         loop(0, 2, lambda k: body(2 * k + cy))
-        if between is not None:
-            between()
+        between()
         ag_pass_across(n, buf)
         ag_finish(n, buf)
         loop(0, 2, lambda k: body(2 * k + 1 - cy))
@@ -762,13 +768,15 @@
             )
         return jnp.concatenate(halves, axis=1)
 
+    A2A_SEM = (0, 2 * CTX - 2, 2 * CTX - 1, 2 * CTX, CTX - 1)
+
     def a2a(n, src, dst_of, i, sem=0):
         to = (c + i) % CTX
-        return rcopy(src.at[to], dst_of(c), a2a_s.at[n], a2a_r.at[n, sem], to, z)
+        return rcopy(src.at[to], dst_of(c), a2a_s.at[n], a2a_r.at[A2A_SEM[n] + sem], to, z)
 
     def a2a_landed(n, dst_of, i):
         frm = (c + CTX - i) % CTX
-        return rcopy(dst_of(frm), dst_of(frm), a2a_s.at[n], a2a_r.at[n, i - 1], sib, z)
+        return rcopy(dst_of(frm), dst_of(frm), a2a_s.at[n], a2a_r.at[A2A_SEM[n] + i - 1], sib, z)
 
     def a2a_start(n, src, dst_of, apart=False):
         loop(1, CTX, lambda i: a2a(n, src, dst_of, i, i - 1 if apart else 0).start())
@@ -781,11 +789,11 @@
 
     def a2a_wait(n, dst):
         seven = dst.at[pl.ds(0, CTX - 1)]
-        rcopy(seven, seven, a2a_s.at[n], a2a_r.at[n, 0], sib, z).wait_recv()
+        rcopy(seven, seven, a2a_s.at[n], a2a_r.at[A2A_SEM[n]], sib, z).wait_recv()
 
     def a2a_drain(n, src):
         seven = src.at[pl.ds(0, CTX - 1)]
-        rcopy(seven, seven, a2a_s.at[n], a2a_r.at[n, 0], sib, z).wait_send()
+        rcopy(seven, seven, a2a_s.at[n], a2a_r.at[A2A_SEM[n]], sib, z).wait_send()
 
     inner = (z == 1) | (z == 2)
     outer = jnp.logical_not(inner)
@@ -1051,13 +1059,6 @@
 
     loop(0, tiles, normed)
     x_own[...] = xg[slot]
-    pl.when(outer)(lambda: a2a_wait(1, wgu_in))
-    zg_start(*g_gu1, outer)
-    zg_start(*g_gu2, outer)
-    zg_start(*g_d, outer)
-    zg_wait(*g_q)
-    zg_wait(*g_kv)
-
     g_query = gains[:, 2 * MODEL_WIDTH : 2 * MODEL_WIDTH + HEAD_SIZE]
     g_key = gains[:, 2 * MODEL_WIDTH + HEAD_SIZE :]
 
@@ -1070,31 +1071,39 @@
     def turned(v):
         return pltpu.roll(v, HEAD_SIZE // 2, 1)
 
-    def project(t):
+    def normed_rope(raw, gain, at):
+        scale = lax.rsqrt(jnp.mean(raw * raw, axis=-1, keepdims=True) + NORM_EPS)
+        y = raw * scale * gain
+        return y * cos_ref[at, :] + turned(y) * sin_ref[at, :]
+
+    def project_queries(t):
         at = tile_rows(t)
-        cosine, sine = cos_ref[at, :], sin_ref[at, :]
-
-        def normed(raw, gain):
-            scale = lax.rsqrt(jnp.mean(raw * raw, axis=-1, keepdims=True) + NORM_EPS)
-            y = raw * scale * gain
-            return y * cosine + turned(y) * sine
-
         out = dot(two(n1, t), wq[0].reshape(MODEL_WIDTH, QCOLS))
-        both = dot(two(n1, t), wq[1].reshape(MODEL_WIDTH, 2 * HEAD_SIZE))
         for h in range(GROUP):
             raw = out[:, h * HEAD_SIZE : (h + 1) * HEAD_SIZE]
             qraw[at, h * HEAD_SIZE : (h + 1) * HEAD_SIZE] = raw
-            q_s[h, at, :] = normed(raw, g_query).astype(BF16)
+            q_s[h, at, :] = normed_rope(raw, g_query, at).astype(BF16)
+
+    def project_pairs(t):
+        at = tile_rows(t)
+        both = dot(two(n1, t), wq[1].reshape(MODEL_WIDTH, 2 * HEAD_SIZE))
         raw = both[:, :HEAD_SIZE]
         kraw[at, :] = raw
-        keys = normed(raw, g_key)
+        keys = normed_rope(raw, g_key, at)
         values = both[:, HEAD_SIZE:]
         k_s[at, :] = keys.astype(BF16)
         v_s[at, :] = values.astype(BF16)
         kt_s[:, at] = keys.T.astype(BF16)
         vt_s[:, at] = values.T.astype(BF16)
 
-    loop(0, tiles, project)
+    zg_wait(*g_q)
+    loop(0, tiles, project_queries)
+    pl.when(outer)(lambda: a2a_wait(1, wgu_in))
+    zg_start(*g_gu1, outer)
+    zg_start(*g_gu2, outer)
+    zg_start(*g_d, outer)
+    zg_wait(*g_kv)
+    loop(0, tiles, project_pairs)
     ag_drain(0, xg)
     zg_far(*g_o)
     pl.when(inner)(lambda: a2a_wait(1, wgu_in))
@@ -1138,14 +1147,14 @@
     rs_give(0, out_part, 1)
     ag_pass_near(1, cot)
     attend(core)
-    ag_pass_across(1, cot)
+    zg_back(*g_gu1)
     for h in range(2):
         rs_keep(0, out_part, h)
         rs_send(0, h)
     zg_across(*g_gu2)
-    zg_back(*g_gu1)
     zg_back(*g_gu2)
     rs_relay(0)
+    ag_pass_across(1, cot)
     zg_far(*g_gu1)
     resid = x_own[...].astype(F32) + rs_finish(0)
     resid_s[...] = resid
@@ -1158,15 +1167,6 @@
     zg_far(*g_gu2)
     zg_start(*g_d, inner)
     zg_across(*g_d)
-    ag_pass_near(2, n2)
-    ag_finish_near(2, n2)
-    zg_back(*g_d)
-    ag_pass_across(2, n2)
-    ag_finish(2, n2)
-    zg_far(*g_d)
-    zg_wait(*g_gu1)
-    zg_wait(*g_gu2)
-
     def feed(t):
         at = tile_rows(t)
         both = dot(two(n2, t), wgu[...].reshape(MODEL_WIDTH, 2 * HID))
@@ -1177,7 +1177,15 @@
         ggu[at, :HID] = (up * sig * (1.0 + gate * (1.0 - sig))).astype(BF16)
         ggu[at, HID:] = silu.astype(BF16)
 
-    loop(0, tiles, feed)
+    def wgu_there():
+        zg_wait(*g_gu1)
+        zg_wait(*g_gu2)
+
+    def pass_down():
+        zg_back(*g_d)
+
+    gathered_tiles(2, n2, feed, pass_down, wgu_there)
+    zg_far(*g_d)
 
     def down_grad(n):
         there = cot[:, :, n_cols(n)].reshape(2 * half, WIDE)
@@ -1315,7 +1323,7 @@
 
     qkv_grad(0)
     qkv_grad(1)
-    zr_start(r_q1, r_q2, part=(0, 1))
+    zr_start(r_q1, r_q2)
     def back_one_part(which, n):
         per = MODEL_WIDTH // CTX
         at = pl.ds(n * (WIDE // per), WIDE // per)
@@ -1326,11 +1334,11 @@
 
     rs_begin(3, back_one_part)
     zr_second(*r_gu2)
+    zr_first(*r_o)
     rs_relay(3)
-    zr_first(*r_o)
+    zr_second(*r_o)
     zr_first(*r_q1)
     zr_first(*r_q2)
-    zr_second(*r_o)
     sum_d = zr_finish(*r_d)
     for g in range(MODEL_WIDTH // 128):
         lines[line_rows(ends[2], g, MODEL_WIDTH // 128, sum_d.shape[0]), :] = sum_d[
@@ -1348,7 +1356,6 @@
     hrow[:, :MODEL_WIDTH] = terms
     hz[z] = hrow[...]
     loop(1, 4, lambda i: row_z(1, hrow, hz, i).start())
-    zr_start(r_q1, r_q2, part=(2,))
     zr_start(r_o, part=(2,))
     arg_at = lambda j: arg_.at[j]
     a2a_start(2, asg, arg_at)
@@ -1356,15 +1363,15 @@
     out_ref[...] = (resid_s[...] + rs_finish(2)).astype(BF16)
     store_out = pltpu.make_async_copy(out_ref, out_hbm.at[0], loc.at[6])
     store_out.start()
-    row_z_wait(1, hz)
-    hpl[c] = jnp.sum(hz[...], axis=0)
-    loop(1, CTX, lambda i: row_plane(1, hpl.at[c], hpl, i).start())
     arq_at = lambda j: arq.at[j]
     asq[first_half] = zr_finish(*r_q1).astype(BF16)
     a2a_half(3, asq, arq_at, 0)
     asq[second_half] = zr_finish(*r_q2).astype(BF16)
     a2a_half(3, asq, arq_at, 1)
     arq[c] = asq[c]
+    row_z_wait(1, hz)
+    hpl[c] = jnp.sum(hz[...], axis=0)
+    loop(1, CTX, lambda i: row_plane(1, hpl.at[c], hpl, i).start())
     a2a_wait(2, arg_)
     for j in range(CTX):
         for part in range(2 * HID // 128):
@@ -1516,13 +1523,13 @@
         vm((CTX, 1, GAIN_WIDTH), F32),
         vm((1, GAIN_WIDTH), F32),
         dma((4,)),
-        dma((3, 11)),
+        dma((3, 8)),
         dma((2,)),
         dma((2, 2)),
         dma((6,)),
         dma((2, 6)),
         dma((5,)),
-        dma((5, CTX - 1)),
+        dma((2 * CTX + 1,)),
         dma((6, 2)),
         dma((6, 4)),
         dma((6,)),
@@ -1555,9 +1562,108 @@
     out, xgrad, lines = layer_call(
         tokens, cotangent, stretch_order, doc_lengths, master
     )
-    grad = lines.reshape(-1)[: master.shape[0]]
-    new = adam(grad, master, first_moment, second_moment, shards, length)
-    return (out, xgrad, *new)
+    return adam_call(out, xgrad, lines, master, first_moment, second_moment, shards, length)
+
+
+def adam_kernel(
+    spans,
+    settings,
+    out_hbm,
+    xgrad_hbm,
+    grad_hbm,
+    master_hbm,
+    first_hbm,
+    second_hbm,
+    out_to,
+    xgrad_to,
+    master_to,
+    first_to,
+    second_to,
+    out,
+    xgrad,
+    grad,
+    master,
+    first,
+    second,
+    sems,
+):
+    held = (grad, first, second, master, out, xgrad)
+    fetch = [
+        pltpu.make_async_copy(src, dst, sems.at[0, k])
+        for k, (src, dst) in enumerate(
+            zip((grad_hbm, first_hbm, second_hbm, master_hbm, out_hbm, xgrad_hbm), held)
+        )
+    ]
+    store = [
+        pltpu.make_async_copy(src, dst, sems.at[1, k])
+        for k, (src, dst) in enumerate(
+            zip(held[1:], (first_to, second_to, master_to, out_to, xgrad_to))
+        )
+    ]
+    for copy in fetch:
+        copy.start()
+
+    def each(body):
+        begin = 0
+        for k, span in enumerate(spans[:-1]):
+            block = span // -(-span // 65536)
+
+            def step(i, carry, begin=begin, k=k, block=block):
+                at = pl.ds(pl.multiple_of(begin + i * block, block), block)
+                line = pl.ds(pl.multiple_of(begin // 128 + i * (block // 128), 8), block // 128)
+                body(at, (block // 128, 128), grad[line, :], k)
+                return carry
+
+            lax.fori_loop(0, span // block, step, 0)
+            begin += span
+        last = spans[-1]
+        body(pl.ds(begin, last), (1, last), grad[pl.ds(begin // 128, 1), :last], len(spans) - 1)
+
+    def step_first(at, shape, g, k):
+        new = BETA_ONE * first[at].reshape(shape) + (1.0 - BETA_ONE) * g
+        first[at] = new.reshape(-1)
+
+    def step_second(at, shape, g, k):
+        new = BETA_TWO * second[at].reshape(shape) + (1.0 - BETA_TWO) * g * g
+        second[at] = new.reshape(-1)
+
+    def step_master(at, shape, g, k):
+        rate, decay = settings[k]
+        old = master[at].reshape(shape)
+        mean = first[at].reshape(shape) * (1.0 / (1.0 - BETA_ONE**STEP))
+        root = jnp.sqrt(second[at].reshape(shape) * (1.0 / (1.0 - BETA_TWO**STEP)))
+        new = old - rate * (mean / (root + ADAM_EPS) + decay * old)
+        master[at] = new.reshape(-1)
+
+    fetch[0].wait()
+    for k, body in enumerate((step_first, step_second, step_master)):
+        fetch[k + 1].wait()
+        each(body)
+        store[k].start()
+        if k == 1:
+            for j in (4, 5):
+                fetch[j].wait()
+                store[j - 1].start()
+    for copy in store:
+        copy.wait()
+
+
+def adam_call(out, xgrad, lines, master, first_moment, second_moment, shards, length):
+    spans = [r // shards * w for r, w in segment_shapes()]
+    shape = lambda v: jax.ShapeDtypeStruct(v.shape, v.dtype)
+    operands = (out, xgrad, lines, master, first_moment, second_moment)
+    results = (out, xgrad, master, first_moment, second_moment)
+    anywhere = pl.BlockSpec(memory_space=pl.ANY)
+    return pl.pallas_call(
+        functools.partial(adam_kernel, spans, step_settings(length)),
+        out_shape=[shape(v) for v in results],
+        in_specs=[anywhere] * 6,
+        out_specs=[anywhere] * 5,
+        scratch_shapes=[pltpu.VMEM(v.shape, v.dtype) for v in operands]
+        + [pltpu.SemaphoreType.DMA((2, 6))],
+        compiler_params=pltpu.CompilerParams(vmem_limit_bytes=63 << 20),
+        name="adam",
+    )(*operands)
 
 
 def step_settings(length):

time: 145 us -> 141 us (0.972)
  other arithmetic: 6.98 us -> 0 us
  Pallas kernels: 136 us -> 140 us
    sub x1 -> x0, other arithmetic: 6.98 us -> none  [adam(): new_master = master - step_rate * (normalized + decay_value * master)]
    pallas_call x0 -> x1, Pallas kernels: none -> 5.88 us  [adam_call(): pl.pallas_call(functools.partial(adam_kernel, spans, step_settings(length...]
    pallas_call x1, Pallas kernels: 136 us -> 134 us  [layer_call(): pl.pallas_call(layer_kernel, out_shape=(shape((1, rows, width), BF16), sh...]
where the time goes in v4:
time: 141 us; the launch traced here: 140 us
  Pallas kernels  140 us (99%)
    pallas_call x1, Pallas kernels, layer_call(): pl.pallas_call(layer_kernel, out_shape=(shape((1, rows, width), BF16), sh...  134 us
    pallas_call x1, Pallas kernels, adam_call(): pl.pallas_call(functools.partial(adam_kernel, spans, step_settings(length...  5.88 us

profile of v4, /device:TPU:0, one launch (start us, length us, event | category | flops | bytes accessed | tf_op | source)
XLA Modules:
  0.0 140.4 jit_solution(9194970575837256652)
XLA Ops:
  0.6 133.7 %layer.1 = (bf16[1,128,1024]{2,1,0:T(8,128)(2,1)}, bf16[1,128,1024]{2,1,0:T(8,128)(2,1)}, f32[3848,128]{1,0:T(8,128)}) custom-call(s32[16]{0:T(128)} %order_hbm.1, s32[1,3]{1,0:T(1,128)} %doc_hbm.1, bf16[1,128,1024]{2,1,0:T(8,128)(2,1)} %x_hbm.1, bf16[1,128,1024]{2,1,0:T(8,128)(2,1)} %cot_hbm.1, f32[491592]{0:T(1024)} %master_hbm.3), custom_call_target="tpu_custom_call" | custom-call | tf_op jit(solution)/shard_map/layer/pallas_call | solution.py:1542
  134.3 5.9 %adam.1 = (bf16[1,128,1024]{2,1,0:T(8,128)(2,1)}, bf16[1,128,1024]{2,1,0:T(8,128)(2,1)}, f32[491592]{0:T(1024)}, f32[491592]{0:T(1024)}, f32[491592]{0:T(1024)}) custom-call(bf16[1,128,1024]{2,1,0:T(8,128)(2,1)} %get-tuple-element.8.out_hbm, bf16[1,128,1024]{2,1,0:T(8,128)(2,1)} %get-tuple-element.9.xgrad_hbm, f32[3848,128]{1,0:T(8,128)} %get-tuple-element.10.grad_hbm, ...), custom_call_target="tpu_custom_call" | custom-call | tf_op jit(solution)/shard_map/adam/pallas_call | solution.py:1657

commit v5 on v4

--- a/solution.py
+++ b/solution.py
@@ -944,7 +944,12 @@
     g_o = (1, lambda j: wo.at[j])
     g_gu1, g_gu2 = ((2 + h, of) for h, of in enumerate(halves(wgu)))
     g_d = (4, lambda j: wd.at[j])
-    r_d = (0, lambda j: gwd.at[j], lambda j: lwd.at[j])
+    def column_half(ref, h):
+        return lambda j: ref.at[j, :, pl.ds(h * WIDE, WIDE)]
+
+    r_d1, r_d2 = (
+        (6 * h, column_half(gwd, h), column_half(lwd, h)) for h in range(2)
+    )
     r_gu1, r_gu2 = (
         (1 + h, *both) for h, both in enumerate(zip(halves(gwgu), land_halves(lwgu)))
     )
@@ -1193,17 +1198,20 @@
             dot(hidden[...], there, TN).astype(BF16).reshape(4, HID // 4, WIDE)
         )
 
-    loop(0, MODEL_WIDTH // WIDE, down_grad)
-    zr_start(r_d)
+    down_grad(0)
+    zr_start(r_d1)
+    down_grad(1)
+    zr_start(r_d2)
     zg_wait(*g_d)
 
     def feed_back(t):
-        at = tile_rows(t)
-        ghid = dot(two(cot, t), wd[...].reshape(HID, MODEL_WIDTH), NT)
+        at = half_rows(t)
+        ghid = dot(half_slots(cot, t), wd[...].reshape(HID, MODEL_WIDTH), NT)
         ggu[at, :HID] = (ghid * ggu[at, :HID].astype(F32)).astype(BF16)
         ggu[at, HID:] = (ghid * ggu[at, HID:].astype(F32)).astype(BF16)
 
-    loop(0, tiles, feed_back)
+    for t in range(2):
+        feed_back(t)
 
     def back_two_part(which, n):
         per = MODEL_WIDTH // CTX
@@ -1225,7 +1233,8 @@
     zr_start(r_gu1)
     gate_up_grad(1)
     zr_start(r_gu2)
-    zr_first(*r_d)
+    zr_first(*r_d1)
+    zr_first(*r_d2)
     rs_relay(1)
 
 
@@ -1247,7 +1256,8 @@
 
     ag_start(3, gb)
     rs_compute(2, down_part)
-    zr_second(*r_d)
+    zr_second(*r_d1)
+    zr_second(*r_d2)
 
     def attn_grad(t):
         gattn[tile_rows(t), :] = dot(
@@ -1339,11 +1349,11 @@
     zr_second(*r_o)
     zr_first(*r_q1)
     zr_first(*r_q2)
-    sum_d = zr_finish(*r_d)
-    for g in range(MODEL_WIDTH // 128):
-        lines[line_rows(ends[2], g, MODEL_WIDTH // 128, sum_d.shape[0]), :] = sum_d[
-            :, g * 128 : (g + 1) * 128
-        ]
+    for h, item in enumerate((r_d1, r_d2)):
+        sum_d = zr_finish(*item)
+        for g in range(WIDE // 128):
+            at = line_rows(ends[2], h * (WIDE // 128) + g, MODEL_WIDTH // 128, HID // 4)
+            lines[at, :] = sum_d[:, g * 128 : (g + 1) * 128]
     first_half, second_half = pl.ds(0, CTX // 2), pl.ds(CTX // 2, CTX // 2)
     asg[first_half] = zr_finish(*r_gu1).astype(BF16)
     asg[second_half] = zr_finish(*r_gu2).astype(BF16)
@@ -1428,7 +1438,8 @@
         zg_drain(n, some)
     three = pl.ds(0, 3)
     for n, part in (
-        (0, lwd.at[three]),
+        (0, lwd.at[three, :, pl.ds(0, WIDE)]),
+        (6, lwd.at[three, :, pl.ds(WIDE, WIDE)]),
         (1, lwgu.at[three, first_four]),
         (2, lwgu.at[three, first_four]),
         (3, lwo.at[three]),
@@ -1532,8 +1543,8 @@
         dma((2 * CTX + 1,)),
         dma((6, 2)),
         dma((6, 4)),
-        dma((6,)),
-        dma((6, 5)),
+        dma((7,)),
+        dma((7, 5)),
         dma((2, 2)),
         dma((2, 2)),
         dma((8,)),

time: 141 us -> 140 us (level)
  no operation moved by 1% of the time
where the time goes in v5:
time: 140 us
  Pallas kernels  139 us (99%)
    pallas_call x1, Pallas kernels, layer_call(): pl.pallas_call(layer_kernel, out_shape=(shape((1, rows, width), BF16), sh...  133 us
    pallas_call x1, Pallas kernels, adam_call(): pl.pallas_call(functools.partial(adam_kernel, spans, step_settings(length...  5.88 us

profile of v5, /device:TPU:0, one launch (start us, length us, event | category | flops | bytes accessed | tf_op | source)
XLA Modules:
  0.0 139.6 jit_solution(163937826548550544)
XLA Ops:
  0.6 132.9 %layer.1 = (bf16[1,128,1024]{2,1,0:T(8,128)(2,1)}, bf16[1,128,1024]{2,1,0:T(8,128)(2,1)}, f32[3848,128]{1,0:T(8,128)}) custom-call(s32[16]{0:T(128)} %order_hbm.1, s32[1,3]{1,0:T(1,128)} %doc_hbm.1, bf16[1,128,1024]{2,1,0:T(8,128)(2,1)} %x_hbm.1, bf16[1,128,1024]{2,1,0:T(8,128)(2,1)} %cot_hbm.1, f32[491592]{0:T(1024)} %master_hbm.3), custom_call_target="tpu_custom_call" | custom-call | tf_op jit(solution)/shard_map/layer/pallas_call | solution.py:1553
  133.6 5.9 %adam.1 = (bf16[1,128,1024]{2,1,0:T(8,128)(2,1)}, bf16[1,128,1024]{2,1,0:T(8,128)(2,1)}, f32[491592]{0:T(1024)}, f32[491592]{0:T(1024)}, f32[491592]{0:T(1024)}) custom-call(bf16[1,128,1024]{2,1,0:T(8,128)(2,1)} %get-tuple-element.8.out_hbm, bf16[1,128,1024]{2,1,0:T(8,128)(2,1)} %get-tuple-element.9.xgrad_hbm, f32[3848,128]{1,0:T(8,128)} %get-tuple-element.10.grad_hbm, ...), custom_call_target="tpu_custom_call" | custom-call | tf_op jit(solution)/shard_map/adam/pallas_call | solution.py:1668

commit v6 on v5

--- a/solution.py
+++ b/solution.py
@@ -706,7 +706,7 @@
 
     def rs_chip(r, k):
         to = chip_at((XN, XN, YN, YN, YN, XN)[k]) * 2 + core
-        return rcopy(csnd.at[k], crcv.at[r % 2, k], rs_cs.at[k], rs_cr.at[r % 2, k], to, z)
+        return rcopy(csnd.at[k], crcv.at[r % 2, k], rs_cs.at[0], rs_cr.at[r % 2, k], to, z)
 
     def rs_give(r, part, h):
         if r > 0:
@@ -720,11 +720,13 @@
     def pair_sum(r, h, i):
         return own[h, chip_at(i)] + prcv[r % 2, h, chip_at(i)].astype(F32)
 
+    def rs_sent():
+        rcopy(csnd, csnd, rs_cs.at[0], rs_cr.at[0, 0], sib, z).wait_send()
+
     def rs_send(r, h):
         rs_pair(r, h).wait_recv()
         if r > 0 and h == 0:
-            for k in range(6):
-                rs_chip(r - 1, k).wait_send()
+            rs_sent()
         csnd[2 * h] = pair_sum(r, h, ACROSS).astype(BF16)
         rs_chip(r, 2 * h).start()
         csnd[2 * h + 1] = pair_sum(r, h, (XN, YN)[h]).astype(BF16)
@@ -747,8 +749,7 @@
     def rs_drain(r):
         for h in range(2):
             rs_pair(r, h).wait_send()
-        for k in range(6):
-            rs_chip(r, k).wait_send()
+        rs_sent()
 
     def rs_relay(r):
         for h, second in ((0, YN), (1, XN)):
@@ -770,22 +771,27 @@
 
     A2A_SEM = (0, 2 * CTX - 2, 2 * CTX - 1, 2 * CTX, CTX - 1)
 
+    PARTNERS = ((3, 0), (3, 1), (1, 0), (2, 0), (1, 1), (2, 1), (0, 1))
+
+    def partner(i):
+        chip_of, other = PARTNERS[i - 1]
+        return chip_at(chip_of) * 2 + (1 - core if other else core)
+
     def a2a(n, src, dst_of, i, sem=0):
-        to = (c + i) % CTX
+        to = partner(i)
         return rcopy(src.at[to], dst_of(c), a2a_s.at[n], a2a_r.at[A2A_SEM[n] + sem], to, z)
 
     def a2a_landed(n, dst_of, i):
-        frm = (c + CTX - i) % CTX
+        frm = partner(i)
         return rcopy(dst_of(frm), dst_of(frm), a2a_s.at[n], a2a_r.at[A2A_SEM[n] + i - 1], sib, z)
 
     def a2a_start(n, src, dst_of, apart=False):
-        loop(1, CTX, lambda i: a2a(n, src, dst_of, i, i - 1 if apart else 0).start())
+        for i in range(1, CTX):
+            a2a(n, src, dst_of, i, i - 1 if apart else 0).start()
 
     def a2a_half(n, src, dst_of, h):
-        def one(i):
-            pl.when((c + i) % CTX // (CTX // 2) == h)(a2a(n, src, dst_of, i).start)
-
-        loop(1, CTX, one)
+        for i in range(1, CTX):
+            pl.when(partner(i) // (CTX // 2) == h)(a2a(n, src, dst_of, i).start)
 
     def a2a_wait(n, dst):
         seven = dst.at[pl.ds(0, CTX - 1)]
@@ -799,20 +805,20 @@
     outer = jnp.logical_not(inner)
     far = 3 * (2 - z)
 
-    def zg(n, of, j, to, sem):
-        return rcopy(of(j), of(j), zg_s.at[n, sem], zg_r.at[n, j], c, to)
+    def zg(n, of, j, to):
+        return rcopy(of(j), of(j), zg_s.at[n], zg_r.at[n, j], c, to)
 
     def zg_own(n, of):
         return (
-            (z < 3, zg(n, of, z, z + 1, 0)),
-            (z > 0, zg(n, of, z, z - 1, 0)),
+            (z < 3, zg(n, of, z, z + 1)),
+            (z > 0, zg(n, of, z, z - 1)),
         )
 
     def zg_onward(n, of):
         return (
-            zg(n, of, z - 1, z + 1, 1),
-            zg(n, of, z + 1, z - 1, 1),
-            zg(n, of, far, 3 * (z - 1), 1),
+            zg(n, of, z - 1, z + 1),
+            zg(n, of, z + 1, z - 1),
+            zg(n, of, far, 3 * (z - 1)),
         )
 
     def zg_start(n, of, who=None):
@@ -821,7 +827,7 @@
 
     def zg_pass(n, of, k, when, j):
         def run():
-            zg(n, of, j, z, 0).wait_recv()
+            zg(n, of, j, z).wait_recv()
             zg_onward(n, of)[k].start()
 
         pl.when(when)(run)
@@ -840,7 +846,7 @@
 
     def zg_far(n, of):
         def run():
-            zg(n, of, far, z, 0).wait_recv()
+            zg(n, of, far, z).wait_recv()
             zg_onward(n, of)[2].start()
 
         pl.when(inner)(run)
@@ -848,21 +854,17 @@
     def zg_wait(n, of):
         def run():
             for i in (1, 2, 3):
-                zg(n, of, (z + i) % 4, z, 0).wait_recv()
+                zg(n, of, (z + i) % 4, z).wait_recv()
 
         pl.when(outer)(run)
 
     def zg_drain(n, some):
-        def sent(count, sem):
+        def sent(count):
             part = some(count)
-            rcopy(part, part, zg_s.at[n, sem], zg_r.at[n, 0], c, c).wait_send()
-
-        def run():
-            sent(2, 0)
-            sent(3, 1)
-
-        pl.when(inner)(run)
-        pl.when(outer)(lambda: sent(1, 0))
+            rcopy(part, part, zg_s.at[n], zg_r.at[n, 0], sib, z).wait_send()
+
+        pl.when(inner)(lambda: sent(5))
+        pl.when(outer)(lambda: sent(1))
 
     def zr(n, of, land, d, to, spot):
         return rcopy(of(d), land(spot), zr_s.at[n], zr_r.at[n, spot], c, to)
@@ -969,14 +971,12 @@
         there = wq.at[part, frm, z]
         n = 5 * part
         for to, here in ((z + 1, z < 3), (z - 1, z > 0)):
-            pl.when(here)(rcopy(there, there, zg_s.at[n, 0], zg_r.at[n, z], c, to).start)
+            pl.when(here)(rcopy(there, there, zg_s.at[n], zg_r.at[n, z], c, to).start)
 
     def shares_landed(part, n, at):
-        def one(i):
+        for i in (7, 3, 4, 5, 6, 1, 2):
             a2a_landed(n, at, i).wait_recv()
-            share(part, (c + CTX - i) % CTX)
-
-        loop(1, CTX, one)
+            share(part, partner(i))
 
     for part in range(2):
         wq[part, c, z] = wq_in[part, c]
@@ -1364,8 +1364,8 @@
     store_xgrad = pltpu.make_async_copy(xgrad_ref, xgrad_hbm.at[0], loc.at[5])
     store_xgrad.start()
     hrow[:, :MODEL_WIDTH] = terms
-    hz[z] = hrow[...]
-    loop(1, 4, lambda i: row_z(1, hrow, hz, i).start())
+    hpl[c] = hrow[...]
+    loop(1, CTX, lambda i: row_plane(1, hpl.at[c], hpl, i).start())
     zr_start(r_o, part=(2,))
     arg_at = lambda j: arg_.at[j]
     a2a_start(2, asg, arg_at)
@@ -1373,15 +1373,15 @@
     out_ref[...] = (resid_s[...] + rs_finish(2)).astype(BF16)
     store_out = pltpu.make_async_copy(out_ref, out_hbm.at[0], loc.at[6])
     store_out.start()
+    row_plane_wait(1, hpl)
+    hz[z] = jnp.sum(hpl[...], axis=0)
+    loop(1, 4, lambda i: row_z(1, hz.at[z], hz, i).start())
     arq_at = lambda j: arq.at[j]
     asq[first_half] = zr_finish(*r_q1).astype(BF16)
     a2a_half(3, asq, arq_at, 0)
     asq[second_half] = zr_finish(*r_q2).astype(BF16)
     a2a_half(3, asq, arq_at, 1)
     arq[c] = asq[c]
-    row_z_wait(1, hz)
-    hpl[c] = jnp.sum(hz[...], axis=0)
-    loop(1, CTX, lambda i: row_plane(1, hpl.at[c], hpl, i).start())
     a2a_wait(2, arg_)
     for j in range(CTX):
         for part in range(2 * HID // 128):
@@ -1411,8 +1411,8 @@
             :, g * 128 : (g + 1) * 128
         ]
     stores[2].start()
-    row_plane_wait(1, hpl)
-    total = jnp.sum(hpl[...], axis=0)
+    row_z_wait(1, hz)
+    total = jnp.sum(hz[...], axis=0)
     lines[pl.ds(tail // 128, 1), :] = pltpu.roll(
         total, GAIN_WIDTH - spans[4] * (4 * c + z), 1
     )[:, :128]
@@ -1428,12 +1428,12 @@
     a2a_drain(3, asq)
     first_four = pl.ds(0, CTX // 2)
     for n, some in (
-        (0, lambda count: wq.at[0, :, pl.ds(0, count)]),
-        (5, lambda count: wq.at[1, :, pl.ds(0, count)]),
-        (1, lambda count: wo.at[pl.ds(0, count)]),
-        (2, lambda count: wgu.at[first_four, pl.ds(0, count)]),
-        (3, lambda count: wgu.at[first_four, pl.ds(0, count)]),
-        (4, lambda count: wd.at[pl.ds(0, count)]),
+        (0, lambda count: lwq.at[pl.ds(0, count), first_four]),
+        (5, lambda count: lwq.at[pl.ds(0, count), first_four]),
+        (1, lambda count: lwo.at[pl.ds(0, count)]),
+        (2, lambda count: lwgu.at[pl.ds(0, count), first_four]),
+        (3, lambda count: lwgu.at[pl.ds(0, count), first_four]),
+        (4, lambda count: lwd.at[pl.ds(0, count)]),
     ):
         zg_drain(n, some)
     three = pl.ds(0, 3)
@@ -1537,11 +1537,11 @@
         dma((3, 8)),
         dma((2,)),
         dma((2, 2)),
-        dma((6,)),
+        dma((1,)),
         dma((2, 6)),
         dma((5,)),
         dma((2 * CTX + 1,)),
-        dma((6, 2)),
+        dma((6,)),
         dma((6, 4)),
         dma((7,)),
         dma((7, 5)),

time: 140 us -> 140 us (level)
  no operation moved by 1% of the time
where the time goes in v6:
time: 140 us
  Pallas kernels  139 us (99%)
    pallas_call x1, Pallas kernels, layer_call(): pl.pallas_call(layer_kernel, out_shape=(shape((1, rows, width), BF16), sh...  133 us
    pallas_call x1, Pallas kernels, adam_call(): pl.pallas_call(functools.partial(adam_kernel, spans, step_settings(length...  5.88 us

profile of v6, /device:TPU:0, one launch (start us, length us, event | category | flops | bytes accessed | tf_op | source)
XLA Modules:
  0.0 139.7 jit_solution(3487688343152140544)
XLA Ops:
  0.6 133.0 %layer.1 = (bf16[1,128,1024]{2,1,0:T(8,128)(2,1)}, bf16[1,128,1024]{2,1,0:T(8,128)(2,1)}, f32[3848,128]{1,0:T(8,128)}) custom-call(s32[16]{0:T(128)} %order_hbm.1, s32[1,3]{1,0:T(1,128)} %doc_hbm.1, bf16[1,128,1024]{2,1,0:T(8,128)(2,1)} %x_hbm.1, bf16[1,128,1024]{2,1,0:T(8,128)(2,1)} %cot_hbm.1, f32[491592]{0:T(1024)} %master_hbm.3), custom_call_target="tpu_custom_call" | custom-call | tf_op jit(solution)/shard_map/layer/pallas_call | solution.py:1553
  133.6 5.9 %adam.1 = (bf16[1,128,1024]{2,1,0:T(8,128)(2,1)}, bf16[1,128,1024]{2,1,0:T(8,128)(2,1)}, f32[491592]{0:T(1024)}, f32[491592]{0:T(1024)}, f32[491592]{0:T(1024)}) custom-call(bf16[1,128,1024]{2,1,0:T(8,128)(2,1)} %get-tuple-element.8.out_hbm, bf16[1,128,1024]{2,1,0:T(8,128)(2,1)} %get-tuple-element.9.xgrad_hbm, f32[3848,128]{1,0:T(8,128)} %get-tuple-element.10.grad_hbm, ...), custom_call_target="tpu_custom_call" | custom-call | tf_op jit(solution)/shard_map/adam/pallas_call | solution.py:1668
